TPU v7x, 32 devices: a whole 2x2x4 slice. The times are simulated.
32 devices in a mesh: grp: 4 (over x, core), mem: 8 (over z, y).
Axes of the slice: x: 2, y: 2, z: 4, core: 2. Of those that a mesh axis runs over, the one named last changes fastest.
Arguments:
- frames: bfloat16 [512, 256, 1024], P('grp', 'mem'), may hold values from -6 to 6
- probe_wave: float32 [2, 128, 128], P(None, 'mem'), may hold values from -6 to 6
Outputs:
- deconv_real: float32 [512, 256, 1024], P('mem', 'grp')
- deconv_imag: float32 [512, 256, 1024], P('mem', 'grp')
All inputs are finite; a program needn't handle non-finite values.
Results may differ from a plain program's by a relative error of at most 0.0087.
Values may be sent and summed in bfloat16 or wider, within the bound.
No kernel may reach another device: no remote copies, remote signals or barrier semaphores. Data moves between devices by JAX's collectives and lax.ppermute only.
A program may use at most 256 MiB of HBM per device.

v0:
```python
import math

import jax
import jax.numpy as jnp
from jax import lax
from jax.sharding import PartitionSpec as P

WIN = 32
SCAN_Y = 512
SCAN_X = 256
STRIDE_Y = 4
STRIDE_X = 2


wiener_floor = 0.5


def scan_table(length):
    positions = jnp.arange(length, dtype=jnp.int32)
    phases = positions[:, None] * positions[None, :] % length
    angles = -2.0 * math.pi / length * phases.astype(jnp.float32)
    factor = 1.0 / math.sqrt(length)
    return (
        (jnp.cos(angles) * factor).astype(jnp.bfloat16),
        (jnp.sin(angles) * factor).astype(jnp.bfloat16),
    )


def detector_parts(window):
    offsets = jnp.arange(window, dtype=jnp.int32)
    phases = (
        offsets[:, None, None, None] * offsets[None, None, :, None]
        + offsets[None, :, None, None] * offsets[None, None, None, :]
    ) % window
    phases = phases.reshape(window * window, window * window)
    angles = -2.0 * math.pi / window * phases.astype(jnp.float32)
    factor = 1.0 / window
    return (
        (jnp.cos(angles) * factor).astype(jnp.bfloat16),
        (jnp.sin(angles) * factor).astype(jnp.bfloat16),
    )


def slab_table_of(part_re, part_im):
    upper = jnp.concatenate([part_re, part_im], axis=1)
    lower = jnp.concatenate([-part_im, part_re], axis=1)
    return jnp.concatenate([upper, lower], axis=0)


def block_columns(part_re, part_im, block_count):
    pixels = part_re.shape[0]
    block_width = pixels // block_count
    stacked = jnp.stack(
        [
            part_re.reshape(pixels, block_count, block_width),
            part_im.reshape(pixels, block_count, block_width),
        ],
        axis=2,
    )
    return stacked.reshape(pixels, 2 * pixels)


def signed_shift(freqs, length, step_size):
    centred = jnp.where(freqs >= length // 2, freqs - length, freqs)
    return jnp.floor_divide(centred, step_size)


def wigner_slab(probe_real, probe_imag, shift_y, shift_x, slab_table):
    grid_size = probe_real.shape[0]
    offsets = jnp.arange(WIN, dtype=jnp.int32)
    row_index = (offsets[None, :] + shift_y[:, None]) % grid_size
    col_index = (offsets[None, :] + shift_x[:, None]) % grid_size
    count_y = shift_y.shape[0]
    count_x = shift_x.shape[0]

    def shifted(plane):
        picked = jnp.take(plane, row_index, axis=0)
        picked = jnp.take(picked, col_index, axis=2)
        return picked.transpose(0, 2, 1, 3).reshape(count_y * count_x, WIN * WIN)

    moved_re = shifted(probe_real)
    moved_im = shifted(probe_imag)
    base_re = probe_real[:WIN, :WIN].reshape(1, WIN * WIN)
    base_im = probe_imag[:WIN, :WIN].reshape(1, WIN * WIN)
    prod_re = (base_re * moved_re + base_im * moved_im).astype(jnp.bfloat16)
    prod_im = (base_im * moved_re - base_re * moved_im).astype(jnp.bfloat16)
    stacked = jnp.concatenate([prod_re, prod_im], axis=1)
    slabs = jnp.dot(stacked, slab_table, preferred_element_type=jnp.float32)
    pixels = WIN * WIN
    slab_shape = (count_y, count_x, pixels)
    return (slabs[:, :pixels].reshape(slab_shape), slabs[:, pixels:].reshape(slab_shape))


def deconvolve(spec_re, spec_im, chi_re, chi_im):
    real_part = spec_re.astype(jnp.float32)
    imag_part = spec_im.astype(jnp.float32)
    denominator = chi_re * chi_re + chi_im * chi_im + wiener_floor
    out_re = (real_part * chi_re + imag_part * chi_im) / denominator
    out_im = (imag_part * chi_re - real_part * chi_im) / denominator
    return (out_re, out_im)


def swap_halves(values):
    half_width = values.shape[-1] // 2
    return jnp.concatenate([-values[..., half_width:], values[..., :half_width]], axis=-1)


def shards(frames, probe_wave):
    highest = lax.Precision.HIGHEST
    rows_dev, cols_dev, pixels = frames.shape
    det_re, det_im = detector_parts(WIN)
    cy_re, cy_im = scan_table(SCAN_Y)
    cx_re, cx_im = scan_table(SCAN_X)
    whole_probe = lax.all_gather(probe_wave, "mem", axis=1, tiled=True)
    flat_rows = frames.reshape(rows_dev * cols_dev, pixels)
    block_count = lax.axis_size("mem")
    merged = block_columns(det_re, det_im, block_count)
    spatial = jnp.dot(flat_rows, merged, preferred_element_type=jnp.float32).astype(jnp.bfloat16)
    spatial = spatial.reshape(rows_dev, cols_dev, 2 * pixels)
    received = lax.all_to_all(spatial, "mem", split_axis=2, concat_axis=1, tiled=True)
    first_term = jnp.einsum("nrc,rq->nqc", received, cx_re, preferred_element_type=jnp.float32)
    partial_x = first_term + jnp.einsum(
        "nrc,rq->nqc", swap_halves(received), cx_im, preferred_element_type=jnp.float32
    )
    gathered = lax.all_to_all(partial_x, "grp", split_axis=1, concat_axis=0, tiled=True)
    spectrum = jnp.einsum("rbc,rq->qbc", gathered, cy_re.astype(jnp.float32), precision=highest)
    spectrum = spectrum + jnp.einsum(
        "rbc,rq->qbc", swap_halves(gathered), cy_im.astype(jnp.float32), precision=highest
    )
    regrouped = lax.all_to_all(
        spectrum.astype(jnp.bfloat16), "mem", split_axis=0, concat_axis=2, tiled=True
    )
    qy_dev = regrouped.shape[0]
    qx_dev = regrouped.shape[1]
    unpacked = regrouped.reshape(qy_dev, qx_dev, block_count, 2, pixels // block_count)
    spec_re = unpacked[:, :, :, 0, :].reshape(qy_dev, qx_dev, pixels)
    spec_im = unpacked[:, :, :, 1, :].reshape(qy_dev, qx_dev, pixels)
    first_y = lax.axis_index("mem") * qy_dev
    first_x = lax.axis_index("grp") * qx_dev
    shift_y = signed_shift(
        first_y + STRIDE_Y * jnp.arange(qy_dev // STRIDE_Y, dtype=jnp.int32), SCAN_Y, STRIDE_Y
    )
    shift_x = signed_shift(
        first_x + STRIDE_X * jnp.arange(qx_dev // STRIDE_X, dtype=jnp.int32), SCAN_X, STRIDE_X
    )
    slab_table = slab_table_of(det_re, det_im)
    chi_re, chi_im = wigner_slab(whole_probe[0], whole_probe[1], shift_y, shift_x, slab_table)
    chi_re = jnp.repeat(jnp.repeat(chi_re, STRIDE_Y, axis=0), STRIDE_X, axis=1)
    chi_im = jnp.repeat(jnp.repeat(chi_im, STRIDE_Y, axis=0), STRIDE_X, axis=1)
    return deconvolve(spec_re, spec_im, chi_re, chi_im)


def solution(mesh):
    placed = (P("grp", "mem", None), P(None, "mem", None))
    return jax.shard_map(
        shards,
        mesh=mesh,
        in_specs=placed,
        out_specs=(P("mem", "grp", None), P("mem", "grp", None)),
        check_vma=False,
    )
```

profile of v0, /device:TPU:0, one launch (start us, length us, event | category | flops | bytes accessed | tf_op | source)
XLA Modules:
  0.0 1872.0 jit_solution(5009732097055460786)
XLA Ops:
  22.7 18.0 multiply_convert_fusion.3
  41.2 23.8 %convert_bitcast_fusion = bf16[4096,2048]{0,1:T(8,128)(2,1)} fusion(bf16[1024,2048]{0,1:T(8,128)(2,1)S(1)} %bitcast.95, bf16[4096,1024]{1,0:T(8,128)(2,1)} %bitcast.98), kind=kOutput, calls=%fused_computation.18 | convolution fusion | flops 17188257792 | bytes 29360128 | tf_op jit(solution)/shard_map/dot_general | solution.py:118
  65.0 22.6 %copy.29 = bf16[4096,2048]{1,0:T(8,128)(2,1)} copy(bf16[4096,2048]{0,1:T(8,128)(2,1)} %convert_bitcast_fusion) | data formatting | bytes 33554432 | tf_op jit(solution)/shard_map/convert_element_type | solution.py:118
  87.6 25.5 %copy.30 = bf16[128,32,2048]{0,1,2:T(8,128)(2,1)} copy(bf16[128,32,2048]{2,1,0:T(8,128)(2,1)} %bitcast.87) | data formatting | bytes 33554432 | tf_op jit(solution)/shard_map/reshape | solution.py:119
  113.1 372.2 %all_to_all.51 = bf16[128,32,2048]{0,1,2:T(8,128)(2,1)} all-to-all(bf16[128,32,2048]{0,1,2:T(8,128)(2,1)} %copy.30), channel_id=1, replica_groups=mesh['grp'=4,'mem'=8] {'mem'}, dimensions={2} | all-to-all | bytes 33554432 | tf_op jit(solution)/shard_map/all_to_all | solution.py:120
  485.2 25.5 %copy.31 = bf16[128,32,8,256]{3,1,2,0:T(8,128)(2,1)} copy(bf16[128,32,8,256]{0,1,3,2:T(8,128)(2,1)} %bitcast.88) | data formatting | bytes 33554432 | tf_op jit(solution)/shard_map/all_to_all | solution.py:120
  510.8 19.3 %fusion.52 = f32[256,128,256]{2,0,1:T(8,128)} fusion(bf16[128,256,256]{2,1,0:T(8,128)(2,1)} %bitcast.85), kind=kOutput, calls=%fused_computation.85 | convolution fusion | flops 4296015872 | bytes 50331648 | tf_op jit(solution)/shard_map/nrc,rq->nqc/dot_general | solution.py:121
  541.6 26.9 %add_bitcast_fusion = f32[128,256,256]{2,1,0:T(8,128)} fusion(f32[256,128,256]{2,0,1:T(8,128)} %fusion.52, bf16[128,256,128]{2,1,0:T(8,128)(2,1)} %get-tuple-element.13, bf16[128,256,128]{2,1,0:T(8,128)(2,1)} %get-tuple-element.12), kind=kOutput, calls=%fused_computation.9 | convolution fusion | flops 4337958912 | bytes 83886080 | tf_op jit(solution)/shard_map/nrc,rq->nqc/dot_general | solution.py:122
  568.5 31.9 %copy.32 = f32[128,256,256]{2,0,1:T(8,128)} copy(f32[128,256,256]{2,1,0:T(8,128)} %add_bitcast_fusion) | data formatting | bytes 67108864 | tf_op jit(solution)/shard_map/add | solution.py:122
  614.1 358.8 %all-to-all-done.1 = f32[128,256,256]{2,0,1:T(8,128)} async-done(((f32[128,256,256]{2,0,1:T(8,128)}), f32[128,256,256]{2,0,1:T(8,128)}, u32[]{:S(2)}, u32[]{:S(2)}) %all-to-all-start.1) | async-done | bytes 33554464 | tf_op jit(solution)/shard_map/all_to_all | solution.py:125
  973.0 22.9 %copy.33 = f32[128,4,64,256]{3,0,1,2:T(8,128)} copy(f32[128,4,64,256]{3,0,2,1:T(8,128)} %bitcast.12) | data formatting | bytes 67108864 | tf_op jit(solution)/shard_map/all_to_all | solution.py:125
  995.9 52.1 %fusion.37 = f32[512,64,256]{2,0,1:T(8,128)} fusion(f32[512,64,256]{2,0,1:T(8,128)} %bitcast.83), kind=kOutput, calls=%fused_computation.67 | convolution fusion | flops 51543801856 | bytes 67108864 | tf_op jit(solution)/shard_map/rbc,rq->qbc/dot_general | solution.py:126
  1048.0 22.0 %slice_negate_fusion = (f32[512,64,128]{2,0,1:T(8,128)}, f32[512,64,128]{2,0,1:T(8,128)}) fusion(f32[512,64,256]{2,0,1:T(8,128)} %bitcast.84), kind=kLoop, calls=%fused_computation.10 | loop fusion | flops 4194304 | bytes 67108864 | tf_op jit(solution)/shard_map/neg | solution.py:105
  1070.0 44.5 %add_convert_fusion = bf16[512,64,256]{2,0,1:T(8,128)(2,1)} fusion(f32[512,64,256]{2,0,1:T(8,128)} %fusion.37, f32[512,64,128]{2,0,1:T(8,128)} %get-tuple-element.9, f32[512,64,128]{2,0,1:T(8,128)} %get-tuple-element.8, bf16[512,512,1]{0,1,2:T(8,128)(2,1)S(1)} %fusion.104), kind=kOutput, calls=%fused_computation.8 | convolution fusion | flops 51564773376 | bytes 84410368 | tf_op jit(solution)/shard_map/rbc,rq->qbc/dot_general | solution.py:127
  1114.5 17.9 copy.34
  1152.1 369.1 %all_gather.3 = f32[2,128,128]{2,1,0:T(8,128)S(1)} all-gather(f32[2,16,128]{2,1,0:T(8,128)S(1)} %copy-done.1), channel_id=1, replica_groups=mesh['grp'=4,'mem'=8] {'mem'}, dimensions={1}, use_global_device_ids=true | all-gather | bytes 147456 | tf_op jit(solution)/shard_map/all_gather | solution.py:114
  1646.7 20.5 %reshape.233 = f32[64,64,1024]{2,1,0:T(8,128)} reshape(f32[64,32,2,1024]{3,2,1,0:T(2,128)} %broadcast_in_dim.45) | data formatting | bytes 33554432 | tf_op jit(solution)/shard_map/reshape | solution.py:149
  1680.6 20.5 %reshape.230 = f32[64,64,1024]{2,1,0:T(8,128)} reshape(f32[64,32,2,1024]{3,2,1,0:T(2,128)} %broadcast_in_dim.27) | data formatting | bytes 33554432 | tf_op jit(solution)/shard_map/reshape | solution.py:148
  1701.1 23.7 %reshape.225 = bf16[64,64,8,2,128]{4,3,1,0,2:T(2,128)(2,1)} reshape(bf16[64,64,8,256]{3,1,0,2:T(8,128)(2,1)} %bitcast.18) | data formatting | bytes 33554432 | tf_op jit(solution)/shard_map/reshape | solution.py:135
  1724.7 37.8 %fusion.92 = (bf16[64,64,8,1,128]{4,3,1,0,2:T(2,128)(2,1)S(1)}, bf16[64,64,8,1,128]{4,3,1,0,2:T(2,128)(2,1)}) fusion(bf16[64,64,8,2,128]{4,3,1,0,2:T(2,128)(2,1)} %reshape.225), kind=kLoop, calls=%fused_computation.146 | loop fusion | bytes 33554432 | tf_op jit(solution)/shard_map/slice | solution.py:136
  1762.5 39.0 %copy_convert_fusion = (f32[64,64,8,1,128]{4,2,1,0,3:T(8,128)}, f32[64,64,8,1,128]{4,2,1,0,3:T(8,128)}) fusion(bf16[64,64,8,1,128]{4,3,1,0,2:T(2,128)(2,1)} %get-tuple-element.11, bf16[64,64,8,1,128]{4,3,1,0,2:T(2,128)(2,1)S(1)} %get-tuple-element.10), kind=kLoop, calls=%fused_computation.28 | loop fusion | flops 8388608 | bytes 50331648 | tf_op jit(solution)/shard_map/convert_element_type | solution.py:96
  1801.5 18.0 reshape.234
  1819.5 18.0 reshape.235
  1837.5 34.1 %subtract_divide_fusion = (f32[64,64,1024]{2,1,0:T(8,128)}, f32[64,64,1024]{2,1,0:T(8,128)}) fusion(f32[64,64,1024]{2,1,0:T(8,128)} %reshape.234, f32[64,64,1024]{2,1,0:T(8,128)} %reshape.233, f32[64,64,1024]{2,1,0:T(8,128)} %reshape.235, f32[64,64,1024]{2,1,0:T(8,128)} %reshape.230), kind=kLoop, calls=%fused_computation.15 | loop fusion | flops 50331648 | bytes 100663296 | tf_op jit(solution)/shard_map/div | solution.py:99
  (50 shorter events, 206.1 us)
Async XLA Ops:
  600.4 372.5 %all-to-all-start.1 = ((f32[128,256,256]{2,0,1:T(8,128)}), f32[128,256,256]{2,0,1:T(8,128)}, u32[]{:S(2)}, u32[]{:S(2)}) async-start(f32[128,256,256]{2,0,1:T(8,128)} %copy.32), calls=%async_computation.1 | async-start | bytes 67108864 | tf_op jit(solution)/shard_map/all_to_all | solution.py:125
  1132.4 568.6 %all-to-all-start.2 = ((bf16[512,64,256]{2,1,0:T(8,128)(2,1)}), bf16[512,64,256]{2,1,0:T(8,128)(2,1)}, u32[]{:S(2)}, u32[]{:S(2)}) async-start(bf16[512,64,256]{2,1,0:T(8,128)(2,1)} %copy.34), calls=%async_computation.2 | async-start | bytes 33554432 | tf_op jit(solution)/shard_map/all_to_all | solution.py:130
  1138.2 13.9 copy-start.1
  1591.3 3.7 copy-start
where the time goes:
time: 1880 us; the launch traced here: 1870 us
  blocking collectives  741 us (39%)
  local copies, waits for them, and re-layouts  397 us (21%)
  waiting for transfers between devices  359 us (19%)
  other arithmetic  186 us (10%)
  matrix products  173 us (9%)
    all_to_all x1, blocking collectives, shards(): lax.all_to_all(spatial, 'mem', split_axis=2, concat_axis=1, tiled=True)  372 us
    all_gather x1, blocking collectives, shards(): whole_probe = lax.all_gather(probe_wave, 'mem', axis=1, tiled=True)  369 us
    all_to_all x1, waiting for transfers between devices, shards(): lax.all_to_all(partial_x, 'grp', split_axis=1, concat_axis=0, tiled=True)  359 us
    dot_general x1, matrix products, shards(): jnp.einsum('rbc,rq->qbc', gathered, cy_re.astype(jnp.float32), precision=...  52.1 us
    dot_general x1, matrix products, shards(): jnp.einsum('rbc,rq->qbc', swap_halves(gathered), cy_im.astype(jnp.float32...  44.5 us
    convert_element_type x1, other arithmetic, deconvolve(): imag_part = spec_im.astype(jnp.float32)  39 us
    gather x4, local copies, waits for them, and re-layouts, shifted(): picked = jnp.take(picked, col_index, axis=2)  38.7 us
    slice x1, local copies, waits for them, and re-layouts, shards(): spec_re = unpacked[:, :, :, 0, :].reshape(qy_dev, qx_dev, pixels)  37.8 us
  transfers between devices with their start and end apart: 2, of which 1 were waited for; matrix products, arithmetic and copies ran while one was open for 11% of the time, Pallas kernels for 0%

commit v1 on v0

v1 whole, which is shorter than its diff:
```python
import math

import jax
import jax.numpy as jnp
import numpy as np
from jax import lax
from jax.experimental import pallas as pl
from jax.experimental.pallas import tpu as pltpu
from jax.sharding import PartitionSpec as P
import ml_dtypes

WIN = 32
STRIDE_Y = 4
STRIDE_X = 2
LANES = 128
U_TILE = 16
VMEM_BYTES = 56 * 1024 * 1024

wiener_floor = 0.5


def rounded(values):
    return values.astype(np.float32).astype(ml_dtypes.bfloat16)


def scan_table(length):
    positions = np.arange(length)
    angles = -2.0 * math.pi / length * (positions[:, None] * positions[None, :] % length)
    factor = 1.0 / math.sqrt(length)
    return rounded(np.cos(angles) * factor), rounded(np.sin(angles) * factor)


def detector_parts(window):
    offsets = np.arange(window)
    phases = (
        offsets[:, None, None, None] * offsets[None, None, :, None]
        + offsets[None, :, None, None] * offsets[None, None, None, :]
    ) % window
    angles = -2.0 * math.pi / window * phases.reshape(window * window, window * window)
    factor = 1.0 / window
    return rounded(np.cos(angles) * factor), rounded(np.sin(angles) * factor)


def y_table(length, owners):
    t_re, t_im = scan_table(length)
    both = np.stack([t_re.T, t_im.T], axis=0).reshape(2, owners, length // owners, length)
    return both.transpose(1, 0, 2, 3).reshape(2 * length, length)


def x_table(length, owners, senders, x_parts):
    t_re, t_im = scan_table(length)
    upper = np.stack([t_re.T, -t_im.T], axis=1)
    lower = np.stack([t_im.T, t_re.T], axis=1)
    both = np.stack([upper, lower], axis=0)
    width = length // owners
    both = both.reshape(2, owners, width, 2, senders, x_parts, length // senders // x_parts)
    both = both.transpose(1, 0, 2, 3, 5, 4, 6)
    return both.reshape(owners, 2 * width, 2 * length)


def pixel_table(window, depth):
    d_re, d_im = detector_parts(window)
    pixels = window * window
    upper = np.concatenate([d_re, d_im], axis=1).reshape(pixels // depth, depth, 2 * pixels)
    lower = np.concatenate([-d_im, d_re], axis=1).reshape(pixels // depth, depth, 2 * pixels)
    return np.stack([upper, lower], axis=1).reshape(pixels // depth, 2 * depth, 2 * pixels)


def params():
    return pltpu.CompilerParams(vmem_limit_bytes=VMEM_BYTES)


def y_transform(table, pieces, owners, u_chunks):
    n_x, n_y, depth = pieces[0].shape
    per_owner = table.shape[0] // owners
    u_own = per_owner // 2
    step = 2

    def body(t_ref, *refs):
        ins, outs = refs[: len(pieces)], refs[len(pieces) :]
        cols = []
        for i in range(step):
            cols.append(jnp.concatenate([p[i] for p in ins], axis=0))
        if depth == LANES:
            rhs = jnp.concatenate(cols, axis=1)
            res = jnp.dot(t_ref[...], rhs, preferred_element_type=jnp.float32)
            parts = [res[:, i * depth : (i + 1) * depth] for i in range(step)]
        else:
            parts = [jnp.dot(t_ref[...], c, preferred_element_type=jnp.float32) for c in cols]
        for i in range(step):
            res = parts[i].astype(jnp.bfloat16)
            for o_ref, (first, count) in zip(outs, u_chunks):
                for d in range(owners):
                    for r in range(2):
                        row = d * per_owner + r * u_own + first
                        o_ref[d, i, r * count : (r + 1) * count, :] = res[row : row + count]

    out_shape = [
        jax.ShapeDtypeStruct((owners, n_x, 2 * count, depth), jnp.bfloat16) for _, count in u_chunks
    ]
    flops = 2 * table.shape[0] * table.shape[1] * n_x * depth
    moved = 2 * n_x * depth * (table.shape[0] + table.shape[1]) + 2 * table.size
    return pl.pallas_call(
        body,
        grid=(n_x // step,),
        in_specs=[pl.BlockSpec(table.shape, lambda s: (0, 0))]
        + [pl.BlockSpec((step, n_y, depth), lambda s: (s, 0, 0)) for _ in pieces],
        out_specs=[
            pl.BlockSpec((owners, step, 2 * count, depth), lambda s: (0, s, 0, 0))
            for _, count in u_chunks
        ],
        out_shape=out_shape,
        compiler_params=params(),
        cost_estimate=pl.CostEstimate(flops=flops, bytes_accessed=moved, transcendentals=0),
        name="y_transform",
    )(table, *pieces)


def x_transform(table, parts, owners):
    senders, width, rows, depth = parts[0].shape
    n_u = rows // 2
    v_own = table.shape[0] // owners // 2
    views = [p.reshape(senders * width, 2, n_u, depth) for p in parts]
    pair = 2

    def body(t_ref, *refs):
        ins, outs = refs[: len(views)], refs[len(views) :]
        turned = [[jnp.swapaxes(p[:, r], 0, 1) for p in ins] for r in range(2)]
        for u in range(0, U_TILE, pair):
            cols = [
                jnp.concatenate([turned[r][h][u + i] for r in range(2) for h in range(len(ins))], axis=0)
                for i in range(pair)
            ]
            if depth == LANES:
                rhs = jnp.concatenate(cols, axis=1)
                res = jnp.dot(t_ref[...], rhs, preferred_element_type=jnp.float32)
                made = [res[:, i * depth : (i + 1) * depth] for i in range(pair)]
            else:
                made = [jnp.dot(t_ref[...], c, preferred_element_type=jnp.float32) for c in cols]
            for i in range(pair):
                res = made[i].astype(jnp.bfloat16)
                for d in range(owners):
                    for r in range(2):
                        row = (2 * d + r) * v_own
                        outs[d][u + i, r] = res[row : row + v_own]

    flops = 2 * table.size * n_u * depth
    moved = 4 * sum(p.size for p in parts) + 2 * table.size
    return pl.pallas_call(
        body,
        grid=(n_u // U_TILE,),
        in_specs=[pl.BlockSpec(table.shape, lambda s: (0, 0))]
        + [pl.BlockSpec((senders * width, 2, U_TILE, depth), lambda s: (0, 0, s, 0)) for _ in views],
        out_specs=[
            pl.BlockSpec((U_TILE, 2, v_own, depth), lambda s: (s, 0, 0, 0)) for _ in range(owners)
        ],
        out_shape=[
            jax.ShapeDtypeStruct((n_u, 2, v_own, depth), jnp.bfloat16) for _ in range(owners)
        ],
        compiler_params=params(),
        cost_estimate=pl.CostEstimate(flops=flops, bytes_accessed=moved, transcendentals=0),
        name="x_transform",
    )(table, *views)


def chi_factors(product, table, count_y, v_own):
    rows, inner = product.shape
    pixels = table.shape[1] // 2
    lanes = 256

    def body(p_ref, t_ref, re_ref, im_ref):
        for n in range(pixels // lanes):
            at = slice(n * lanes, (n + 1) * lanes)
            to = slice(pixels + n * lanes, pixels + (n + 1) * lanes)
            c_re = jnp.dot(p_ref[...], t_ref[:, at], preferred_element_type=jnp.float32)
            c_im = jnp.dot(p_ref[...], t_ref[:, to], preferred_element_type=jnp.float32)
            scale = 1.0 / (c_re * c_re + c_im * c_im + wiener_floor)
            re_ref[0, :, at] = c_re * scale
            im_ref[0, :, at] = c_im * scale

    return pl.pallas_call(
        body,
        grid=(count_y,),
        in_specs=[
            pl.BlockSpec((v_own, inner), lambda s: (s, 0)),
            pl.BlockSpec(table.shape, lambda s: (0, 0)),
        ],
        out_specs=[pl.BlockSpec((1, v_own, pixels), lambda s: (s, 0, 0))] * 2,
        out_shape=[jax.ShapeDtypeStruct((count_y, v_own, pixels), jnp.float32)] * 2,
        compiler_params=params(),
        cost_estimate=pl.CostEstimate(
            flops=2 * rows * table.size, bytes_accessed=2 * table.size + 8 * rows * pixels, transcendentals=0
        ),
        name="chi_factors",
    )(product, table)


def pixel_transform(table, early, late, factor_re, factor_im, first, count, total_u, previous):
    inner = table.shape[0]
    pixels = table.shape[1] // 2
    v_own, depth = late[0].shape[2:]
    step = STRIDE_Y
    rows = step * v_own
    lanes = 256
    base = first // step
    n_early, n_late = len(early), len(late)

    def body(t_ref, cr_ref, ci_ref, *refs):
        ins = refs[: n_early + n_late]
        re_ref, im_ref = refs[-2:]
        cuts = [p[:, r].reshape(rows, depth) for p in ins for r in range(2)]
        if depth == LANES:
            cuts = [jnp.concatenate(cuts, axis=1)]
        size = inner // len(cuts)

        def total(at):
            made = None
            for i, cut in enumerate(cuts):
                term = jnp.dot(cut, t_ref[i * size : (i + 1) * size, at], preferred_element_type=jnp.float32)
                made = term if made is None else made + term
            return made.reshape(step, v_own, lanes)

        for n in range(pixels // lanes):
            at = slice(n * lanes, (n + 1) * lanes)
            s_re = total(at)
            s_im = total(slice(pixels + n * lanes, pixels + (n + 1) * lanes))
            c_re = cr_ref[:, :, at]
            c_im = ci_ref[:, :, at]
            re_ref[:, :, at] = s_re * c_re + s_im * c_im
            im_ref[:, :, at] = s_im * c_re - s_re * c_im

    factor_spec = pl.BlockSpec((1, v_own, pixels), lambda s: (base + s, 0, 0))
    out_spec = pl.BlockSpec((step, v_own, pixels), lambda s: (base + s, 0, 0))
    shape = jax.ShapeDtypeStruct((total_u, v_own, pixels), jnp.float32)
    operands = [table, factor_re, factor_im, *early, *late]
    aliases = {}
    for i, array in enumerate(previous):
        aliases[len(operands)] = i
        operands.append(array)
    return pl.pallas_call(
        body,
        grid=(count // step,),
        in_specs=[pl.BlockSpec(table.shape, lambda s: (0, 0)), factor_spec, factor_spec]
        + [pl.BlockSpec((step, 2, v_own, depth), lambda s: (base + s, 0, 0, 0)) for _ in early]
        + [pl.BlockSpec((step, 2, v_own, depth), lambda s: (s, 0, 0, 0)) for _ in late]
        + [pl.BlockSpec(memory_space=pl.ANY) for _ in previous],
        out_specs=[out_spec] * 2,
        out_shape=[shape] * 2,
        input_output_aliases=aliases,
        compiler_params=params(),
        cost_estimate=pl.CostEstimate(
            flops=2 * count * v_own * table.size,
            bytes_accessed=2 * table.size + 12 * count * v_own * pixels,
            transcendentals=0,
        ),
        name="pixel_transform",
    )(*operands)


def signed_shift(freqs, length, step_size):
    centred = jnp.where(freqs >= length // 2, freqs - length, freqs)
    return jnp.floor_divide(centred, step_size)


def probe_product(probe, shift_y, shift_x, repeat, depth):
    grid_size = probe.shape[-1]
    offsets = jnp.arange(WIN, dtype=jnp.int32)
    row_index = (offsets[None, :] + shift_y[:, None]) % grid_size
    col_index = (offsets[None, :] + shift_x[:, None]) % grid_size
    count_y = shift_y.shape[0]
    count_x = shift_x.shape[0]
    pixels = WIN * WIN

    def shifted(plane):
        picked = jnp.take(plane, row_index, axis=0)
        picked = jnp.take(picked, col_index, axis=2)
        return picked.transpose(0, 2, 1, 3).reshape(count_y, count_x, pixels)

    moved_re = shifted(probe[0])
    moved_im = shifted(probe[1])
    base_re = probe[0, :WIN, :WIN].reshape(1, 1, pixels)
    base_im = probe[1, :WIN, :WIN].reshape(1, 1, pixels)
    prod_re = (base_re * moved_re + base_im * moved_im).astype(jnp.bfloat16)
    prod_im = (base_im * moved_re - base_re * moved_im).astype(jnp.bfloat16)
    blocks = []
    for b in range(pixels // depth):
        blocks.append(prod_re[..., b * depth : (b + 1) * depth])
        blocks.append(prod_im[..., b * depth : (b + 1) * depth])
    stacked = jnp.concatenate(blocks, axis=-1)
    stacked = jnp.repeat(stacked, repeat, axis=1)
    return stacked.reshape(count_y * count_x * repeat, 2 * pixels)


def swap(array, partner, size):
    return lax.ppermute(array, "grp", [(i, i ^ partner) for i in range(size)])


def shards(frames, probe_wave):
    n_grp, n_mem = lax.axis_size("grp"), lax.axis_size("mem")
    grp, mem = lax.axis_index("grp"), lax.axis_index("mem")
    n_y, n_x, pixels = frames.shape
    scan_y, scan_x = n_y * n_grp, n_x * n_mem
    u_own, v_own = scan_y // n_mem, scan_x // n_grp
    depth = min(LANES, pixels // n_grp)
    n_q = pixels // (n_grp * depth)
    partners = grp ^ jnp.arange(n_grp, dtype=jnp.int32)
    x_parts = 2 if n_x >= 32 else 1
    width = n_x // x_parts

    if u_own >= 4 * U_TILE:
        sizes = [u_own // 2, u_own // 4, u_own // 4]
    else:
        sizes = [U_TILE] * (u_own // U_TILE)
    late_chunks = []
    for size in sizes:
        late_chunks.append((sum(c for _, c in late_chunks), size))

    whole_probe = lax.all_gather(probe_wave, "mem", axis=1, tiled=True)

    def cut(q, first, count):
        made = []
        for j in range(n_grp):
            at = (q * n_grp + (grp ^ j)) * depth
            piece = lax.dynamic_slice(frames, (0, first, at), (n_y, count, depth))
            made.append(piece.transpose(1, 0, 2))
        return made

    def exchange(pieces):
        return [pieces[0]] + [swap(pieces[j], j, n_grp) for j in range(1, n_grp)]

    def to_owners(array):
        return lax.all_to_all(array, "mem", split_axis=0, concat_axis=0, tiled=True)

    ty = jnp.asarray(y_table(scan_y, n_mem)).reshape(2 * scan_y, n_grp, n_y)
    ty = jnp.take(ty, partners, axis=1).reshape(2 * scan_y, scan_y)
    tx, tx_late = (
        jnp.take(jnp.asarray(x_table(scan_x, n_grp, n_mem, parts)), partners, axis=0).reshape(
            2 * scan_x, 2 * scan_x
        )
        for parts in (x_parts, 1)
    )
    tk_all = jnp.asarray(pixel_table(WIN, depth))
    blocks = (jnp.arange(n_q, dtype=jnp.int32)[:, None] * n_grp + partners[None, :]).reshape(-1)
    tk = jnp.take(tk_all, blocks, axis=0).reshape(2 * pixels, 2 * pixels)
    tk_all = tk_all.reshape(2 * pixels, 2 * pixels)

    fronts = [(q, h * width, width) for q in range(n_q - 1) for h in range(x_parts)]
    fronts.append((n_q - 1, 0, n_x))
    pieces = exchange(cut(*fronts[0]))
    early_sent = []
    ready = None
    for i in range(len(fronts) - 1):
        (ready,) = y_transform(ty, pieces, n_mem, [(0, u_own)])
        following = cut(*fronts[i + 1])
        ready, following = lax.optimization_barrier((ready, following))
        early_sent.append(to_owners(ready))
        pieces = exchange(following)
    late_ready = y_transform(ty, pieces, n_mem, late_chunks)

    shift_y = signed_shift(
        mem * u_own + STRIDE_Y * jnp.arange(u_own // STRIDE_Y, dtype=jnp.int32), scan_y, STRIDE_Y
    )
    shift_x = signed_shift(
        grp * v_own + STRIDE_X * jnp.arange(v_own // STRIDE_X, dtype=jnp.int32), scan_x, STRIDE_X
    )
    product = probe_product(whole_probe, shift_y, shift_x, STRIDE_X, depth)
    factor_re, factor_im = chi_factors(product, tk_all, u_own // STRIDE_Y, v_own)

    early = []
    waiting = [early_sent[q * x_parts : (q + 1) * x_parts] for q in range(n_q - 1)]
    late = []
    for c in range(len(late_chunks)):
        sending = late_ready[c]
        if c == 0:
            sending, waiting = lax.optimization_barrier((sending, waiting))
            arrived = to_owners(sending)
            for parts in waiting:
                early += exchange(x_transform(tx, parts, n_grp))
        else:
            sending, previous = lax.optimization_barrier((sending, arrived))
            arrived = to_owners(sending)
            late.append(exchange(x_transform(tx_late, [previous], n_grp)))
    late.append(exchange(x_transform(tx_late, [arrived], n_grp)))

    outs = []
    for (first, count), pieces in zip(late_chunks, late):
        outs = pixel_transform(tk, early, pieces, factor_re, factor_im, first, count, u_own, outs)
    return tuple(outs)


def solution(mesh):
    return jax.shard_map(
        shards,
        mesh=mesh,
        in_specs=(P("grp", "mem", None), P(None, "mem", None)),
        out_specs=(P("mem", "grp", None), P("mem", "grp", None)),
        check_vma=False,
    )
```

time: 1880 us -> 678 us (0.36)
  blocking collectives: 741 us -> 112 us
  local copies, waits for them, and re-layouts: 397 us -> 112 us
  matrix products: 173 us -> 0 us
  other arithmetic: 186 us -> 25 us
  Pallas kernels: 0 us -> 140 us
  waiting for transfers between devices: 359 us -> 245 us
  starting transfers between devices: 15.5 us -> 39.2 us
    all_to_all x1 -> x0, blocking collectives: 372 us -> none  [shards(): lax.all_to_all(spatial, 'mem', split_axis=2, concat_axis=1, tiled=True)]
    all_to_all x2 -> x5, waiting for transfers between devices: 359 us -> 94.6 us  [to_owners(): return lax.all_to_all(array, 'mem', split_axis=0, concat_axis=0, tiled=True)]
    all_gather x1, blocking collectives: 369 us -> 112 us  [shards(): whole_probe = lax.all_gather(probe_wave, 'mem', axis=1, tiled=True)]
    dot_general x6 -> x0, matrix products: 173 us -> none  [the longest x1 52.1 us: shards(): jnp.einsum('rbc,rq->qbc', gathered, cy_re.astype(jnp.float32), precision=...]
    ppermute x0 -> x21, waiting for transfers between devices: none -> 150 us  [swap(): return lax.ppermute(array, 'grp', [(i, i ^ partner) for i in range(size)])]
    pallas_call x0 -> x11, Pallas kernels: none -> 140 us  [the longest x3 55.3 us: pixel_transform(): pl.pallas_call(body, grid=(count // step,), in_specs=[pl.BlockSpec(table....]
    reshape x6 -> x2, local copies, waits for them, and re-layouts: 105 us -> 14.3 us  [shifted(): return picked.transpose(0, 2, 1, 3).reshape(count_y, count_x, pixels)]
    convert_element_type x4 -> x0, local copies, waits for them, and re-layouts: 76.5 us -> none  [the longest x1 22.6 us: shards(): jnp.dot(flat_rows, merged, preferred_element_type=jnp.float32)]
  transfers between devices with their start and end apart: 2 -> 26, of which waited for: 1 -> 14; matrix products, arithmetic and copies ran while one was open for 11% -> 19% of each run, Pallas kernels for 0% -> 17%
where the time goes in v1:
time: 678 us; the launch traced here: 674 us
  waiting for transfers between devices  245 us (36%)
  Pallas kernels  140 us (21%)
  local copies, waits for them, and re-layouts  112 us (17%)
  blocking collectives  112 us (17%)
  starting transfers between devices  39.2 us (6%)
  other arithmetic  25 us (4%)
    ppermute x21, waiting for transfers between devices, swap(): return lax.ppermute(array, 'grp', [(i, i ^ partner) for i in range(size)])  150 us
    all_gather x1, blocking collectives, shards(): whole_probe = lax.all_gather(probe_wave, 'mem', axis=1, tiled=True)  112 us
    all_to_all x5, waiting for transfers between devices, to_owners(): return lax.all_to_all(array, 'mem', split_axis=0, concat_axis=0, tiled=True)  94.6 us
    pallas_call x3, Pallas kernels, pixel_transform(): pl.pallas_call(body, grid=(count // step,), in_specs=[pl.BlockSpec(table....  55.3 us
    gather x4, local copies, waits for them, and re-layouts, shifted(): picked = jnp.take(picked, col_index, axis=2)  38.7 us
    pallas_call x3, Pallas kernels, y_transform(): pl.pallas_call(body, grid=(n_x // step,), in_specs=[pl.BlockSpec(table.sh...  30.7 us
    pallas_call x1, Pallas kernels, chi_factors(): pl.pallas_call(body, grid=(count_y,), in_specs=[pl.BlockSpec((v_own, inne...  30 us
    all_to_all x5, starting transfers between devices, to_owners(): return lax.all_to_all(array, 'mem', split_axis=0, concat_axis=0, tiled=True)  24.2 us
  transfers between devices with their start and end apart: 26, of which 14 were waited for; matrix products, arithmetic and copies ran while one was open for 19% of the time, Pallas kernels for 17%

profile of v1, /device:TPU:0, one launch (start us, length us, event | category | flops | bytes accessed | tf_op | source)
XLA Modules:
  0.0 674.2 jit_solution(2973003606901798230)
XLA Ops:
  20.9 10.8 %collective-permute-done.2.refs_3_ = bf16[16,128,128]{2,1,0:T(8,128)(2,1)} collective-permute-done((bf16[16,128,128]{2,1,0:T(8,128)(2,1)}, bf16[16,128,128]{2,1,0:T(8,128)(2,1)}, u32[]{:S(2)}, u32[]{:S(2)}) %collective-permute-start.2) | collective-permute-done | bytes 524320 | tf_op jit(solution)/shard_map/ppermute | solution.py:295
  53.6 10.3 %collective-permute-done.4.refs_2_ = bf16[16,128,128]{2,1,0:T(8,128)(2,1)S(1)} collective-permute-done((bf16[16,128,128]{2,1,0:T(8,128)(2,1)S(1)}, bf16[16,128,128]{2,1,0:T(8,128)(2,1)S(1)}, u32[]{:S(2)}, u32[]{:S(2)}) %collective-permute-start.4) | collective-permute-done | bytes 524320 | tf_op jit(solution)/shard_map/ppermute | solution.py:295
  63.9 10.3 %collective-permute-done.5.refs_3_ = bf16[16,128,128]{2,1,0:T(8,128)(2,1)S(1)} collective-permute-done((bf16[16,128,128]{2,1,0:T(8,128)(2,1)S(1)}, bf16[16,128,128]{2,1,0:T(8,128)(2,1)S(1)}, u32[]{:S(2)}, u32[]{:S(2)}) %collective-permute-start.5) | collective-permute-done | bytes 524320 | tf_op jit(solution)/shard_map/ppermute | solution.py:295
  83.0 56.3 %all-to-all-done = bf16[8,16,128,128]{3,2,1,0:T(8,128)(2,1)} async-done(((bf16[8,16,128,128]{3,2,1,0:T(8,128)(2,1)}), bf16[8,16,128,128]{3,2,1,0:T(8,128)(2,1)}, u32[]{:S(2)}, u32[]{:S(2)}) %all-to-all-start) | async-done | bytes 4194336 | tf_op jit(solution)/shard_map/all_to_all | solution.py:332
  146.7 23.4 %collective-permute-done.7.refs_2_ = bf16[32,128,128]{2,1,0:T(8,128)(2,1)S(1)} collective-permute-done((bf16[32,128,128]{2,1,0:T(8,128)(2,1)S(1)}, bf16[32,128,128]{2,1,0:T(8,128)(2,1)S(1)}, u32[]{:S(2)}, u32[]{:S(2)}) %collective-permute-start.7) | collective-permute-done | bytes 1048608 | tf_op jit(solution)/shard_map/ppermute | solution.py:295
  170.1 21.6 %collective-permute-done.8.refs_3_ = bf16[32,128,128]{2,1,0:T(8,128)(2,1)S(1)} collective-permute-done((bf16[32,128,128]{2,1,0:T(8,128)(2,1)S(1)}, bf16[32,128,128]{2,1,0:T(8,128)(2,1)S(1)}, u32[]{:S(2)}, u32[]{:S(2)}) %collective-permute-start.8) | collective-permute-done | bytes 1048608 | tf_op jit(solution)/shard_map/ppermute | solution.py:295
  192.6 14.6 %y_transform.5 = (bf16[8,32,64,128]{3,2,1,0:T(8,128)(2,1)}, bf16[8,32,32,128]{3,2,1,0:T(8,128)(2,1)}, bf16[8,32,32,128]{3,2,1,0:T(8,128)(2,1)}) custom-call(bf16[1024,512]{1,0:T(8,128)(2,1)} %bitcast_select_fusion.1.t_ref, bf16[32,128,128]{2,1,0:T(8,128)(2,1)} %get-tuple-element.53.refs_0_, bf16[32,128,128]{2,1,0:T(8,128)(2,1)} %copy-done.16, ...), custom_call_target="tpu_custom_call" | custom-call | flops 4294967296 | bytes 13631488 | tf_op jit(solution)/shard_map/y_transform/pallas_call | solution.py:103
  207.2 29.4 %all-to-all-done.1 = bf16[8,16,128,128]{3,2,1,0:T(8,128)(2,1)} async-done(((bf16[8,16,128,128]{3,2,1,0:T(8,128)(2,1)}), bf16[8,16,128,128]{3,2,1,0:T(8,128)(2,1)}, u32[]{:S(2)}, u32[]{:S(2)}) %all-to-all-start.1) | async-done | bytes 4194336 | tf_op jit(solution)/shard_map/all_to_all | solution.py:332
  241.8 112.1 %all_gather.3 = f32[2,128,128]{2,1,0:T(8,128)S(1)} all-gather(f32[2,16,128]{2,1,0:T(8,128)S(1)} %copy-done.15), channel_id=1, replica_groups=mesh['grp'=4,'mem'=8] {'mem'}, dimensions={1}, use_global_device_ids=true | all-gather | bytes 147456 | tf_op jit(solution)/shard_map/all_gather | solution.py:318
  359.5 10.4 %gather_fusion.3 = f32[1024,16,32]{2,1,0:T(8,128)} fusion(f32[16,32,128]{1,0,2:T(8,128)S(1)} %get-tuple-element.109, s32[1024]{0:T(1024)S(1)} %get-tuple-element.116), kind=kCustom, calls=%fused_computation.1.clone | custom fusion | bytes 4198400 | tf_op jit(solution)/shard_map/jit(_take)/gather | solution.py:276
  369.9 8.9 %copy.42 = f32[32,32,16,32]{1,3,0,2:T(8,128)} copy(f32[32,32,16,32]{3,2,1,0:T(8,128)} %bitcast.70) | data formatting | bytes 4194304 | tf_op jit(solution)/shard_map/jit(_take)/gather | solution.py:276
  378.9 10.4 %gather_fusion.5 = f32[1024,16,32]{2,1,0:T(8,128)} fusion(f32[16,32,128]{1,0,2:T(8,128)S(1)} %get-tuple-element.110, s32[1024]{0:T(1024)S(1)} %get-tuple-element.116), kind=kCustom, calls=%fused_computation.4.clone | custom fusion | bytes 4198400 | tf_op jit(solution)/shard_map/jit(_take)/gather | solution.py:276
  389.3 9.0 %copy.44 = f32[32,32,16,32]{1,3,0,2:T(8,128)} copy(f32[32,32,16,32]{3,2,1,0:T(8,128)} %bitcast.69) | data formatting | bytes 4194304 | tf_op jit(solution)/shard_map/jit(_take)/gather | solution.py:276
  398.3 11.1 %select_bitcast_fusion.1 = (f32[16,32,32,32]{3,2,1,0:T(8,128)}, f32[16,32,32,32]{3,2,1,0:T(8,128)}) fusion(f32[32,32,16,32]{1,3,0,2:T(8,128)} %copy.42, pred[32,32]{1,0:T(8,128)(4,1)S(1)} %compare_and_fusion, f32[32,32,16,32]{1,3,0,2:T(8,128)} %copy.44), kind=kLoop, calls=%fused_computation.10 | loop fusion | flops 1048576 | bytes 8389632 | tf_op jit(solution)/shard_map/transpose | solution.py:277
  434.6 8.3 %gather_fusion = bf16[8,256,2048]{2,1,0:T(8,128)(2,1)} fusion(bf16[8,256,2048]{2,1,0:T(8,128)(2,1)} %constant.147.clone, s32[1024]{0:T(1024)S(1)} %pad_clamp_fusion.3), kind=kCustom, calls=%fused_computation.6 | custom fusion | bytes 16777248 | tf_op jit(solution)/shard_map/jit(_take)/gather | solution.py:344
  449.0 9.5 %x_transform.4 = (bf16[64,2,64,128]{3,2,1,0:T(8,128)(2,1)}, bf16[64,2,64,128]{3,2,1,0:T(8,128)(2,1)}, bf16[64,2,64,128]{3,2,1,0:T(8,128)(2,1)}, bf16[64,2,64,128]{3,2,1,0:T(8,128)(2,1)}) custom-call(bf16[512,512]{1,0:T(8,128)(2,1)} %bitcast.76, bf16[128,2,64,128]{3,2,1,0:T(8,128)(2,1)} %bitcast.28.refs_0_, bf16[128,2,64,128]{3,2,1,0:T(8,128)(2,1)} %bitcast.29.refs_1_), custom_call_target="tpu_custom_call" | custom-call | flops 4294967296 | bytes 17301504 | tf_op jit(solution)/shard_map/x_transform/pallas_call | solution.py:149
  467.8 8.9 %all-to-all-done.3 = bf16[8,32,32,128]{3,2,1,0:T(8,128)(2,1)} async-done(((bf16[8,32,32,128]{3,2,1,0:T(8,128)(2,1)}), bf16[8,32,32,128]{3,2,1,0:T(8,128)(2,1)}, u32[]{:S(2)}, u32[]{:S(2)}) %all-to-all-start.3) | async-done | bytes 2097184 | tf_op jit(solution)/shard_map/all_to_all | solution.py:332
  506.8 30.0 %chi_factors.1 = (f32[16,64,1024]{2,1,0:T(8,128)}, f32[16,64,1024]{2,1,0:T(8,128)}) custom-call(bf16[1024,2048]{1,0:T(8,128)(2,1)} %reshape_reshape.3.p_ref, bf16[2048,2048]{1,0:T(8,128)(2,1)} %constant.148.t_ref), custom_call_target="tpu_custom_call" | custom-call | flops 8589934592 | bytes 16777216 | tf_op jit(solution)/shard_map/chi_factors/pallas_call | solution.py:181
  541.3 17.5 %collective-permute-done.11.refs_3_ = bf16[64,2,64,128]{3,2,1,0:T(8,128)(2,1)} collective-permute-done((bf16[64,2,64,128]{3,2,1,0:T(8,128)(2,1)}, bf16[64,2,64,128]{3,2,1,0:T(8,128)(2,1)}, u32[]{:S(2)}, u32[]{:S(2)}) %collective-permute-start.11) | collective-permute-done | bytes 2097184 | tf_op jit(solution)/shard_map/ppermute | solution.py:295
  560.8 21.3 %collective-permute-done.19.refs_6_ = bf16[32,2,64,128]{3,2,1,0:T(8,128)(2,1)} collective-permute-done((bf16[32,2,64,128]{3,2,1,0:T(8,128)(2,1)}, bf16[32,2,64,128]{3,2,1,0:T(8,128)(2,1)}, u32[]{:S(2)}, u32[]{:S(2)}) %collective-permute-start.19) | collective-permute-done | bytes 1048608 | tf_op jit(solution)/shard_map/ppermute | solution.py:295
  582.1 21.7 %collective-permute-done.20.refs_7_ = bf16[32,2,64,128]{3,2,1,0:T(8,128)(2,1)} collective-permute-done((bf16[32,2,64,128]{3,2,1,0:T(8,128)(2,1)}, bf16[32,2,64,128]{3,2,1,0:T(8,128)(2,1)}, u32[]{:S(2)}, u32[]{:S(2)}) %collective-permute-start.20) | collective-permute-done | bytes 1048608 | tf_op jit(solution)/shard_map/ppermute | solution.py:295
  603.8 24.8 %pixel_transform.3 = (f32[64,64,1024]{2,1,0:T(8,128)}, f32[64,64,1024]{2,1,0:T(8,128)}) custom-call(bf16[2048,2048]{1,0:T(8,128)(2,1)} %bitcast_select_fusion.t_ref, f32[16,64,1024]{2,1,0:T(8,128)} %get-tuple-element.47.cr_ref, f32[16,64,1024]{2,1,0:T(8,128)} %get-tuple-element.48.ci_ref, bf16[64,2,64,128]{3,2,1,0:T(8,128)(2,1)} %get-tuple-element.62.refs_0_, ...), custom_call_target="tpu_custom_call" | custom-call | flops 17179869184 | bytes 33554432 | tf_op jit(solution)/shard_map/pixel_transform/pallas_call | solution.py:240
  636.3 15.2 %pixel_transform.4 = (f32[64,64,1024]{2,1,0:T(8,128)}, f32[64,64,1024]{2,1,0:T(8,128)}) custom-call(bf16[2048,2048]{1,0:T(8,128)(2,1)} %bitcast_select_fusion.t_ref, f32[16,64,1024]{2,1,0:T(8,128)} %get-tuple-element.47.cr_ref, f32[16,64,1024]{2,1,0:T(8,128)} %get-tuple-element.48.ci_ref, ...), custom_call_target="tpu_custom_call", output_to_operand_aliasing={{0}: (11, {}), {1}: (12, {})} | custom-call | flops 8589934592 | bytes 20971520 | tf_op jit(solution)/shard_map/pixel_transform/pallas_call | solution.py:240
  658.8 15.2 %pixel_transform.5 = (f32[64,64,1024]{2,1,0:T(8,128)}, f32[64,64,1024]{2,1,0:T(8,128)}) custom-call(bf16[2048,2048]{1,0:T(8,128)(2,1)} %bitcast_select_fusion.t_ref, f32[16,64,1024]{2,1,0:T(8,128)} %get-tuple-element.47.cr_ref, f32[16,64,1024]{2,1,0:T(8,128)} %get-tuple-element.48.ci_ref, ...), custom_call_target="tpu_custom_call", output_to_operand_aliasing={{0}: (11, {}), {1}: (12, {})} | custom-call | flops 8589934592 | bytes 20971520 | tf_op jit(solution)/shard_map/pixel_transform/pallas_call | solution.py:240
  (160 shorter events, 161.8 us)
Async XLA Ops:
  3.9 10.8 %collective-permute-start = (bf16[16,128,128]{2,1,0:T(8,128)(2,1)S(1)}, bf16[16,128,128]{2,1,0:T(8,128)(2,1)}, u32[]{:S(2)}, u32[]{:S(2)}) collective-permute-start(bf16[16,128,128]{2,1,0:T(8,128)(2,1)S(1)} %bitcast.77), channel_id=1, source_target_pairs={{0,8},{8,0},{16,24},{24,16},{1,9},{9,1},{17,25},{25,17},{2,10},{10... | collective-permute-start | bytes 1572872 | tf_op jit(solution)/shard_map/ppermute | solution.py:295
  5.3 15.6 %collective-permute-start.1 = (bf16[16,128,128]{2,1,0:T(8,128)(2,1)}, bf16[16,128,128]{2,1,0:T(8,128)(2,1)}, u32[]{:S(2)}, u32[]{:S(2)}) collective-permute-start(bf16[16,128,128]{2,1,0:T(8,128)(2,1)} %bitcast.66), channel_id=1, source_target_pairs={{0,16},{8,24},{16,0},{24,8},{1,17},{9,25},{17,1},{25,9},{2,18},{10... | collective-permute-start | bytes 1572872 | tf_op jit(solution)/shard_map/ppermute | solution.py:295
  8.7 23.0 %collective-permute-start.2 = (bf16[16,128,128]{2,1,0:T(8,128)(2,1)}, bf16[16,128,128]{2,1,0:T(8,128)(2,1)}, u32[]{:S(2)}, u32[]{:S(2)}) collective-permute-start(bf16[16,128,128]{2,1,0:T(8,128)(2,1)} %bitcast.65), channel_id=1, source_target_pairs={{0,24},{8,16},{16,8},{24,0},{1,25},{9,17},{17,9},{25,1},{2,26},{10... | collective-permute-start | bytes 1572872 | tf_op jit(solution)/shard_map/ppermute | solution.py:295
  39.8 99.6 %all-to-all-start = ((bf16[8,16,128,128]{3,2,1,0:T(8,128)(2,1)}), bf16[8,16,128,128]{3,2,1,0:T(8,128)(2,1)}, u32[]{:S(2)}, u32[]{:S(2)}) async-start(bf16[8,16,128,128]{3,2,1,0:T(8,128)(2,1)} %y_transform.3), calls=%async_computation | async-start | bytes 8388608 | tf_op jit(solution)/shard_map/all_to_all | solution.py:332
  49.1 14.8 %collective-permute-start.4 = (bf16[16,128,128]{2,1,0:T(8,128)(2,1)S(1)}, bf16[16,128,128]{2,1,0:T(8,128)(2,1)S(1)}, u32[]{:S(2)}, u32[]{:S(2)}) collective-permute-start(bf16[16,128,128]{2,1,0:T(8,128)(2,1)S(1)} %copy-done.7), channel_id=1, source_target_pairs={{0,16},{8,24},{16,0},{24,8},{1,17},{9,25},{17,1},{25,9},{2,18},{10... | collective-permute-start | bytes 1572872 | tf_op jit(solution)/shard_map/ppermute | solution.py:295
  50.6 23.5 %collective-permute-start.5 = (bf16[16,128,128]{2,1,0:T(8,128)(2,1)S(1)}, bf16[16,128,128]{2,1,0:T(8,128)(2,1)S(1)}, u32[]{:S(2)}, u32[]{:S(2)}) collective-permute-start(bf16[16,128,128]{2,1,0:T(8,128)(2,1)S(1)} %copy-done.6), channel_id=1, source_target_pairs={{0,24},{8,16},{16,8},{24,0},{1,25},{9,17},{17,9},{25,1},{2,26},{10... | collective-permute-start | bytes 1572872 | tf_op jit(solution)/shard_map/ppermute | solution.py:295
  139.3 97.3 %all-to-all-start.1 = ((bf16[8,16,128,128]{3,2,1,0:T(8,128)(2,1)}), bf16[8,16,128,128]{3,2,1,0:T(8,128)(2,1)}, u32[]{:S(2)}, u32[]{:S(2)}) async-start(bf16[8,16,128,128]{3,2,1,0:T(8,128)(2,1)} %y_transform.4), calls=%async_computation.1 | async-start | bytes 8388608 | tf_op jit(solution)/shard_map/all_to_all | solution.py:332
  144.0 26.0 %collective-permute-start.7 = (bf16[32,128,128]{2,1,0:T(8,128)(2,1)S(1)}, bf16[32,128,128]{2,1,0:T(8,128)(2,1)S(1)}, u32[]{:S(2)}, u32[]{:S(2)}) collective-permute-start(bf16[32,128,128]{2,1,0:T(8,128)(2,1)S(1)} %get-tuple-element.55), channel_id=1, source_target_pairs={{0,16},{8,24},{16,0},{24,8},{1,17},{9,25},{17,1},{25,9},{2,18},{10... | collective-permute-start | bytes 3145736 | tf_op jit(solution)/shard_map/ppermute | solution.py:295
  145.6 46.0 %collective-permute-start.8 = (bf16[32,128,128]{2,1,0:T(8,128)(2,1)S(1)}, bf16[32,128,128]{2,1,0:T(8,128)(2,1)S(1)}, u32[]{:S(2)}, u32[]{:S(2)}) collective-permute-start(bf16[32,128,128]{2,1,0:T(8,128)(2,1)S(1)} %get-tuple-element.56), channel_id=1, source_target_pairs={{0,24},{8,16},{16,8},{24,0},{1,25},{9,17},{17,9},{25,1},{2,26},{10... | collective-permute-start | bytes 3145736 | tf_op jit(solution)/shard_map/ppermute | solution.py:295
  236.7 192.1 %all-to-all-start.2 = ((bf16[8,32,64,128]{3,2,1,0:T(8,128)(2,1)}), bf16[8,32,64,128]{3,2,1,0:T(8,128)(2,1)}, u32[]{:S(2)}, u32[]{:S(2)}) async-start(bf16[8,32,64,128]{3,2,1,0:T(8,128)(2,1)} %get-tuple-element.68), calls=%async_computation.2 | async-start | bytes 8388608 | tf_op jit(solution)/shard_map/all_to_all | solution.py:332
  428.8 47.9 %all-to-all-start.3 = ((bf16[8,32,32,128]{3,2,1,0:T(8,128)(2,1)}), bf16[8,32,32,128]{3,2,1,0:T(8,128)(2,1)}, u32[]{:S(2)}, u32[]{:S(2)}) async-start(bf16[8,32,32,128]{3,2,1,0:T(8,128)(2,1)} %get-tuple-element.69), calls=%async_computation.3 | async-start | bytes 4194304 | tf_op jit(solution)/shard_map/all_to_all | solution.py:332
  458.4 34.6 %collective-permute-start.9 = (bf16[64,2,64,128]{3,2,1,0:T(8,128)(2,1)}, bf16[64,2,64,128]{3,2,1,0:T(8,128)(2,1)S(1)}, u32[]{:S(2)}, u32[]{:S(2)}) collective-permute-start(bf16[64,2,64,128]{3,2,1,0:T(8,128)(2,1)} %get-tuple-element.63), channel_id=1, source_target_pairs={{0,8},{8,0},{16,24},{24,16},{1,9},{9,1},{17,25},{25,17},{2,10},{10... | collective-permute-start | bytes 6291464 | tf_op jit(solution)/shard_map/ppermute | solution.py:295
  466.0 75.2 %collective-permute-start.10 = (bf16[64,2,64,128]{3,2,1,0:T(8,128)(2,1)}, bf16[64,2,64,128]{3,2,1,0:T(8,128)(2,1)}, u32[]{:S(2)}, u32[]{:S(2)}) collective-permute-start(bf16[64,2,64,128]{3,2,1,0:T(8,128)(2,1)} %get-tuple-element.64), channel_id=1, source_target_pairs={{0,16},{8,24},{16,0},{24,8},{1,17},{9,25},{17,1},{25,9},{2,18},{10... | collective-permute-start | bytes 6291464 | tf_op jit(solution)/shard_map/ppermute | solution.py:295
  467.5 91.4 %collective-permute-start.11 = (bf16[64,2,64,128]{3,2,1,0:T(8,128)(2,1)}, bf16[64,2,64,128]{3,2,1,0:T(8,128)(2,1)}, u32[]{:S(2)}, u32[]{:S(2)}) collective-permute-start(bf16[64,2,64,128]{3,2,1,0:T(8,128)(2,1)} %get-tuple-element.65), channel_id=1, source_target_pairs={{0,24},{8,16},{16,8},{24,0},{1,25},{9,17},{17,9},{25,1},{2,26},{10... | collective-permute-start | bytes 6291464 | tf_op jit(solution)/shard_map/ppermute | solution.py:295
  476.7 152.0 %all-to-all-start.4 = ((bf16[8,32,32,128]{3,2,1,0:T(8,128)(2,1)}), bf16[8,32,32,128]{3,2,1,0:T(8,128)(2,1)}, u32[]{:S(2)}, u32[]{:S(2)}) async-start(bf16[8,32,32,128]{3,2,1,0:T(8,128)(2,1)} %get-tuple-element.70), calls=%async_computation.4 | async-start | bytes 4194304 | tf_op jit(solution)/shard_map/all_to_all | solution.py:332
  491.5 68.9 %collective-permute-start.18 = (bf16[32,2,64,128]{3,2,1,0:T(8,128)(2,1)}, bf16[32,2,64,128]{3,2,1,0:T(8,128)(2,1)}, u32[]{:S(2)}, u32[]{:S(2)}) collective-permute-start(bf16[32,2,64,128]{3,2,1,0:T(8,128)(2,1)} %get-tuple-element.82), channel_id=1, source_target_pairs={{0,8},{8,0},{16,24},{24,16},{1,9},{9,1},{17,25},{25,17},{2,10},{10... | collective-permute-start | bytes 3145736 | tf_op jit(solution)/shard_map/ppermute | solution.py:295
  491.5 90.7 %collective-permute-start.19 = (bf16[32,2,64,128]{3,2,1,0:T(8,128)(2,1)}, bf16[32,2,64,128]{3,2,1,0:T(8,128)(2,1)}, u32[]{:S(2)}, u32[]{:S(2)}) collective-permute-start(bf16[32,2,64,128]{3,2,1,0:T(8,128)(2,1)} %get-tuple-element.83), channel_id=1, source_target_pairs={{0,16},{8,24},{16,0},{24,8},{1,17},{9,25},{17,1},{25,9},{2,18},{10... | collective-permute-start | bytes 3145736 | tf_op jit(solution)/shard_map/ppermute | solution.py:295
  493.0 110.8 %collective-permute-start.20 = (bf16[32,2,64,128]{3,2,1,0:T(8,128)(2,1)}, bf16[32,2,64,128]{3,2,1,0:T(8,128)(2,1)}, u32[]{:S(2)}, u32[]{:S(2)}) collective-permute-start(bf16[32,2,64,128]{3,2,1,0:T(8,128)(2,1)} %get-tuple-element.84), channel_id=1, source_target_pairs={{0,24},{8,16},{16,8},{24,0},{1,25},{9,17},{17,9},{25,1},{2,26},{10... | collective-permute-start | bytes 3145736 | tf_op jit(solution)/shard_map/ppermute | solution.py:295
  541.2 94.0 %collective-permute-start.15 = (bf16[16,2,64,128]{3,2,1,0:T(8,128)(2,1)}, bf16[16,2,64,128]{3,2,1,0:T(8,128)(2,1)S(1)}, u32[]{:S(2)}, u32[]{:S(2)}) collective-permute-start(bf16[16,2,64,128]{3,2,1,0:T(8,128)(2,1)} %get-tuple-element.77), channel_id=1, source_target_pairs={{0,8},{8,0},{16,24},{24,16},{1,9},{9,1},{17,25},{25,17},{2,10},{10... | collective-permute-start | bytes 1572872 | tf_op jit(solution)/shard_map/ppermute | solution.py:295
  558.9 76.2 %collective-permute-start.16 = (bf16[16,2,64,128]{3,2,1,0:T(8,128)(2,1)}, bf16[16,2,64,128]{3,2,1,0:T(8,128)(2,1)S(1)}, u32[]{:S(2)}, u32[]{:S(2)}) collective-permute-start(bf16[16,2,64,128]{3,2,1,0:T(8,128)(2,1)} %get-tuple-element.78), channel_id=1, source_target_pairs={{0,16},{8,24},{16,0},{24,8},{1,17},{9,25},{17,1},{25,9},{2,18},{10... | collective-permute-start | bytes 1572872 | tf_op jit(solution)/shard_map/ppermute | solution.py:295
  560.4 74.8 %collective-permute-start.17 = (bf16[16,2,64,128]{3,2,1,0:T(8,128)(2,1)}, bf16[16,2,64,128]{3,2,1,0:T(8,128)(2,1)S(1)}, u32[]{:S(2)}, u32[]{:S(2)}) collective-permute-start(bf16[16,2,64,128]{3,2,1,0:T(8,128)(2,1)} %get-tuple-element.79), channel_id=1, source_target_pairs={{0,24},{8,16},{16,8},{24,0},{1,25},{9,17},{17,9},{25,1},{2,26},{10... | collective-permute-start | bytes 1572872 | tf_op jit(solution)/shard_map/ppermute | solution.py:295
  633.0 18.6 %collective-permute-start.12 = (bf16[16,2,64,128]{3,2,1,0:T(8,128)(2,1)}, bf16[16,2,64,128]{3,2,1,0:T(8,128)(2,1)S(1)}, u32[]{:S(2)}, u32[]{:S(2)}) collective-permute-start(bf16[16,2,64,128]{3,2,1,0:T(8,128)(2,1)} %get-tuple-element.72), channel_id=1, source_target_pairs={{0,8},{8,0},{16,24},{24,16},{1,9},{9,1},{17,25},{25,17},{2,10},{10... | collective-permute-start | bytes 1572872 | tf_op jit(solution)/shard_map/ppermute | solution.py:295
  633.6 18.0 %collective-permute-start.13 = (bf16[16,2,64,128]{3,2,1,0:T(8,128)(2,1)}, bf16[16,2,64,128]{3,2,1,0:T(8,128)(2,1)S(1)}, u32[]{:S(2)}, u32[]{:S(2)}) collective-permute-start(bf16[16,2,64,128]{3,2,1,0:T(8,128)(2,1)} %get-tuple-element.73), channel_id=1, source_target_pairs={{0,16},{8,24},{16,0},{24,8},{1,17},{9,25},{17,1},{25,9},{2,18},{10... | collective-permute-start | bytes 1572872 | tf_op jit(solution)/shard_map/ppermute | solution.py:295
  635.1 22.9 %collective-permute-start.14 = (bf16[16,2,64,128]{3,2,1,0:T(8,128)(2,1)}, bf16[16,2,64,128]{3,2,1,0:T(8,128)(2,1)S(1)}, u32[]{:S(2)}, u32[]{:S(2)}) collective-permute-start(bf16[16,2,64,128]{3,2,1,0:T(8,128)(2,1)} %get-tuple-element.74), channel_id=1, source_target_pairs={{0,24},{8,16},{16,8},{24,0},{1,25},{9,17},{17,9},{25,1},{2,26},{10... | collective-permute-start | bytes 1572872 | tf_op jit(solution)/shard_map/ppermute | solution.py:295
  (24 other events, 168.4 us)

commit v2 on v1

--- a/solution.py
+++ b/solution.py
@@ -47,15 +47,18 @@
     return both.transpose(1, 0, 2, 3).reshape(2 * length, length)
 
 
-def x_table(length, owners, senders, x_parts):
+def x_table(length, owners, senders, cuts):
     t_re, t_im = scan_table(length)
     upper = np.stack([t_re.T, -t_im.T], axis=1)
     lower = np.stack([t_im.T, t_re.T], axis=1)
     both = np.stack([upper, lower], axis=0)
     width = length // owners
-    both = both.reshape(2, owners, width, 2, senders, x_parts, length // senders // x_parts)
-    both = both.transpose(1, 0, 2, 3, 5, 4, 6)
-    return both.reshape(owners, 2 * width, 2 * length)
+    both = both.reshape(2, owners, width, 2, senders, length // senders).transpose(1, 0, 2, 3, 4, 5)
+    parts = [
+        both[..., first : first + count].reshape(owners, 2 * width, 2, senders * count)
+        for first, count in cuts
+    ]
+    return np.concatenate(parts, axis=-1).reshape(owners, 2 * width, 2 * length)
 
 
 def pixel_table(window, depth):
@@ -117,10 +120,10 @@
 
 
 def x_transform(table, parts, owners):
-    senders, width, rows, depth = parts[0].shape
+    rows, depth = parts[0].shape[2:]
     n_u = rows // 2
     v_own = table.shape[0] // owners // 2
-    views = [p.reshape(senders * width, 2, n_u, depth) for p in parts]
+    views = [p.reshape(p.shape[0] * p.shape[1], 2, n_u, depth) for p in parts]
     pair = 2
 
     def body(t_ref, *refs):
@@ -150,7 +153,7 @@
         body,
         grid=(n_u // U_TILE,),
         in_specs=[pl.BlockSpec(table.shape, lambda s: (0, 0))]
-        + [pl.BlockSpec((senders * width, 2, U_TILE, depth), lambda s: (0, 0, s, 0)) for _ in views],
+        + [pl.BlockSpec((v.shape[0], 2, U_TILE, depth), lambda s: (0, 0, s, 0)) for v in views],
         out_specs=[
             pl.BlockSpec((U_TILE, 2, v_own, depth), lambda s: (s, 0, 0, 0)) for _ in range(owners)
         ],
@@ -163,36 +166,54 @@
     )(table, *views)
 
 
-def chi_factors(product, table, count_y, v_own):
-    rows, inner = product.shape
-    pixels = table.shape[1] // 2
-    lanes = 256
-
-    def body(p_ref, t_ref, re_ref, im_ref):
-        for n in range(pixels // lanes):
-            at = slice(n * lanes, (n + 1) * lanes)
-            to = slice(pixels + n * lanes, pixels + (n + 1) * lanes)
-            c_re = jnp.dot(p_ref[...], t_ref[:, at], preferred_element_type=jnp.float32)
-            c_im = jnp.dot(p_ref[...], t_ref[:, to], preferred_element_type=jnp.float32)
+def chi_factors(windows, base, table, count_y):
+    n_rows, v_own, lanes = windows.shape[1:]
+    n_blocks = base.shape[1]
+    stride = lanes // WIN
+    inner, columns = table.shape
+    pixels = columns // 2
+    step = min(4, count_y)
+    wide = 256
+
+    def body(w_ref, b_ref, t_ref, re_ref, im_ref, left):
+        first = pl.program_id(0) * step
+        for i in range(step):
+            for b in range(n_blocks):
+                w_re = w_ref[0, first + i + b * stride]
+                w_im = w_ref[1, first + i + b * stride]
+                a_re = b_ref[0, b : b + 1]
+                a_im = b_ref[1, b : b + 1]
+                rows = slice(i * v_own, (i + 1) * v_own)
+                at = 2 * b * lanes
+                left[rows, at : at + lanes] = (a_re * w_re + a_im * w_im).astype(jnp.bfloat16)
+                left[rows, at + lanes : at + 2 * lanes] = (a_im * w_re - a_re * w_im).astype(jnp.bfloat16)
+        for n in range(pixels // wide):
+            at = slice(n * wide, (n + 1) * wide)
+            to = slice(pixels + n * wide, pixels + (n + 1) * wide)
+            c_re = jnp.dot(left[...], t_ref[:, at], preferred_element_type=jnp.float32)
+            c_im = jnp.dot(left[...], t_ref[:, to], preferred_element_type=jnp.float32)
             scale = 1.0 / (c_re * c_re + c_im * c_im + wiener_floor)
-            re_ref[0, :, at] = c_re * scale
-            im_ref[0, :, at] = c_im * scale
-
+            re_ref[:, :, at] = (c_re * scale).reshape(step, v_own, wide)
+            im_ref[:, :, at] = (c_im * scale).reshape(step, v_own, wide)
+
+    rows = count_y * v_own
     return pl.pallas_call(
         body,
-        grid=(count_y,),
+        grid=(count_y // step,),
         in_specs=[
-            pl.BlockSpec((v_own, inner), lambda s: (s, 0)),
+            pl.BlockSpec(windows.shape, lambda s: (0, 0, 0, 0)),
+            pl.BlockSpec(base.shape, lambda s: (0, 0, 0)),
             pl.BlockSpec(table.shape, lambda s: (0, 0)),
         ],
-        out_specs=[pl.BlockSpec((1, v_own, pixels), lambda s: (s, 0, 0))] * 2,
+        out_specs=[pl.BlockSpec((step, v_own, pixels), lambda s: (s, 0, 0))] * 2,
         out_shape=[jax.ShapeDtypeStruct((count_y, v_own, pixels), jnp.float32)] * 2,
+        scratch_shapes=[pltpu.VMEM((step * v_own, inner), jnp.bfloat16)],
         compiler_params=params(),
         cost_estimate=pl.CostEstimate(
             flops=2 * rows * table.size, bytes_accessed=2 * table.size + 8 * rows * pixels, transcendentals=0
         ),
         name="chi_factors",
-    )(product, table)
+    )(windows, base, table)
 
 
 def pixel_transform(table, early, late, factor_re, factor_im, first, count, total_u, previous):
@@ -262,37 +283,36 @@
     return jnp.floor_divide(centred, step_size)
 
 
-def probe_product(probe, shift_y, shift_x, repeat, depth):
+def probe_windows(probe, shift_y, shift_x, lanes):
     grid_size = probe.shape[-1]
-    offsets = jnp.arange(WIN, dtype=jnp.int32)
-    row_index = (offsets[None, :] + shift_y[:, None]) % grid_size
-    col_index = (offsets[None, :] + shift_x[:, None]) % grid_size
-    count_y = shift_y.shape[0]
+    stride = lanes // WIN
     count_x = shift_x.shape[0]
-    pixels = WIN * WIN
-
-    def shifted(plane):
-        picked = jnp.take(plane, row_index, axis=0)
-        picked = jnp.take(picked, col_index, axis=2)
-        return picked.transpose(0, 2, 1, 3).reshape(count_y, count_x, pixels)
-
-    moved_re = shifted(probe[0])
-    moved_im = shifted(probe[1])
-    base_re = probe[0, :WIN, :WIN].reshape(1, 1, pixels)
-    base_im = probe[1, :WIN, :WIN].reshape(1, 1, pixels)
-    prod_re = (base_re * moved_re + base_im * moved_im).astype(jnp.bfloat16)
-    prod_im = (base_im * moved_re - base_re * moved_im).astype(jnp.bfloat16)
-    blocks = []
-    for b in range(pixels // depth):
-        blocks.append(prod_re[..., b * depth : (b + 1) * depth])
-        blocks.append(prod_im[..., b * depth : (b + 1) * depth])
-    stacked = jnp.concatenate(blocks, axis=-1)
-    stacked = jnp.repeat(stacked, repeat, axis=1)
-    return stacked.reshape(count_y * count_x * repeat, 2 * pixels)
-
-
-def swap(array, partner, size):
-    return lax.ppermute(array, "grp", [(i, i ^ partner) for i in range(size)])
+    n_rows = shift_y.shape[0] + WIN - stride
+    rows = (shift_y[0] + jnp.arange(n_rows + stride - 1, dtype=jnp.int32)) % grid_size
+    columns = (shift_x[:, None] + jnp.arange(WIN, dtype=jnp.int32)[None, :]) % grid_size
+    picked = jnp.take(probe, rows, axis=1, mode="clip")
+    chosen = (jnp.arange(grid_size, dtype=jnp.int32)[:, None] == columns.reshape(1, -1)).astype(jnp.float32)
+    moved = jnp.einsum("prc,cm->prm", picked, chosen, precision=lax.Precision.HIGHEST)
+    moved = moved.reshape(2, n_rows + stride - 1, count_x, WIN)
+    return jnp.concatenate([moved[:, p : p + n_rows] for p in range(stride)], axis=-1)
+
+
+def swap(array, partner, axis):
+    size = lax.axis_size(axis)
+    return lax.ppermute(array, axis, [(i, i ^ partner) for i in range(size)])
+
+
+def gather_rows(block, axis):
+    rank = lax.axis_index(axis)
+    partner = 1
+    while partner < lax.axis_size(axis):
+        other = swap(block, partner, axis)
+        ahead = (rank & partner) > 0
+        block = jnp.concatenate(
+            [jnp.where(ahead, other, block), jnp.where(ahead, block, other)], axis=1
+        )
+        partner *= 2
+    return block
 
 
 def shards(frames, probe_wave):
@@ -304,18 +324,19 @@
     depth = min(LANES, pixels // n_grp)
     n_q = pixels // (n_grp * depth)
     partners = grp ^ jnp.arange(n_grp, dtype=jnp.int32)
-    x_parts = 2 if n_x >= 32 else 1
-    width = n_x // x_parts
+    if n_x >= 32:
+        opening = 2 * (n_x * 5 // 32)
+        x_cuts = [(0, opening), (opening, n_x - opening)]
+    else:
+        x_cuts = [(0, n_x)]
 
     if u_own >= 4 * U_TILE:
         sizes = [u_own // 2, u_own // 4, u_own // 4]
     else:
         sizes = [U_TILE] * (u_own // U_TILE)
-    late_chunks = []
+    u_chunks = []
     for size in sizes:
-        late_chunks.append((sum(c for _, c in late_chunks), size))
-
-    whole_probe = lax.all_gather(probe_wave, "mem", axis=1, tiled=True)
+        u_chunks.append((sum(c for _, c in u_chunks), size))
 
     def cut(q, first, count):
         made = []
@@ -326,65 +347,70 @@
         return made
 
     def exchange(pieces):
-        return [pieces[0]] + [swap(pieces[j], j, n_grp) for j in range(1, n_grp)]
+        return [pieces[0]] + [swap(pieces[j], j, "grp") for j in range(1, n_grp)]
 
     def to_owners(array):
         return lax.all_to_all(array, "mem", split_axis=0, concat_axis=0, tiled=True)
 
-    ty = jnp.asarray(y_table(scan_y, n_mem)).reshape(2 * scan_y, n_grp, n_y)
-    ty = jnp.take(ty, partners, axis=1).reshape(2 * scan_y, scan_y)
-    tx, tx_late = (
-        jnp.take(jnp.asarray(x_table(scan_x, n_grp, n_mem, parts)), partners, axis=0).reshape(
-            2 * scan_x, 2 * scan_x
-        )
-        for parts in (x_parts, 1)
-    )
-    tk_all = jnp.asarray(pixel_table(WIN, depth))
-    blocks = (jnp.arange(n_q, dtype=jnp.int32)[:, None] * n_grp + partners[None, :]).reshape(-1)
-    tk = jnp.take(tk_all, blocks, axis=0).reshape(2 * pixels, 2 * pixels)
-    tk_all = tk_all.reshape(2 * pixels, 2 * pixels)
-
-    fronts = [(q, h * width, width) for q in range(n_q - 1) for h in range(x_parts)]
+    def chosen(table, index, axis):
+        return jnp.take(jnp.asarray(table), index, axis=axis, mode="clip")
+
+    ty = chosen(y_table(scan_y, n_mem).reshape(2 * scan_y, n_grp, n_y), partners, 1)
+    ty = ty.reshape(2 * scan_y, scan_y)
+
+    fronts = [(q, first, count) for q in range(n_q - 1) for first, count in x_cuts]
     fronts.append((n_q - 1, 0, n_x))
     pieces = exchange(cut(*fronts[0]))
-    early_sent = []
-    ready = None
+    whole_probe = gather_rows(probe_wave, "mem")
+    arrived = []
     for i in range(len(fronts) - 1):
         (ready,) = y_transform(ty, pieces, n_mem, [(0, u_own)])
         following = cut(*fronts[i + 1])
-        ready, following = lax.optimization_barrier((ready, following))
-        early_sent.append(to_owners(ready))
+        ready, following, whole_probe = lax.optimization_barrier((ready, following, whole_probe))
+        arrived.append(to_owners(ready))
         pieces = exchange(following)
-    late_ready = y_transform(ty, pieces, n_mem, late_chunks)
+    late_ready = y_transform(ty, pieces, n_mem, u_chunks)
 
     shift_y = signed_shift(
         mem * u_own + STRIDE_Y * jnp.arange(u_own // STRIDE_Y, dtype=jnp.int32), scan_y, STRIDE_Y
     )
-    shift_x = signed_shift(
-        grp * v_own + STRIDE_X * jnp.arange(v_own // STRIDE_X, dtype=jnp.int32), scan_x, STRIDE_X
+    shift_x = signed_shift(grp * v_own + jnp.arange(v_own, dtype=jnp.int32), scan_x, STRIDE_X)
+    base = whole_probe[:, :WIN, :WIN].reshape(2, WIN * WIN // LANES, LANES)
+    windows = probe_windows(whole_probe, shift_y, shift_x, LANES)
+    chi_table = jnp.asarray(pixel_table(WIN, LANES).reshape(2 * pixels, 2 * pixels))
+    factors = chi_factors(windows, base, chi_table, u_own // STRIDE_Y)
+    tx, tx_late = (
+        chosen(x_table(scan_x, n_grp, n_mem, cuts), partners, 0).reshape(2 * scan_x, 2 * scan_x)
+        for cuts in (x_cuts, [(0, n_x)])
     )
-    product = probe_product(whole_probe, shift_y, shift_x, STRIDE_X, depth)
-    factor_re, factor_im = chi_factors(product, tk_all, u_own // STRIDE_Y, v_own)
-
+    blocks = (jnp.arange(n_q, dtype=jnp.int32)[:, None] * n_grp + partners[None, :]).reshape(-1)
+    tk = chosen(pixel_table(WIN, depth), blocks, 0).reshape(2 * pixels, 2 * pixels)
+
+    late_ready, arrived, factors, tx, tx_late, tk = lax.optimization_barrier(
+        (late_ready, arrived, factors, tx, tx_late, tk)
+    )
+    last = to_owners(late_ready[0])
     early = []
-    waiting = [early_sent[q * x_parts : (q + 1) * x_parts] for q in range(n_q - 1)]
+    for q in range(n_q - 1):
+        early += exchange(x_transform(tx, arrived[q * len(x_cuts) : (q + 1) * len(x_cuts)], n_grp))
     late = []
-    for c in range(len(late_chunks)):
-        sending = late_ready[c]
-        if c == 0:
-            sending, waiting = lax.optimization_barrier((sending, waiting))
-            arrived = to_owners(sending)
-            for parts in waiting:
-                early += exchange(x_transform(tx, parts, n_grp))
-        else:
-            sending, previous = lax.optimization_barrier((sending, arrived))
-            arrived = to_owners(sending)
-            late.append(exchange(x_transform(tx_late, [previous], n_grp)))
-    late.append(exchange(x_transform(tx_late, [arrived], n_grp)))
-
+    ahead = early
     outs = []
-    for (first, count), pieces in zip(late_chunks, late):
-        outs = pixel_transform(tk, early, pieces, factor_re, factor_im, first, count, u_own, outs)
+    for c in range(1, len(u_chunks)):
+        sending, last, _ = lax.optimization_barrier((late_ready[c], last, ahead))
+        following = to_owners(sending)
+        ahead = exchange(x_transform(tx_late, [last], n_grp))
+        late.append(ahead)
+        last = following
+    if len(u_chunks) > 1:
+        first, count = u_chunks[0]
+        outs = pixel_transform(tk, early, late[0], *factors, first, count, u_own, outs)
+        last, _ = lax.optimization_barrier((last, outs[0][0, 0]))
+    late.append(exchange(x_transform(tx_late, [last], n_grp)))
+
+    for c in range(min(1, len(u_chunks) - 1), len(u_chunks)):
+        first, count = u_chunks[c]
+        outs = pixel_transform(tk, early, late[c], *factors, first, count, u_own, outs)
     return tuple(outs)
 
 

time: 678 us -> 500 us (0.74)
  blocking collectives: 112 us -> 0 us
  local copies, waits for them, and re-layouts: 112 us -> 47.6 us
  waiting for transfers between devices: 245 us -> 266 us
  other arithmetic: 25 us -> 8.68 us
  Pallas kernels: 140 us -> 126 us
  starting transfers between devices: 39.2 us -> 46.9 us
    all_gather x1 -> x0, blocking collectives: 112 us -> none  [shards(): whole_probe = lax.all_gather(probe_wave, 'mem', axis=1, tiled=True)]
    gather x12 -> x5, local copies, waits for them, and re-layouts: 52.9 us -> 13.3 us  [the longest x4 12.7 us: chosen(): return jnp.take(jnp.asarray(table), index, axis=axis, mode='clip')]
    ppermute x21 -> x24, waiting for transfers between devices: 150 us -> 184 us  [swap(): return lax.ppermute(array, axis, [(i, i ^ partner) for i in range(size)])]
    pallas_call x1, Pallas kernels: 30 us -> 15.4 us  [chi_factors(): pl.pallas_call(body, grid=(count_y // step,), in_specs=[pl.BlockSpec(wind...]
    all_to_all x5, waiting for transfers between devices: 94.6 us -> 81.4 us  [to_owners(): return lax.all_to_all(array, 'mem', split_axis=0, concat_axis=0, tiled=True)]
    select_n x9 -> x5, other arithmetic: 11.4 us -> 0.16 us  [the longest x3 0.1 us: gather_rows(): jnp.where(ahead, other, block)]
    transpose x1 -> x0, other arithmetic: 11.1 us -> none  [shifted(): return picked.transpose(0, 2, 1, 3).reshape(count_y, count_x, pixels)]
    reshape x2 -> x3, local copies, waits for them, and re-layouts: 14.3 us -> 3.87 us  [the longest x1 2.13 us: probe_windows(): moved = moved.reshape(2, n_rows + stride - 1, count_x, WIN)]
  transfers between devices with their start and end apart: 26 -> 29, of which waited for: 14 -> 15; matrix products, arithmetic and copies ran while one was open for 19% -> 10% of each run, Pallas kernels for 17% -> 21%
where the time goes in v2:
time: 500 us; the launch traced here: 497 us
  waiting for transfers between devices  266 us (53%)
  Pallas kernels  126 us (25%)
  local copies, waits for them, and re-layouts  47.6 us (10%)
  starting transfers between devices  46.9 us (9%)
  other arithmetic  8.68 us (2%)
    ppermute x24, waiting for transfers between devices, swap(): return lax.ppermute(array, axis, [(i, i ^ partner) for i in range(size)])  184 us
    all_to_all x5, waiting for transfers between devices, to_owners(): return lax.all_to_all(array, 'mem', split_axis=0, concat_axis=0, tiled=True)  81.4 us
    pallas_call x3, Pallas kernels, pixel_transform(): pl.pallas_call(body, grid=(count // step,), in_specs=[pl.BlockSpec(table....  55.3 us
    pallas_call x3, Pallas kernels, y_transform(): pl.pallas_call(body, grid=(n_x // step,), in_specs=[pl.BlockSpec(table.sh...  31.1 us
    all_to_all x5, starting transfers between devices, to_owners(): return lax.all_to_all(array, 'mem', split_axis=0, concat_axis=0, tiled=True)  26.5 us
    pallas_call x4, Pallas kernels, x_transform(): pl.pallas_call(body, grid=(n_u // U_TILE,), in_specs=[pl.BlockSpec(table....  24 us
    ppermute x24, starting transfers between devices, swap(): return lax.ppermute(array, axis, [(i, i ^ partner) for i in range(size)])  20.4 us
    pallas_call x1, Pallas kernels, chi_factors(): pl.pallas_call(body, grid=(count_y // step,), in_specs=[pl.BlockSpec(wind...  15.4 us
  transfers between devices with their start and end apart: 29, of which 15 were waited for; matrix products, arithmetic and copies ran while one was open for 10% of the time, Pallas kernels for 21%

profile of v2, /device:TPU:0, one launch (start us, length us, event | category | flops | bytes accessed | tf_op | source)
XLA Modules:
  0.0 497.1 jit_solution(14022197440079050549)
XLA Ops:
  27.2 5.9 %y_transform.3 = bf16[8,10,128,128]{3,2,1,0:T(8,128)(2,1)} custom-call(bf16[1024,512]{1,0:T(8,128)(2,1)} %copy_bitcast_fusion.t_ref, bf16[10,128,128]{2,1,0:T(8,128)(2,1)} %bitcast.57, bf16[10,128,128]{2,1,0:T(8,128)(2,1)} %collective-permute-done.refs_1_, bf16[10,128,128]{2,1,0:T(8,128)(2,1)} %collective-permute-done.1.refs_2_, ...), custom_call_target="tpu_custom_call" | custom-call | flops 1342177280 | bytes 4980736 | tf_op jit(solution)/shard_map/y_transform/pallas_call | solution.py:106
  47.6 9.9 %collective-permute-done.7.refs_2_ = bf16[22,128,128]{2,1,0:T(8,128)(2,1)S(1)} collective-permute-done((bf16[22,128,128]{2,1,0:T(8,128)(2,1)}, bf16[22,128,128]{2,1,0:T(8,128)(2,1)S(1)}, u32[]{:S(2)}, u32[]{:S(2)}) %collective-permute-start.7) | collective-permute-done | bytes 720928 | tf_op jit(solution)/shard_map/ppermute | solution.py:302
  57.5 14.5 %collective-permute-done.8.refs_3_ = bf16[22,128,128]{2,1,0:T(8,128)(2,1)S(1)} collective-permute-done((bf16[22,128,128]{2,1,0:T(8,128)(2,1)S(1)}, bf16[22,128,128]{2,1,0:T(8,128)(2,1)S(1)}, u32[]{:S(2)}, u32[]{:S(2)}) %collective-permute-start.8) | collective-permute-done | bytes 720928 | tf_op jit(solution)/shard_map/ppermute | solution.py:302
  72.9 10.7 %y_transform.4 = bf16[8,22,128,128]{3,2,1,0:T(8,128)(2,1)} custom-call(bf16[1024,512]{1,0:T(8,128)(2,1)} %copy_bitcast_fusion.t_ref, bf16[22,128,128]{2,1,0:T(8,128)(2,1)} %get-tuple-element.53.refs_0_, bf16[22,128,128]{2,1,0:T(8,128)(2,1)} %copy-done.11, bf16[22,128,128]{2,1,0:T(8,128)(2,1)} %copy-done.12, bf16[22,128,128]{2,1,0:T(8,128)(2,1)} %copy-done.13), custom_call_target="tpu_custom_call" | custom-call | flops 2952790016 | bytes 9699328 | tf_op jit(solution)/shard_map/y_transform/pallas_call | solution.py:106
  83.5 12.7 %all-to-all-done = bf16[8,10,128,128]{3,2,1,0:T(8,128)(2,1)S(1)} async-done(((bf16[8,10,128,128]{3,2,1,0:T(8,128)(2,1)}), bf16[8,10,128,128]{3,2,1,0:T(8,128)(2,1)S(1)}, u32[]{:S(2)}, u32[]{:S(2)}) %all-to-all-start) | async-done | bytes 2621472 | tf_op jit(solution)/shard_map/all_to_all | solution.py:353
  106.8 8.1 %gather_fusion.4 = bf16[8,256,2048]{2,1,0:T(8,128)(2,1)} fusion(bf16[8,256,2048]{2,1,0:T(8,128)(2,1)} %constant.92.clone, s32[1024]{0:T(1024)S(1)} %pad_clamp_fusion), kind=kCustom, calls=%fused_computation.4 | custom fusion | bytes 16777248 | tf_op jit(solution)/shard_map/jit(_take)/gather | solution.py:356
  126.6 8.2 %pad_maximum_fusion.w_ref = f32[2,44,64,128]{3,2,1,0:T(8,128)} fusion(f32[2,44,64,32]{3,2,1,0:T(8,128)} %get-tuple-element.117, f32[2,44,64,32]{3,2,1,0:T(8,128)} %get-tuple-element.118, f32[2,44,64,32]{3,2,1,0:T(8,128)} %get-tuple-element.119, f32[2,44,64,32]{3,2,1,0:T(8,128)} %get-tuple-element.116), kind=kLoop, calls=%fused_computation.5 | loop fusion | flops 2162688 | bytes 5767168 | tf_op jit(solution)/shard_map/concatenate | solution.py:297
  134.8 15.4 %chi_factors.1 = (f32[16,64,1024]{2,1,0:T(8,128)}, f32[16,64,1024]{2,1,0:T(8,128)}) custom-call(f32[2,44,64,128]{3,2,1,0:T(8,128)} %pad_maximum_fusion.w_ref, f32[2,8,128]{2,1,0:T(8,128)} %reshape.167.b_ref, bf16[2048,2048]{1,0:T(8,128)(2,1)} %constant.89.clone.t_ref), custom_call_target="tpu_custom_call" | custom-call | flops 8589934592 | bytes 16777216 | tf_op jit(solution)/shard_map/chi_factors/pallas_call | solution.py:200
  150.2 12.8 %collective-permute-done.11.refs_3_ = bf16[32,128,128]{2,1,0:T(8,128)(2,1)} collective-permute-done((bf16[32,128,128]{2,1,0:T(8,128)(2,1)}, bf16[32,128,128]{2,1,0:T(8,128)(2,1)}, u32[]{:S(2)}, u32[]{:S(2)}) %collective-permute-start.11) | collective-permute-done | bytes 1048608 | tf_op jit(solution)/shard_map/ppermute | solution.py:302
  163.1 14.5 %y_transform.5 = (bf16[8,32,64,128]{3,2,1,0:T(8,128)(2,1)}, bf16[8,32,32,128]{3,2,1,0:T(8,128)(2,1)}, bf16[8,32,32,128]{3,2,1,0:T(8,128)(2,1)}) custom-call(bf16[1024,512]{1,0:T(8,128)(2,1)} %copy_bitcast_fusion.t_ref, bf16[32,128,128]{2,1,0:T(8,128)(2,1)} %get-tuple-element.58.refs_0_, bf16[32,128,128]{2,1,0:T(8,128)(2,1)} %collective-permute-done.9.refs_1_, ...), custom_call_target="tpu_custom_call" | custom-call | flops 4294967296 | bytes 13631488 | tf_op jit(solution)/shard_map/y_transform/pallas_call | solution.py:106
  177.6 51.1 %all-to-all-done.1 = bf16[8,22,128,128]{3,2,1,0:T(8,128)(2,1)} async-done(((bf16[8,22,128,128]{3,2,1,0:T(8,128)(2,1)}), bf16[8,22,128,128]{3,2,1,0:T(8,128)(2,1)}, u32[]{:S(2)}, u32[]{:S(2)}) %all-to-all-start.1) | async-done | bytes 5767200 | tf_op jit(solution)/shard_map/all_to_all | solution.py:353
  233.3 9.6 %x_transform.4 = (bf16[64,2,64,128]{3,2,1,0:T(8,128)(2,1)}, bf16[64,2,64,128]{3,2,1,0:T(8,128)(2,1)}, bf16[64,2,64,128]{3,2,1,0:T(8,128)(2,1)}, bf16[64,2,64,128]{3,2,1,0:T(8,128)(2,1)}) custom-call(bf16[512,512]{1,0:T(8,128)(2,1)} %bitcast.61, bf16[80,2,64,128]{3,2,1,0:T(8,128)(2,1)} %bitcast.55, bf16[176,2,64,128]{3,2,1,0:T(8,128)(2,1)} %bitcast.22.refs_1_), custom_call_target="tpu_custom_call" | custom-call | flops 4294967296 | bytes 17301504 | tf_op jit(solution)/shard_map/x_transform/pallas_call | solution.py:152
  247.2 44.4 %collective-permute-done.13.refs_2_ = bf16[64,2,64,128]{3,2,1,0:T(8,128)(2,1)} collective-permute-done((bf16[64,2,64,128]{3,2,1,0:T(8,128)(2,1)}, bf16[64,2,64,128]{3,2,1,0:T(8,128)(2,1)}, u32[]{:S(2)}, u32[]{:S(2)}) %collective-permute-start.13) | collective-permute-done | bytes 2097184 | tf_op jit(solution)/shard_map/ppermute | solution.py:302
  291.7 44.0 %collective-permute-done.14.refs_3_ = bf16[64,2,64,128]{3,2,1,0:T(8,128)(2,1)} collective-permute-done((bf16[64,2,64,128]{3,2,1,0:T(8,128)(2,1)}, bf16[64,2,64,128]{3,2,1,0:T(8,128)(2,1)}, u32[]{:S(2)}, u32[]{:S(2)}) %collective-permute-start.14) | collective-permute-done | bytes 2097184 | tf_op jit(solution)/shard_map/ppermute | solution.py:302
  335.7 5.9 %all-to-all-start.3 = ((bf16[8,32,32,128]{3,2,1,0:T(8,128)(2,1)}), bf16[8,32,32,128]{3,2,1,0:T(8,128)(2,1)}, u32[]{:S(2)}, u32[]{:S(2)}) async-start(bf16[8,32,32,128]{3,2,1,0:T(8,128)(2,1)} %get-tuple-element.84), calls=%async_computation.3 | async-start | bytes 4194304 | tf_op jit(solution)/shard_map/all_to_all | solution.py:353
  341.6 5.7 %x_transform.5 = (bf16[32,2,64,128]{3,2,1,0:T(8,128)(2,1)}, bf16[32,2,64,128]{3,2,1,0:T(8,128)(2,1)}, bf16[32,2,64,128]{3,2,1,0:T(8,128)(2,1)}, bf16[32,2,64,128]{3,2,1,0:T(8,128)(2,1)}) custom-call(bf16[512,512]{1,0:T(8,128)(2,1)} %bitcast.58, bf16[256,2,32,128]{3,2,1,0:T(8,128)(2,1)} %bitcast.23.refs_0_), custom_call_target="tpu_custom_call" | custom-call | flops 2147483648 | bytes 8912896 | tf_op jit(solution)/shard_map/x_transform/pallas_call | solution.py:152
  350.3 23.4 %collective-permute-done.16.refs_6_ = bf16[32,2,64,128]{3,2,1,0:T(8,128)(2,1)} collective-permute-done((bf16[32,2,64,128]{3,2,1,0:T(8,128)(2,1)}, bf16[32,2,64,128]{3,2,1,0:T(8,128)(2,1)}, u32[]{:S(2)}, u32[]{:S(2)}) %collective-permute-start.16) | collective-permute-done | bytes 1048608 | tf_op jit(solution)/shard_map/ppermute | solution.py:302
  373.6 21.5 %collective-permute-done.17.refs_7_ = bf16[32,2,64,128]{3,2,1,0:T(8,128)(2,1)} collective-permute-done((bf16[32,2,64,128]{3,2,1,0:T(8,128)(2,1)}, bf16[32,2,64,128]{3,2,1,0:T(8,128)(2,1)}, u32[]{:S(2)}, u32[]{:S(2)}) %collective-permute-start.17) | collective-permute-done | bytes 1048608 | tf_op jit(solution)/shard_map/ppermute | solution.py:302
  395.2 6.0 %all-to-all-start.4 = ((bf16[8,32,32,128]{3,2,1,0:T(8,128)(2,1)}), bf16[8,32,32,128]{3,2,1,0:T(8,128)(2,1)S(1)}, u32[]{:S(2)}, u32[]{:S(2)}) async-start(bf16[8,32,32,128]{3,2,1,0:T(8,128)(2,1)} %get-tuple-element.90), calls=%async_computation.4 | async-start | bytes 4194304 | tf_op jit(solution)/shard_map/all_to_all | solution.py:353
  407.4 24.8 %pixel_transform.3 = (f32[64,64,1024]{2,1,0:T(8,128)}, f32[64,64,1024]{2,1,0:T(8,128)}) custom-call(bf16[2048,2048]{1,0:T(8,128)(2,1)} %bitcast.52, f32[16,64,1024]{2,1,0:T(8,128)} %get-tuple-element.71.cr_ref, f32[16,64,1024]{2,1,0:T(8,128)} %get-tuple-element.72.ci_ref, bf16[64,2,64,128]{3,2,1,0:T(8,128)(2,1)} %get-tuple-element.76.refs_0_, ...), custom_call_target="tpu_custom_call" | custom-call | flops 17179869184 | bytes 33554432 | tf_op jit(solution)/shard_map/pixel_transform/pallas_call | solution.py:261
  432.3 17.6 %all-to-all-done.4 = bf16[8,32,32,128]{3,2,1,0:T(8,128)(2,1)S(1)} async-done(((bf16[8,32,32,128]{3,2,1,0:T(8,128)(2,1)}), bf16[8,32,32,128]{3,2,1,0:T(8,128)(2,1)S(1)}, u32[]{:S(2)}, u32[]{:S(2)}) %all-to-all-start.4) | async-done | bytes 2097184 | tf_op jit(solution)/shard_map/all_to_all | solution.py:353
  458.2 15.2 %pixel_transform.4 = (f32[64,64,1024]{2,1,0:T(8,128)}, f32[64,64,1024]{2,1,0:T(8,128)}) custom-call(bf16[2048,2048]{1,0:T(8,128)(2,1)} %bitcast.53, f32[16,64,1024]{2,1,0:T(8,128)} %get-tuple-element.71.cr_ref, f32[16,64,1024]{2,1,0:T(8,128)} %get-tuple-element.72.ci_ref, ...), custom_call_target="tpu_custom_call", output_to_operand_aliasing={{0}: (11, {}), {1}: (12, {})} | custom-call | flops 8589934592 | bytes 20971520 | tf_op jit(solution)/shard_map/pixel_transform/pallas_call | solution.py:261
  473.5 7.4 %collective-permute-done.20.refs_7_ = bf16[16,2,64,128]{3,2,1,0:T(8,128)(2,1)S(1)} collective-permute-done((bf16[16,2,64,128]{3,2,1,0:T(8,128)(2,1)}, bf16[16,2,64,128]{3,2,1,0:T(8,128)(2,1)S(1)}, u32[]{:S(2)}, u32[]{:S(2)}) %collective-permute-start.20) | collective-permute-done | bytes 524320 | tf_op jit(solution)/shard_map/ppermute | solution.py:302
  481.7 15.2 %pixel_transform.5 = (f32[64,64,1024]{2,1,0:T(8,128)}, f32[64,64,1024]{2,1,0:T(8,128)}) custom-call(bf16[2048,2048]{1,0:T(8,128)(2,1)} %bitcast.54, f32[16,64,1024]{2,1,0:T(8,128)} %get-tuple-element.71.cr_ref, f32[16,64,1024]{2,1,0:T(8,128)} %get-tuple-element.72.ci_ref, ...), custom_call_target="tpu_custom_call", output_to_operand_aliasing={{0}: (11, {}), {1}: (12, {})} | custom-call | flops 8589934592 | bytes 20971520 | tf_op jit(solution)/shard_map/pixel_transform/pallas_call | solution.py:261
  (118 shorter events, 91.4 us)
Async XLA Ops:
  1.4 16.0 %collective-permute-start.3 = (f32[2,16,128]{2,0,1:T(2,128)S(1)}, f32[2,16,128]{2,0,1:T(2,128)S(1)}, u32[]{:S(2)}, u32[]{:S(2)}) collective-permute-start(f32[2,16,128]{2,0,1:T(2,128)S(1)} %copy.34), channel_id=1, source_target_pairs={{0,1},{1,0},{2,3},{3,2},{4,5},{5,4},{6,7},{7,6},{8,9},{9,8},{10,11... | collective-permute-start | bytes 49160 | tf_op jit(solution)/shard_map/ppermute | solution.py:302
  7.2 20.0 %collective-permute-start = (bf16[10,128,128]{2,1,0:T(8,128)(2,1)}, bf16[10,128,128]{2,1,0:T(8,128)(2,1)}, u32[]{:S(2)}, u32[]{:S(2)}) collective-permute-start(bf16[10,128,128]{2,1,0:T(8,128)(2,1)} %bitcast.49), channel_id=1, source_target_pairs={{0,8},{8,0},{16,24},{24,16},{1,9},{9,1},{17,25},{25,17},{2,10},{10... | collective-permute-start | bytes 983048 | tf_op jit(solution)/shard_map/ppermute | solution.py:302
  8.0 19.2 %collective-permute-start.1 = (bf16[10,128,128]{2,1,0:T(8,128)(2,1)}, bf16[10,128,128]{2,1,0:T(8,128)(2,1)}, u32[]{:S(2)}, u32[]{:S(2)}) collective-permute-start(bf16[10,128,128]{2,1,0:T(8,128)(2,1)} %bitcast.48), channel_id=1, source_target_pairs={{0,16},{8,24},{16,0},{24,8},{1,17},{9,25},{17,1},{25,9},{2,18},{10... | collective-permute-start | bytes 983048 | tf_op jit(solution)/shard_map/ppermute | solution.py:302
  10.3 16.9 %collective-permute-start.2 = (bf16[10,128,128]{2,1,0:T(8,128)(2,1)}, bf16[10,128,128]{2,1,0:T(8,128)(2,1)}, u32[]{:S(2)}, u32[]{:S(2)}) collective-permute-start(bf16[10,128,128]{2,1,0:T(8,128)(2,1)} %bitcast.47), channel_id=1, source_target_pairs={{0,24},{8,16},{16,8},{24,0},{1,25},{9,17},{17,9},{25,1},{2,26},{10... | collective-permute-start | bytes 983048 | tf_op jit(solution)/shard_map/ppermute | solution.py:302
  33.0 63.2 %all-to-all-start = ((bf16[8,10,128,128]{3,2,1,0:T(8,128)(2,1)}), bf16[8,10,128,128]{3,2,1,0:T(8,128)(2,1)S(1)}, u32[]{:S(2)}, u32[]{:S(2)}) async-start(bf16[8,10,128,128]{3,2,1,0:T(8,128)(2,1)} %y_transform.3), calls=%async_computation | async-start | bytes 5242880 | tf_op jit(solution)/shard_map/all_to_all | solution.py:353
  38.2 19.2 %collective-permute-start.7 = (bf16[22,128,128]{2,1,0:T(8,128)(2,1)}, bf16[22,128,128]{2,1,0:T(8,128)(2,1)S(1)}, u32[]{:S(2)}, u32[]{:S(2)}) collective-permute-start(bf16[22,128,128]{2,1,0:T(8,128)(2,1)} %get-tuple-element.55), channel_id=1, source_target_pairs={{0,16},{8,24},{16,0},{24,8},{1,17},{9,25},{17,1},{25,9},{2,18},{10... | collective-permute-start | bytes 2162696 | tf_op jit(solution)/shard_map/ppermute | solution.py:302
  39.8 32.2 %collective-permute-start.8 = (bf16[22,128,128]{2,1,0:T(8,128)(2,1)S(1)}, bf16[22,128,128]{2,1,0:T(8,128)(2,1)S(1)}, u32[]{:S(2)}, u32[]{:S(2)}) collective-permute-start(bf16[22,128,128]{2,1,0:T(8,128)(2,1)S(1)} %get-tuple-element.56), channel_id=1, source_target_pairs={{0,24},{8,16},{16,8},{24,0},{1,25},{9,17},{17,9},{25,1},{2,26},{10... | collective-permute-start | bytes 2162696 | tf_op jit(solution)/shard_map/ppermute | solution.py:302
  97.8 130.9 %all-to-all-start.1 = ((bf16[8,22,128,128]{3,2,1,0:T(8,128)(2,1)}), bf16[8,22,128,128]{3,2,1,0:T(8,128)(2,1)}, u32[]{:S(2)}, u32[]{:S(2)}) async-start(bf16[8,22,128,128]{3,2,1,0:T(8,128)(2,1)} %y_transform.4), calls=%async_computation.1 | async-start | bytes 11534336 | tf_op jit(solution)/shard_map/all_to_all | solution.py:353
  115.1 35.2 %collective-permute-start.9 = (bf16[32,128,128]{2,1,0:T(8,128)(2,1)}, bf16[32,128,128]{2,1,0:T(8,128)(2,1)}, u32[]{:S(2)}, u32[]{:S(2)}) collective-permute-start(bf16[32,128,128]{2,1,0:T(8,128)(2,1)} %get-tuple-element.59), channel_id=1, source_target_pairs={{0,8},{8,0},{16,24},{24,16},{1,9},{9,1},{17,25},{25,17},{2,10},{10... | collective-permute-start | bytes 3145736 | tf_op jit(solution)/shard_map/ppermute | solution.py:302
  115.2 35.1 %collective-permute-start.10 = (bf16[32,128,128]{2,1,0:T(8,128)(2,1)}, bf16[32,128,128]{2,1,0:T(8,128)(2,1)}, u32[]{:S(2)}, u32[]{:S(2)}) collective-permute-start(bf16[32,128,128]{2,1,0:T(8,128)(2,1)} %get-tuple-element.60), channel_id=1, source_target_pairs={{0,16},{8,24},{16,0},{24,8},{1,17},{9,25},{17,1},{25,9},{2,18},{10... | collective-permute-start | bytes 3145736 | tf_op jit(solution)/shard_map/ppermute | solution.py:302
  116.7 46.3 %collective-permute-start.11 = (bf16[32,128,128]{2,1,0:T(8,128)(2,1)}, bf16[32,128,128]{2,1,0:T(8,128)(2,1)}, u32[]{:S(2)}, u32[]{:S(2)}) collective-permute-start(bf16[32,128,128]{2,1,0:T(8,128)(2,1)} %get-tuple-element.61), channel_id=1, source_target_pairs={{0,24},{8,16},{16,8},{24,0},{1,25},{9,17},{17,9},{25,1},{2,26},{10... | collective-permute-start | bytes 3145736 | tf_op jit(solution)/shard_map/ppermute | solution.py:302
  228.7 107.0 %all-to-all-start.2 = ((bf16[8,32,64,128]{3,2,1,0:T(8,128)(2,1)}), bf16[8,32,64,128]{3,2,1,0:T(8,128)(2,1)}, u32[]{:S(2)}, u32[]{:S(2)}) async-start(bf16[8,32,64,128]{3,2,1,0:T(8,128)(2,1)} %get-tuple-element.83), calls=%async_computation.2 | async-start | bytes 8388608 | tf_op jit(solution)/shard_map/all_to_all | solution.py:353
  242.8 48.8 %collective-permute-start.13 = (bf16[64,2,64,128]{3,2,1,0:T(8,128)(2,1)}, bf16[64,2,64,128]{3,2,1,0:T(8,128)(2,1)}, u32[]{:S(2)}, u32[]{:S(2)}) collective-permute-start(bf16[64,2,64,128]{3,2,1,0:T(8,128)(2,1)} %get-tuple-element.78), channel_id=1, source_target_pairs={{0,16},{8,24},{16,0},{24,8},{1,17},{9,25},{17,1},{25,9},{2,18},{10... | collective-permute-start | bytes 6291464 | tf_op jit(solution)/shard_map/ppermute | solution.py:302
  244.4 91.3 %collective-permute-start.14 = (bf16[64,2,64,128]{3,2,1,0:T(8,128)(2,1)}, bf16[64,2,64,128]{3,2,1,0:T(8,128)(2,1)}, u32[]{:S(2)}, u32[]{:S(2)}) collective-permute-start(bf16[64,2,64,128]{3,2,1,0:T(8,128)(2,1)} %get-tuple-element.79), channel_id=1, source_target_pairs={{0,24},{8,16},{16,8},{24,0},{1,25},{9,17},{17,9},{25,1},{2,26},{10... | collective-permute-start | bytes 6291464 | tf_op jit(solution)/shard_map/ppermute | solution.py:302
  335.7 59.5 %all-to-all-start.3 = ((bf16[8,32,32,128]{3,2,1,0:T(8,128)(2,1)}), bf16[8,32,32,128]{3,2,1,0:T(8,128)(2,1)}, u32[]{:S(2)}, u32[]{:S(2)}) async-start(bf16[8,32,32,128]{3,2,1,0:T(8,128)(2,1)} %get-tuple-element.84), calls=%async_computation.3 | async-start | bytes 4194304 | tf_op jit(solution)/shard_map/all_to_all | solution.py:353
  347.3 26.3 %collective-permute-start.16 = (bf16[32,2,64,128]{3,2,1,0:T(8,128)(2,1)}, bf16[32,2,64,128]{3,2,1,0:T(8,128)(2,1)}, u32[]{:S(2)}, u32[]{:S(2)}) collective-permute-start(bf16[32,2,64,128]{3,2,1,0:T(8,128)(2,1)} %get-tuple-element.88), channel_id=1, source_target_pairs={{0,16},{8,24},{16,0},{24,8},{1,17},{9,25},{17,1},{25,9},{2,18},{10... | collective-permute-start | bytes 3145736 | tf_op jit(solution)/shard_map/ppermute | solution.py:302
  348.8 46.3 %collective-permute-start.17 = (bf16[32,2,64,128]{3,2,1,0:T(8,128)(2,1)}, bf16[32,2,64,128]{3,2,1,0:T(8,128)(2,1)}, u32[]{:S(2)}, u32[]{:S(2)}) collective-permute-start(bf16[32,2,64,128]{3,2,1,0:T(8,128)(2,1)} %get-tuple-element.89), channel_id=1, source_target_pairs={{0,24},{8,16},{16,8},{24,0},{1,25},{9,17},{17,9},{25,1},{2,26},{10... | collective-permute-start | bytes 3145736 | tf_op jit(solution)/shard_map/ppermute | solution.py:302
  395.2 54.7 %all-to-all-start.4 = ((bf16[8,32,32,128]{3,2,1,0:T(8,128)(2,1)}), bf16[8,32,32,128]{3,2,1,0:T(8,128)(2,1)S(1)}, u32[]{:S(2)}, u32[]{:S(2)}) async-start(bf16[8,32,32,128]{3,2,1,0:T(8,128)(2,1)} %get-tuple-element.90), calls=%async_computation.4 | async-start | bytes 4194304 | tf_op jit(solution)/shard_map/all_to_all | solution.py:353
  405.5 51.5 %collective-permute-start.21 = (bf16[16,2,64,128]{3,2,1,0:T(8,128)(2,1)}, bf16[16,2,64,128]{3,2,1,0:T(8,128)(2,1)S(1)}, u32[]{:S(2)}, u32[]{:S(2)}) collective-permute-start(bf16[16,2,64,128]{3,2,1,0:T(8,128)(2,1)} %get-tuple-element.97), channel_id=1, source_target_pairs={{0,8},{8,0},{16,24},{24,16},{1,9},{9,1},{17,25},{25,17},{2,10},{10... | collective-permute-start | bytes 1572872 | tf_op jit(solution)/shard_map/ppermute | solution.py:302
  405.6 51.8 %collective-permute-start.22 = (bf16[16,2,64,128]{3,2,1,0:T(8,128)(2,1)}, bf16[16,2,64,128]{3,2,1,0:T(8,128)(2,1)S(1)}, u32[]{:S(2)}, u32[]{:S(2)}) collective-permute-start(bf16[16,2,64,128]{3,2,1,0:T(8,128)(2,1)} %get-tuple-element.98), channel_id=1, source_target_pairs={{0,16},{8,24},{16,0},{24,8},{1,17},{9,25},{17,1},{25,9},{2,18},{10... | collective-permute-start | bytes 1572872 | tf_op jit(solution)/shard_map/ppermute | solution.py:302
  407.1 50.3 %collective-permute-start.23 = (bf16[16,2,64,128]{3,2,1,0:T(8,128)(2,1)}, bf16[16,2,64,128]{3,2,1,0:T(8,128)(2,1)}, u32[]{:S(2)}, u32[]{:S(2)}) collective-permute-start(bf16[16,2,64,128]{3,2,1,0:T(8,128)(2,1)} %get-tuple-element.99), channel_id=1, source_target_pairs={{0,24},{8,16},{16,8},{24,0},{1,25},{9,17},{17,9},{25,1},{2,26},{10... | collective-permute-start | bytes 1572872 | tf_op jit(solution)/shard_map/ppermute | solution.py:302
  455.5 17.9 %collective-permute-start.18 = (bf16[16,2,64,128]{3,2,1,0:T(8,128)(2,1)}, bf16[16,2,64,128]{3,2,1,0:T(8,128)(2,1)S(1)}, u32[]{:S(2)}, u32[]{:S(2)}) collective-permute-start(bf16[16,2,64,128]{3,2,1,0:T(8,128)(2,1)} %get-tuple-element.92), channel_id=1, source_target_pairs={{0,8},{8,0},{16,24},{24,16},{1,9},{9,1},{17,25},{25,17},{2,10},{10... | collective-permute-start | bytes 1572872 | tf_op jit(solution)/shard_map/ppermute | solution.py:302
  455.5 18.0 %collective-permute-start.19 = (bf16[16,2,64,128]{3,2,1,0:T(8,128)(2,1)}, bf16[16,2,64,128]{3,2,1,0:T(8,128)(2,1)S(1)}, u32[]{:S(2)}, u32[]{:S(2)}) collective-permute-start(bf16[16,2,64,128]{3,2,1,0:T(8,128)(2,1)} %get-tuple-element.93), channel_id=1, source_target_pairs={{0,16},{8,24},{16,0},{24,8},{1,17},{9,25},{17,1},{25,9},{2,18},{10... | collective-permute-start | bytes 1572872 | tf_op jit(solution)/shard_map/ppermute | solution.py:302
  457.0 23.9 %collective-permute-start.20 = (bf16[16,2,64,128]{3,2,1,0:T(8,128)(2,1)}, bf16[16,2,64,128]{3,2,1,0:T(8,128)(2,1)S(1)}, u32[]{:S(2)}, u32[]{:S(2)}) collective-permute-start(bf16[16,2,64,128]{3,2,1,0:T(8,128)(2,1)} %get-tuple-element.94), channel_id=1, source_target_pairs={{0,24},{8,16},{16,8},{24,0},{1,25},{9,17},{17,9},{25,1},{2,26},{10... | collective-permute-start | bytes 1572872 | tf_op jit(solution)/shard_map/ppermute | solution.py:302
  (19 other events, 215.3 us)

commit v3 on v2

--- a/solution.py
+++ b/solution.py
@@ -13,7 +13,7 @@
 STRIDE_Y = 4
 STRIDE_X = 2
 LANES = 128
-U_TILE = 16
+U_TILE = 8
 VMEM_BYTES = 56 * 1024 * 1024
 
 wiener_floor = 0.5
@@ -41,10 +41,9 @@
     return rounded(np.cos(angles) * factor), rounded(np.sin(angles) * factor)
 
 
-def y_table(length, owners):
+def y_table(length):
     t_re, t_im = scan_table(length)
-    both = np.stack([t_re.T, t_im.T], axis=0).reshape(2, owners, length // owners, length)
-    return both.transpose(1, 0, 2, 3).reshape(2 * length, length)
+    return np.stack([t_re.T, t_im.T], axis=1).reshape(2 * length, length)
 
 
 def x_table(length, owners, senders, cuts):
@@ -76,7 +75,6 @@
 def y_transform(table, pieces, owners, u_chunks):
     n_x, n_y, depth = pieces[0].shape
     per_owner = table.shape[0] // owners
-    u_own = per_owner // 2
     step = 2
 
     def body(t_ref, *refs):
@@ -94,9 +92,8 @@
             res = parts[i].astype(jnp.bfloat16)
             for o_ref, (first, count) in zip(outs, u_chunks):
                 for d in range(owners):
-                    for r in range(2):
-                        row = d * per_owner + r * u_own + first
-                        o_ref[d, i, r * count : (r + 1) * count, :] = res[row : row + count]
+                    row = d * per_owner + 2 * first
+                    o_ref[d, i] = res[row : row + 2 * count]
 
     out_shape = [
         jax.ShapeDtypeStruct((owners, n_x, 2 * count, depth), jnp.bfloat16) for _, count in u_chunks
@@ -119,19 +116,20 @@
     )(table, *pieces)
 
 
-def x_transform(table, parts, owners):
-    rows, depth = parts[0].shape[2:]
-    n_u = rows // 2
+def x_transform(table, parts, first, n_u, owners):
+    starts = [(first - start) // U_TILE for start, _ in parts]
+    parts = [p for _, p in parts]
+    depth = parts[0].shape[3]
     v_own = table.shape[0] // owners // 2
-    views = [p.reshape(p.shape[0] * p.shape[1], 2, n_u, depth) for p in parts]
+    views = [p.reshape(p.shape[0] * p.shape[1], p.shape[2], depth) for p in parts]
     pair = 2
 
     def body(t_ref, *refs):
         ins, outs = refs[: len(views)], refs[len(views) :]
-        turned = [[jnp.swapaxes(p[:, r], 0, 1) for p in ins] for r in range(2)]
+        turned = [jnp.swapaxes(p[...], 0, 1) for p in ins]
         for u in range(0, U_TILE, pair):
             cols = [
-                jnp.concatenate([turned[r][h][u + i] for r in range(2) for h in range(len(ins))], axis=0)
+                jnp.concatenate([t[2 * (u + i) + r] for r in range(2) for t in turned], axis=0)
                 for i in range(pair)
             ]
             if depth == LANES:
@@ -148,12 +146,16 @@
                         outs[d][u + i, r] = res[row : row + v_own]
 
     flops = 2 * table.size * n_u * depth
-    moved = 4 * sum(p.size for p in parts) + 2 * table.size
+    moved = 4 * n_u * depth * table.shape[1] + 2 * table.size
+
+    def placed(view, start):
+        return pl.BlockSpec((view.shape[0], 2 * U_TILE, depth), lambda s: (0, start + s, 0))
+
     return pl.pallas_call(
         body,
         grid=(n_u // U_TILE,),
         in_specs=[pl.BlockSpec(table.shape, lambda s: (0, 0))]
-        + [pl.BlockSpec((v.shape[0], 2, U_TILE, depth), lambda s: (0, 0, s, 0)) for v in views],
+        + [placed(v, start) for v, start in zip(views, starts)],
         out_specs=[
             pl.BlockSpec((U_TILE, 2, v_own, depth), lambda s: (s, 0, 0, 0)) for _ in range(owners)
         ],
@@ -216,18 +218,20 @@
     )(windows, base, table)
 
 
-def pixel_transform(table, early, late, factor_re, factor_im, first, count, total_u, previous):
-    inner = table.shape[0]
+def pixel_transform(table, table_rows, pieces, factors, partial, first, count, total_u, previous):
     pixels = table.shape[1] // 2
-    v_own, depth = late[0].shape[2:]
+    arrays = [p for _, p in pieces]
+    v_own, depth = arrays[0].shape[2:]
+    inner = 2 * depth * len(arrays)
     step = STRIDE_Y
     rows = step * v_own
     lanes = 256
     base = first // step
-    n_early, n_late = len(early), len(late)
-
-    def body(t_ref, cr_ref, ci_ref, *refs):
-        ins = refs[: n_early + n_late]
+    block = table_rows // inner
+
+    def body(t_ref, *refs):
+        ins, refs = refs[: len(arrays)], refs[len(arrays) :]
+        sums, refs = refs[: len(partial)], refs[len(partial) :]
         re_ref, im_ref = refs[-2:]
         cuts = [p[:, r].reshape(rows, depth) for p in ins for r in range(2)]
         if depth == LANES:
@@ -245,15 +249,22 @@
             at = slice(n * lanes, (n + 1) * lanes)
             s_re = total(at)
             s_im = total(slice(pixels + n * lanes, pixels + (n + 1) * lanes))
-            c_re = cr_ref[:, :, at]
-            c_im = ci_ref[:, :, at]
-            re_ref[:, :, at] = s_re * c_re + s_im * c_im
-            im_ref[:, :, at] = s_im * c_re - s_re * c_im
-
-    factor_spec = pl.BlockSpec((1, v_own, pixels), lambda s: (base + s, 0, 0))
-    out_spec = pl.BlockSpec((step, v_own, pixels), lambda s: (base + s, 0, 0))
-    shape = jax.ShapeDtypeStruct((total_u, v_own, pixels), jnp.float32)
-    operands = [table, factor_re, factor_im, *early, *late]
+            if sums:
+                s_re = s_re + sums[0][:, :, at]
+                s_im = s_im + sums[1][:, :, at]
+            if factors:
+                c_re = refs[0][:, :, at]
+                c_im = refs[1][:, :, at]
+                s_re, s_im = s_re * c_re + s_im * c_im, s_im * c_re - s_re * c_im
+            re_ref[:, :, at] = s_re
+            im_ref[:, :, at] = s_im
+
+    def placed(start, array):
+        return pl.BlockSpec((step, 2, v_own, depth), lambda s: ((first - start) // step + s, 0, 0, 0))
+
+    here = 0 if not factors else base
+    shape = jax.ShapeDtypeStruct((total_u if factors else count, v_own, pixels), jnp.float32)
+    operands = [table, *arrays, *partial, *factors]
     aliases = {}
     for i, array in enumerate(previous):
         aliases[len(operands)] = i
@@ -261,17 +272,18 @@
     return pl.pallas_call(
         body,
         grid=(count // step,),
-        in_specs=[pl.BlockSpec(table.shape, lambda s: (0, 0)), factor_spec, factor_spec]
-        + [pl.BlockSpec((step, 2, v_own, depth), lambda s: (base + s, 0, 0, 0)) for _ in early]
-        + [pl.BlockSpec((step, 2, v_own, depth), lambda s: (s, 0, 0, 0)) for _ in late]
+        in_specs=[pl.BlockSpec((inner, 2 * pixels), lambda s: (block, 0))]
+        + [placed(start, p) for start, p in pieces]
+        + [pl.BlockSpec((step, v_own, pixels), lambda s: (s, 0, 0)) for _ in partial]
+        + [pl.BlockSpec((1, v_own, pixels), lambda s: (base + s, 0, 0)) for _ in factors]
         + [pl.BlockSpec(memory_space=pl.ANY) for _ in previous],
-        out_specs=[out_spec] * 2,
+        out_specs=[pl.BlockSpec((step, v_own, pixels), lambda s: (here + s, 0, 0))] * 2,
         out_shape=[shape] * 2,
         input_output_aliases=aliases,
         compiler_params=params(),
         cost_estimate=pl.CostEstimate(
-            flops=2 * count * v_own * table.size,
-            bytes_accessed=2 * table.size + 12 * count * v_own * pixels,
+            flops=4 * count * v_own * inner * pixels,
+            bytes_accessed=4 * inner * pixels + 12 * count * v_own * pixels,
             transcendentals=0,
         ),
         name="pixel_transform",
@@ -330,24 +342,25 @@
     else:
         x_cuts = [(0, n_x)]
 
-    if u_own >= 4 * U_TILE:
-        sizes = [u_own // 2, u_own // 4, u_own // 4]
+    if u_own >= 8 * U_TILE:
+        sizes = [u_own * 3 // 8, u_own // 4, u_own // 4, u_own // 8]
     else:
-        sizes = [U_TILE] * (u_own // U_TILE)
+        sizes = [u_own // 2, u_own // 2]
     u_chunks = []
     for size in sizes:
         u_chunks.append((sum(c for _, c in u_chunks), size))
 
     def cut(q, first, count):
         made = []
-        for j in range(n_grp):
+        for j in range(n_grp - 1, -1, -1):
             at = (q * n_grp + (grp ^ j)) * depth
             piece = lax.dynamic_slice(frames, (0, first, at), (n_y, count, depth))
             made.append(piece.transpose(1, 0, 2))
-        return made
+        return made[::-1]
 
     def exchange(pieces):
-        return [pieces[0]] + [swap(pieces[j], j, "grp") for j in range(1, n_grp)]
+        far = [swap(pieces[j], j, "grp") for j in range(n_grp - 1, 0, -1)]
+        return [pieces[0]] + far[::-1]
 
     def to_owners(array):
         return lax.all_to_all(array, "mem", split_axis=0, concat_axis=0, tiled=True)
@@ -355,21 +368,24 @@
     def chosen(table, index, axis):
         return jnp.take(jnp.asarray(table), index, axis=axis, mode="clip")
 
-    ty = chosen(y_table(scan_y, n_mem).reshape(2 * scan_y, n_grp, n_y), partners, 1)
+    ty = chosen(y_table(scan_y).reshape(2 * scan_y, n_grp, n_y), partners, 1)
     ty = ty.reshape(2 * scan_y, scan_y)
 
     fronts = [(q, first, count) for q in range(n_q - 1) for first, count in x_cuts]
     fronts.append((n_q - 1, 0, n_x))
+    halves = [u_chunks[0], (u_chunks[0][1], u_own - u_chunks[0][1])]
     pieces = exchange(cut(*fronts[0]))
     whole_probe = gather_rows(probe_wave, "mem")
     arrived = []
     for i in range(len(fronts) - 1):
-        (ready,) = y_transform(ty, pieces, n_mem, [(0, u_own)])
+        chunks = halves if i == len(fronts) - 2 else [(0, u_own)]
+        ready = y_transform(ty, pieces, n_mem, chunks)
         following = cut(*fronts[i + 1])
-        ready, following, whole_probe = lax.optimization_barrier((ready, following, whole_probe))
-        arrived.append(to_owners(ready))
+        ready, following, whole_probe, arrived = lax.optimization_barrier(
+            (ready, following, whole_probe, arrived)
+        )
+        arrived.append(to_owners(ready[0]))
         pieces = exchange(following)
-    late_ready = y_transform(ty, pieces, n_mem, u_chunks)
 
     shift_y = signed_shift(
         mem * u_own + STRIDE_Y * jnp.arange(u_own // STRIDE_Y, dtype=jnp.int32), scan_y, STRIDE_Y
@@ -386,31 +402,55 @@
     blocks = (jnp.arange(n_q, dtype=jnp.int32)[:, None] * n_grp + partners[None, :]).reshape(-1)
     tk = chosen(pixel_table(WIN, depth), blocks, 0).reshape(2 * pixels, 2 * pixels)
 
-    late_ready, arrived, factors, tx, tx_late, tk = lax.optimization_barrier(
-        (late_ready, arrived, factors, tx, tx_late, tk)
-    )
-    last = to_owners(late_ready[0])
     early = []
-    for q in range(n_q - 1):
-        early += exchange(x_transform(tx, arrived[q * len(x_cuts) : (q + 1) * len(x_cuts)], n_grp))
     late = []
-    ahead = early
+    if fronts[:-1]:
+        arrived, pending, factors, tx, pieces = lax.optimization_barrier((arrived, ready[1], factors, tx, pieces))
+        last = to_owners(pending)
+        late_ready = y_transform(ty, pieces, n_mem, u_chunks)
+        sources = [(0, a) for a in arrived]
+        early.append(exchange(x_transform(tx, sources, *halves[0], n_grp)))
+        late_ready, last, tk, tx_late, early[0] = lax.optimization_barrier(
+            (late_ready, last, tk, tx_late, early[0])
+        )
+        sources = sources[:-1] + [(halves[1][0], last)]
+        last = to_owners(late_ready[0])
+        early.append(exchange(x_transform(tx, sources, *halves[1], n_grp)))
+    else:
+        late_ready = y_transform(ty, pieces, n_mem, u_chunks)
+        last = to_owners(late_ready[0])
+
+    def early_of(first):
+        return [(start, p) for (start, size), part in zip(halves, early) if start <= first < start + size for p in part]
+
+    inner = 2 * pixels // n_q
+    def finish(c, outs):
+        first, count = u_chunks[c]
+        own = [(first, p) for p in late[c]]
+        if c == len(u_chunks) - 1 and partial:
+            return pixel_transform(tk, inner, own, factors, partial, first, count, u_own, outs)
+        return pixel_transform(tk, 0, early_of(first) + own, factors, [], first, count, u_own, outs)
+
     outs = []
+    partial = []
     for c in range(1, len(u_chunks)):
-        sending, last, _ = lax.optimization_barrier((late_ready[c], last, ahead))
+        sending, last, early, late, partial, outs = lax.optimization_barrier(
+            (late_ready[c], last, early, late, partial, outs)
+        )
         following = to_owners(sending)
-        ahead = exchange(x_transform(tx_late, [last], n_grp))
-        late.append(ahead)
+        first, count = u_chunks[c - 1]
+        late.append(exchange(x_transform(tx_late, [(first, last)], first, count, n_grp)))
         last = following
-    if len(u_chunks) > 1:
-        first, count = u_chunks[0]
-        outs = pixel_transform(tk, early, late[0], *factors, first, count, u_own, outs)
-        last, _ = lax.optimization_barrier((last, outs[0][0, 0]))
-    late.append(exchange(x_transform(tx_late, [last], n_grp)))
-
-    for c in range(min(1, len(u_chunks) - 1), len(u_chunks)):
-        first, count = u_chunks[c]
-        outs = pixel_transform(tk, early, late[c], *factors, first, count, u_own, outs)
+        if c == 1 and early:
+            first, count = u_chunks[-1]
+            partial = pixel_transform(tk, 0, early_of(first), [], [], first, count, u_own, [])
+        if c >= 2:
+            outs = finish(c - 2, outs)
+    last, partial, outs = lax.optimization_barrier((last, partial, outs))
+    first, count = u_chunks[-1]
+    late.append(exchange(x_transform(tx_late, [(first, last)], first, count, n_grp)))
+    for c in range(max(0, len(u_chunks) - 2), len(u_chunks)):
+        outs = finish(c, outs)
     return tuple(outs)
 
 

time: 500 us -> 479 us (0.958)
  waiting for transfers between devices: 266 us -> 222 us
  Pallas kernels: 126 us -> 140 us
  starting transfers between devices: 46.9 us -> 56 us
    ppermute x24 -> x30, waiting for transfers between devices: 184 us -> 138 us  [swap(): return lax.ppermute(array, axis, [(i, i ^ partner) for i in range(size)])]
    pallas_call x3 -> x5, Pallas kernels: 55.3 us -> 64.6 us  [pixel_transform(): pl.pallas_call(body, grid=(count // step,), in_specs=[pl.BlockSpec((inner...]
    pallas_call x4 -> x6, Pallas kernels: 24 us -> 29.4 us  [x_transform(): pl.pallas_call(body, grid=(n_u // U_TILE,), in_specs=[pl.BlockSpec(table....]
    all_to_all x5 -> x7, starting transfers between devices: 26.5 us -> 31.7 us  [to_owners(): return lax.all_to_all(array, 'mem', split_axis=0, concat_axis=0, tiled=True)]
    ppermute x24 -> x30, starting transfers between devices: 20.4 us -> 24.2 us  [swap(): return lax.ppermute(array, axis, [(i, i ^ partner) for i in range(size)])]
    all_to_all x5 -> x7, waiting for transfers between devices: 81.4 us -> 84.7 us  [to_owners(): return lax.all_to_all(array, 'mem', split_axis=0, concat_axis=0, tiled=True)]
  transfers between devices with their start and end apart: 29 -> 37, of which waited for: 15 -> 18; matrix products, arithmetic and copies ran while one was open for 10% -> 11% of each run, Pallas kernels for 21% -> 27%
where the time goes in v3:
time: 479 us; the launch traced here: 477 us
  waiting for transfers between devices  222 us (46%)
  Pallas kernels  140 us (29%)
  starting transfers between devices  56 us (12%)
  local copies, waits for them, and re-layouts  46.7 us (10%)
  other arithmetic  8.68 us (2%)
    ppermute x30, waiting for transfers between devices, swap(): return lax.ppermute(array, axis, [(i, i ^ partner) for i in range(size)])  138 us
    all_to_all x7, waiting for transfers between devices, to_owners(): return lax.all_to_all(array, 'mem', split_axis=0, concat_axis=0, tiled=True)  84.7 us
    pallas_call x5, Pallas kernels, pixel_transform(): pl.pallas_call(body, grid=(count // step,), in_specs=[pl.BlockSpec((inner...  64.6 us
    all_to_all x7, starting transfers between devices, to_owners(): return lax.all_to_all(array, 'mem', split_axis=0, concat_axis=0, tiled=True)  31.7 us
    pallas_call x3, Pallas kernels, y_transform(): pl.pallas_call(body, grid=(n_x // step,), in_specs=[pl.BlockSpec(table.sh...  31 us
    pallas_call x6, Pallas kernels, x_transform(): pl.pallas_call(body, grid=(n_u // U_TILE,), in_specs=[pl.BlockSpec(table....  29.4 us
    ppermute x30, starting transfers between devices, swap(): return lax.ppermute(array, axis, [(i, i ^ partner) for i in range(size)])  24.2 us
    pallas_call x1, Pallas kernels, chi_factors(): pl.pallas_call(body, grid=(count_y // step,), in_specs=[pl.BlockSpec(wind...  15.4 us
  transfers between devices with their start and end apart: 37, of which 18 were waited for; matrix products, arithmetic and copies ran while one was open for 11% of the time, Pallas kernels for 27%

profile of v3, /device:TPU:0, one launch (start us, length us, event | category | flops | bytes accessed | tf_op | source)
XLA Modules:
  0.0 476.6 jit_solution(219132322985323695)
XLA Ops:
  27.2 5.9 %y_transform.3 = bf16[8,10,128,128]{3,2,1,0:T(8,128)(2,1)} custom-call(bf16[1024,512]{1,0:T(8,128)(2,1)} %copy_bitcast_fusion.t_ref, bf16[10,128,128]{2,1,0:T(8,128)(2,1)} %bitcast.62, bf16[10,128,128]{2,1,0:T(8,128)(2,1)} %collective-permute-done.refs_1_, bf16[10,128,128]{2,1,0:T(8,128)(2,1)} %collective-permute-done.1.refs_2_, ...), custom_call_target="tpu_custom_call" | custom-call | flops 1342177280 | bytes 4980736 | tf_op jit(solution)/shard_map/y_transform/pallas_call | solution.py:103
  47.6 9.9 %collective-permute-done.7.refs_2_ = bf16[22,128,128]{2,1,0:T(8,128)(2,1)S(1)} collective-permute-done((bf16[22,128,128]{2,1,0:T(8,128)(2,1)}, bf16[22,128,128]{2,1,0:T(8,128)(2,1)S(1)}, u32[]{:S(2)}, u32[]{:S(2)}) %collective-permute-start.7) | collective-permute-done | bytes 720928 | tf_op jit(solution)/shard_map/ppermute | solution.py:314
  57.5 14.5 %collective-permute-done.8.refs_3_ = bf16[22,128,128]{2,1,0:T(8,128)(2,1)S(1)} collective-permute-done((bf16[22,128,128]{2,1,0:T(8,128)(2,1)S(1)}, bf16[22,128,128]{2,1,0:T(8,128)(2,1)S(1)}, u32[]{:S(2)}, u32[]{:S(2)}) %collective-permute-start.8) | collective-permute-done | bytes 720928 | tf_op jit(solution)/shard_map/ppermute | solution.py:314
  72.9 10.7 %y_transform.4 = (bf16[8,22,48,128]{3,2,1,0:T(8,128)(2,1)}, bf16[8,22,80,128]{3,2,1,0:T(8,128)(2,1)}) custom-call(bf16[1024,512]{1,0:T(8,128)(2,1)} %copy_bitcast_fusion.t_ref, bf16[22,128,128]{2,1,0:T(8,128)(2,1)} %get-tuple-element.122.refs_0_, bf16[22,128,128]{2,1,0:T(8,128)(2,1)} %copy-done.21, bf16[22,128,128]{2,1,0:T(8,128)(2,1)} %copy-done.22, ...), custom_call_target="tpu_custom_call" | custom-call | flops 2952790016 | bytes 9699328 | tf_op jit(solution)/shard_map/y_transform/pallas_call | solution.py:103
  83.6 12.7 %all-to-all-done = bf16[8,10,128,128]{3,2,1,0:T(8,128)(2,1)S(1)} async-done(((bf16[8,10,128,128]{3,2,1,0:T(8,128)(2,1)}), bf16[8,10,128,128]{3,2,1,0:T(8,128)(2,1)S(1)}, u32[]{:S(2)}, u32[]{:S(2)}) %all-to-all-start) | async-done | bytes 2621472 | tf_op jit(solution)/shard_map/all_to_all | solution.py:366
  114.1 8.2 %pad_maximum_fusion.w_ref = f32[2,44,64,128]{3,2,1,0:T(8,128)} fusion(f32[2,44,64,32]{3,2,1,0:T(8,128)} %get-tuple-element.255, f32[2,44,64,32]{3,2,1,0:T(8,128)} %get-tuple-element.256, f32[2,44,64,32]{3,2,1,0:T(8,128)} %get-tuple-element.257, f32[2,44,64,32]{3,2,1,0:T(8,128)} %get-tuple-element.254), kind=kLoop, calls=%fused_computation.5 | loop fusion | flops 2162688 | bytes 5767168 | tf_op jit(solution)/shard_map/concatenate | solution.py:309
  122.3 15.4 %chi_factors.1 = (f32[16,64,1024]{2,1,0:T(8,128)}, f32[16,64,1024]{2,1,0:T(8,128)}) custom-call(f32[2,44,64,128]{3,2,1,0:T(8,128)} %pad_maximum_fusion.w_ref, f32[2,8,128]{2,1,0:T(8,128)} %reshape.174.b_ref, bf16[2048,2048]{1,0:T(8,128)(2,1)} %constant.89.clone.t_ref), custom_call_target="tpu_custom_call" | custom-call | flops 8589934592 | bytes 16777216 | tf_op jit(solution)/shard_map/chi_factors/pallas_call | solution.py:202
  137.7 12.8 %collective-permute-done.11.refs_3_ = bf16[32,128,128]{2,1,0:T(8,128)(2,1)} collective-permute-done((bf16[32,128,128]{2,1,0:T(8,128)(2,1)}, bf16[32,128,128]{2,1,0:T(8,128)(2,1)}, u32[]{:S(2)}, u32[]{:S(2)}) %collective-permute-start.11) | collective-permute-done | bytes 1048608 | tf_op jit(solution)/shard_map/ppermute | solution.py:314
  150.5 5.7 %all-to-all-start.2 = ((bf16[8,22,80,128]{3,2,1,0:T(8,128)(2,1)}), bf16[8,22,80,128]{3,2,1,0:T(8,128)(2,1)}, u32[]{:S(2)}, u32[]{:S(2)}) async-start(bf16[8,22,80,128]{3,2,1,0:T(8,128)(2,1)} %get-tuple-element.148), calls=%async_computation.2 | async-start | bytes 7208960 | tf_op jit(solution)/shard_map/all_to_all | solution.py:366
  165.1 8.2 %gather_fusion.3 = bf16[8,256,2048]{2,1,0:T(8,128)(2,1)} fusion(bf16[8,256,2048]{2,1,0:T(8,128)(2,1)} %constant.92.clone, s32[1024]{0:T(1024)S(1)} %pad_clamp_fusion), kind=kCustom, calls=%fused_computation.3 | custom fusion | bytes 16777248 | tf_op jit(solution)/shard_map/jit(_take)/gather | solution.py:369
  173.3 14.4 %y_transform.5 = (bf16[8,32,48,128]{3,2,1,0:T(8,128)(2,1)}, bf16[8,32,32,128]{3,2,1,0:T(8,128)(2,1)}, bf16[8,32,32,128]{3,2,1,0:T(8,128)(2,1)}, bf16[8,32,16,128]{3,2,1,0:T(8,128)(2,1)}) custom-call(bf16[1024,512]{1,0:T(8,128)(2,1)} %copy_bitcast_fusion.t_ref, bf16[32,128,128]{2,1,0:T(8,128)(2,1)} %get-tuple-element.140.refs_0_, ...), custom_call_target="tpu_custom_call" | custom-call | flops 4294967296 | bytes 13631488 | tf_op jit(solution)/shard_map/y_transform/pallas_call | solution.py:103
  187.8 10.5 %collective-permute-done.14.refs_3_ = bf16[24,2,64,128]{3,2,1,0:T(8,128)(2,1)S(1)} collective-permute-done((bf16[24,2,64,128]{3,2,1,0:T(8,128)(2,1)}, bf16[24,2,64,128]{3,2,1,0:T(8,128)(2,1)S(1)}, u32[]{:S(2)}, u32[]{:S(2)}) %collective-permute-start.14) | collective-permute-done | bytes 786464 | tf_op jit(solution)/shard_map/ppermute | solution.py:314
  198.3 39.0 %all-to-all-done.2 = bf16[8,22,80,128]{3,2,1,0:T(8,128)(2,1)} async-done(((bf16[8,22,80,128]{3,2,1,0:T(8,128)(2,1)}), bf16[8,22,80,128]{3,2,1,0:T(8,128)(2,1)}, u32[]{:S(2)}, u32[]{:S(2)}) %all-to-all-start.2) | async-done | bytes 3604512 | tf_op jit(solution)/shard_map/all_to_all | solution.py:366
  241.8 7.6 %x_transform.7 = (bf16[40,2,64,128]{3,2,1,0:T(8,128)(2,1)}, bf16[40,2,64,128]{3,2,1,0:T(8,128)(2,1)}, bf16[40,2,64,128]{3,2,1,0:T(8,128)(2,1)}, bf16[40,2,64,128]{3,2,1,0:T(8,128)(2,1)}) custom-call(bf16[512,512]{1,0:T(8,128)(2,1)} %bitcast.69, bf16[80,128,128]{2,1,0:T(8,128)(2,1)} %bitcast.60, bf16[176,80,128]{2,1,0:T(8,128)(2,1)} %bitcast.23.refs_1_), custom_call_target="tpu_custom_call" | custom-call | flops 2684354560 | bytes 11010048 | tf_op jit(solution)/shard_map/x_transform/pallas_call | solution.py:154
  252.7 28.6 %collective-permute-done.16.refs_2_ = bf16[40,2,64,128]{3,2,1,0:T(8,128)(2,1)S(1)} collective-permute-done((bf16[40,2,64,128]{3,2,1,0:T(8,128)(2,1)}, bf16[40,2,64,128]{3,2,1,0:T(8,128)(2,1)S(1)}, u32[]{:S(2)}, u32[]{:S(2)}) %collective-permute-start.16) | collective-permute-done | bytes 1310752 | tf_op jit(solution)/shard_map/ppermute | solution.py:314
  281.3 27.3 %collective-permute-done.17.refs_3_ = bf16[40,2,64,128]{3,2,1,0:T(8,128)(2,1)} collective-permute-done((bf16[40,2,64,128]{3,2,1,0:T(8,128)(2,1)}, bf16[40,2,64,128]{3,2,1,0:T(8,128)(2,1)}, u32[]{:S(2)}, u32[]{:S(2)}) %collective-permute-start.17) | collective-permute-done | bytes 1310752 | tf_op jit(solution)/shard_map/ppermute | solution.py:314
  324.1 6.5 %pixel_transform.5 = (f32[8,64,1024]{2,1,0:T(8,128)}, f32[8,64,1024]{2,1,0:T(8,128)}) custom-call(bf16[2048,2048]{1,0:T(8,128)(2,1)} %bitcast.54, bf16[40,2,64,128]{3,2,1,0:T(8,128)(2,1)} %get-tuple-element.214.refs_0_, bf16[40,2,64,128]{3,2,1,0:T(8,128)(2,1)} %copy-done, bf16[40,2,64,128]{3,2,1,0:T(8,128)(2,1)} %copy-done.1, ...), custom_call_target="tpu_custom_call" | custom-call | flops 2147483648 | bytes 10485760 | tf_op jit(solution)/shard_map/pixel_transform/pallas_call | solution.py:272
  330.6 12.3 %collective-permute-done.19.refs_6_ = bf16[24,2,64,128]{3,2,1,0:T(8,128)(2,1)} collective-permute-done((bf16[24,2,64,128]{3,2,1,0:T(8,128)(2,1)}, bf16[24,2,64,128]{3,2,1,0:T(8,128)(2,1)}, u32[]{:S(2)}, u32[]{:S(2)}) %collective-permute-start.19) | collective-permute-done | bytes 786464 | tf_op jit(solution)/shard_map/ppermute | solution.py:314
  342.9 15.9 %collective-permute-done.20.refs_7_ = bf16[24,2,64,128]{3,2,1,0:T(8,128)(2,1)} collective-permute-done((bf16[24,2,64,128]{3,2,1,0:T(8,128)(2,1)}, bf16[24,2,64,128]{3,2,1,0:T(8,128)(2,1)}, u32[]{:S(2)}, u32[]{:S(2)}) %collective-permute-start.20) | collective-permute-done | bytes 786464 | tf_op jit(solution)/shard_map/ppermute | solution.py:314
  373.7 20.0 %pixel_transform.6 = (f32[64,64,1024]{2,1,0:T(8,128)}, f32[64,64,1024]{2,1,0:T(8,128)}) custom-call(bf16[2048,2048]{1,0:T(8,128)(2,1)} %bitcast.55, bf16[24,2,64,128]{3,2,1,0:T(8,128)(2,1)} %get-tuple-element.188.refs_0_, bf16[24,2,64,128]{3,2,1,0:T(8,128)(2,1)} %copy-done.17, bf16[24,2,64,128]{3,2,1,0:T(8,128)(2,1)} %copy-done.18, ...), custom_call_target="tpu_custom_call" | custom-call | flops 12884901888 | bytes 27262976 | tf_op jit(solution)/shard_map/pixel_transform/pallas_call | solution.py:272
  397.3 19.0 %all-to-all-done.5 = bf16[8,32,32,128]{3,2,1,0:T(8,128)(2,1)S(1)} async-done(((bf16[8,32,32,128]{3,2,1,0:T(8,128)(2,1)}), bf16[8,32,32,128]{3,2,1,0:T(8,128)(2,1)S(1)}, u32[]{:S(2)}, u32[]{:S(2)}) %all-to-all-start.5) | async-done | bytes 2097184 | tf_op jit(solution)/shard_map/all_to_all | solution.py:366
  425.7 15.2 %pixel_transform.7 = (f32[64,64,1024]{2,1,0:T(8,128)}, f32[64,64,1024]{2,1,0:T(8,128)}) custom-call(bf16[2048,2048]{1,0:T(8,128)(2,1)} %bitcast.56, bf16[40,2,64,128]{3,2,1,0:T(8,128)(2,1)} %get-tuple-element.214.refs_0_, bf16[40,2,64,128]{3,2,1,0:T(8,128)(2,1)} %copy-done, ...), custom_call_target="tpu_custom_call", output_to_operand_aliasing={{0}: (11, {}), {1}: (12, {})} | custom-call | flops 8589934592 | bytes 20971520 | tf_op jit(solution)/shard_map/pixel_transform/pallas_call | solution.py:272
  452.7 15.2 %pixel_transform.8 = (f32[64,64,1024]{2,1,0:T(8,128)}, f32[64,64,1024]{2,1,0:T(8,128)}) custom-call(bf16[2048,2048]{1,0:T(8,128)(2,1)} %bitcast.57, bf16[40,2,64,128]{3,2,1,0:T(8,128)(2,1)} %get-tuple-element.214.refs_0_, bf16[40,2,64,128]{3,2,1,0:T(8,128)(2,1)} %copy-done, ...), custom_call_target="tpu_custom_call", output_to_operand_aliasing={{0}: (11, {}), {1}: (12, {})} | custom-call | flops 8589934592 | bytes 20971520 | tf_op jit(solution)/shard_map/pixel_transform/pallas_call | solution.py:272
  468.9 7.7 %pixel_transform.9 = (f32[64,64,1024]{2,1,0:T(8,128)}, f32[64,64,1024]{2,1,0:T(8,128)}) custom-call(bf16[2048,2048]{1,0:T(8,128)(2,1)} %bitcast.58, bf16[8,2,64,128]{3,2,1,0:T(8,128)(2,1)} %get-tuple-element.227.refs_0_, bf16[8,2,64,128]{3,2,1,0:T(8,128)(2,1)} %copy-done.13, ...), custom_call_target="tpu_custom_call", output_to_operand_aliasing={{0}: (9, {}), {1}: (10, {})} | custom-call | flops 2147483648 | bytes 10485760 | tf_op jit(solution)/shard_map/pixel_transform/pallas_call | solution.py:272
  (158 shorter events, 132.2 us)
Async XLA Ops:
  33.1 63.2 %all-to-all-start = ((bf16[8,10,128,128]{3,2,1,0:T(8,128)(2,1)}), bf16[8,10,128,128]{3,2,1,0:T(8,128)(2,1)S(1)}, u32[]{:S(2)}, u32[]{:S(2)}) async-start(bf16[8,10,128,128]{3,2,1,0:T(8,128)(2,1)} %y_transform.3), calls=%async_computation | async-start | bytes 5242880 | tf_op jit(solution)/shard_map/all_to_all | solution.py:366
  39.8 32.2 %collective-permute-start.8 = (bf16[22,128,128]{2,1,0:T(8,128)(2,1)S(1)}, bf16[22,128,128]{2,1,0:T(8,128)(2,1)S(1)}, u32[]{:S(2)}, u32[]{:S(2)}) collective-permute-start(bf16[22,128,128]{2,1,0:T(8,128)(2,1)S(1)} %get-tuple-element.125), channel_id=1, source_target_pairs={{0,24},{8,16},{16,8},{24,0},{1,25},{9,17},{17,9},{25,1},{2,26},{10... | collective-permute-start | bytes 2162696 | tf_op jit(solution)/shard_map/ppermute | solution.py:314
  96.3 54.2 %all-to-all-start.1 = ((bf16[8,22,48,128]{3,2,1,0:T(8,128)(2,1)}), bf16[8,22,48,128]{3,2,1,0:T(8,128)(2,1)}, u32[]{:S(2)}, u32[]{:S(2)}) async-start(bf16[8,22,48,128]{3,2,1,0:T(8,128)(2,1)} %get-tuple-element.131), calls=%async_computation.1 | async-start | bytes 4325376 | tf_op jit(solution)/shard_map/all_to_all | solution.py:366
  102.5 35.2 %collective-permute-start.9 = (bf16[32,128,128]{2,1,0:T(8,128)(2,1)}, bf16[32,128,128]{2,1,0:T(8,128)(2,1)}, u32[]{:S(2)}, u32[]{:S(2)}) collective-permute-start(bf16[32,128,128]{2,1,0:T(8,128)(2,1)} %get-tuple-element.137), channel_id=1, source_target_pairs={{0,8},{8,0},{16,24},{24,16},{1,9},{9,1},{17,25},{25,17},{2,10},{10... | collective-permute-start | bytes 3145736 | tf_op jit(solution)/shard_map/ppermute | solution.py:314
  102.6 35.1 %collective-permute-start.10 = (bf16[32,128,128]{2,1,0:T(8,128)(2,1)}, bf16[32,128,128]{2,1,0:T(8,128)(2,1)}, u32[]{:S(2)}, u32[]{:S(2)}) collective-permute-start(bf16[32,128,128]{2,1,0:T(8,128)(2,1)} %get-tuple-element.138), channel_id=1, source_target_pairs={{0,16},{8,24},{16,0},{24,8},{1,17},{9,25},{17,1},{25,9},{2,18},{10... | collective-permute-start | bytes 3145736 | tf_op jit(solution)/shard_map/ppermute | solution.py:314
  104.1 46.4 %collective-permute-start.11 = (bf16[32,128,128]{2,1,0:T(8,128)(2,1)}, bf16[32,128,128]{2,1,0:T(8,128)(2,1)}, u32[]{:S(2)}, u32[]{:S(2)}) collective-permute-start(bf16[32,128,128]{2,1,0:T(8,128)(2,1)} %get-tuple-element.139), channel_id=1, source_target_pairs={{0,24},{8,16},{16,8},{24,0},{1,25},{9,17},{17,9},{25,1},{2,26},{10... | collective-permute-start | bytes 3145736 | tf_op jit(solution)/shard_map/ppermute | solution.py:314
  150.5 86.8 %all-to-all-start.2 = ((bf16[8,22,80,128]{3,2,1,0:T(8,128)(2,1)}), bf16[8,22,80,128]{3,2,1,0:T(8,128)(2,1)}, u32[]{:S(2)}, u32[]{:S(2)}) async-start(bf16[8,22,80,128]{3,2,1,0:T(8,128)(2,1)} %get-tuple-element.148), calls=%async_computation.2 | async-start | bytes 7208960 | tf_op jit(solution)/shard_map/all_to_all | solution.py:366
  161.7 26.0 %collective-permute-start.12 = (bf16[24,2,64,128]{3,2,1,0:T(8,128)(2,1)}, bf16[24,2,64,128]{3,2,1,0:T(8,128)(2,1)S(1)}, u32[]{:S(2)}, u32[]{:S(2)}) collective-permute-start(bf16[24,2,64,128]{3,2,1,0:T(8,128)(2,1)} %get-tuple-element.153), channel_id=1, source_target_pairs={{0,8},{8,0},{16,24},{24,16},{1,9},{9,1},{17,25},{25,17},{2,10},{10... | collective-permute-start | bytes 2359304 | tf_op jit(solution)/shard_map/ppermute | solution.py:314
  161.7 26.1 %collective-permute-start.13 = (bf16[24,2,64,128]{3,2,1,0:T(8,128)(2,1)}, bf16[24,2,64,128]{3,2,1,0:T(8,128)(2,1)S(1)}, u32[]{:S(2)}, u32[]{:S(2)}) collective-permute-start(bf16[24,2,64,128]{3,2,1,0:T(8,128)(2,1)} %get-tuple-element.154), channel_id=1, source_target_pairs={{0,16},{8,24},{16,0},{24,8},{1,17},{9,25},{17,1},{25,9},{2,18},{10... | collective-permute-start | bytes 2359304 | tf_op jit(solution)/shard_map/ppermute | solution.py:314
  163.3 35.0 %collective-permute-start.14 = (bf16[24,2,64,128]{3,2,1,0:T(8,128)(2,1)}, bf16[24,2,64,128]{3,2,1,0:T(8,128)(2,1)S(1)}, u32[]{:S(2)}, u32[]{:S(2)}) collective-permute-start(bf16[24,2,64,128]{3,2,1,0:T(8,128)(2,1)} %get-tuple-element.155), channel_id=1, source_target_pairs={{0,24},{8,16},{16,8},{24,0},{1,25},{9,17},{17,9},{25,1},{2,26},{10... | collective-permute-start | bytes 2359304 | tf_op jit(solution)/shard_map/ppermute | solution.py:314
  237.3 74.8 %all-to-all-start.3 = ((bf16[8,32,48,128]{3,2,1,0:T(8,128)(2,1)}), bf16[8,32,48,128]{3,2,1,0:T(8,128)(2,1)}, u32[]{:S(2)}, u32[]{:S(2)}) async-start(bf16[8,32,48,128]{3,2,1,0:T(8,128)(2,1)} %get-tuple-element.161), calls=%async_computation.3 | async-start | bytes 6291456 | tf_op jit(solution)/shard_map/all_to_all | solution.py:366
  249.4 31.9 %collective-permute-start.16 = (bf16[40,2,64,128]{3,2,1,0:T(8,128)(2,1)}, bf16[40,2,64,128]{3,2,1,0:T(8,128)(2,1)S(1)}, u32[]{:S(2)}, u32[]{:S(2)}) collective-permute-start(bf16[40,2,64,128]{3,2,1,0:T(8,128)(2,1)} %get-tuple-element.169), channel_id=1, source_target_pairs={{0,16},{8,24},{16,0},{24,8},{1,17},{9,25},{17,1},{25,9},{2,18},{10... | collective-permute-start | bytes 3932168 | tf_op jit(solution)/shard_map/ppermute | solution.py:314
  251.0 57.6 %collective-permute-start.17 = (bf16[40,2,64,128]{3,2,1,0:T(8,128)(2,1)}, bf16[40,2,64,128]{3,2,1,0:T(8,128)(2,1)}, u32[]{:S(2)}, u32[]{:S(2)}) collective-permute-start(bf16[40,2,64,128]{3,2,1,0:T(8,128)(2,1)} %get-tuple-element.170), channel_id=1, source_target_pairs={{0,24},{8,16},{16,8},{24,0},{1,25},{9,17},{17,9},{25,1},{2,26},{10... | collective-permute-start | bytes 3932168 | tf_op jit(solution)/shard_map/ppermute | solution.py:314
  312.1 52.3 %all-to-all-start.4 = ((bf16[8,32,32,128]{3,2,1,0:T(8,128)(2,1)}), bf16[8,32,32,128]{3,2,1,0:T(8,128)(2,1)}, u32[]{:S(2)}, u32[]{:S(2)}) async-start(bf16[8,32,32,128]{3,2,1,0:T(8,128)(2,1)} %get-tuple-element.171), calls=%async_computation.4 | async-start | bytes 4194304 | tf_op jit(solution)/shard_map/all_to_all | solution.py:366
  322.2 20.7 %collective-permute-start.19 = (bf16[24,2,64,128]{3,2,1,0:T(8,128)(2,1)}, bf16[24,2,64,128]{3,2,1,0:T(8,128)(2,1)}, u32[]{:S(2)}, u32[]{:S(2)}) collective-permute-start(bf16[24,2,64,128]{3,2,1,0:T(8,128)(2,1)} %get-tuple-element.183), channel_id=1, source_target_pairs={{0,16},{8,24},{16,0},{24,8},{1,17},{9,25},{17,1},{25,9},{2,18},{10... | collective-permute-start | bytes 2359304 | tf_op jit(solution)/shard_map/ppermute | solution.py:314
  323.8 35.1 %collective-permute-start.20 = (bf16[24,2,64,128]{3,2,1,0:T(8,128)(2,1)}, bf16[24,2,64,128]{3,2,1,0:T(8,128)(2,1)}, u32[]{:S(2)}, u32[]{:S(2)}) collective-permute-start(bf16[24,2,64,128]{3,2,1,0:T(8,128)(2,1)} %get-tuple-element.184), channel_id=1, source_target_pairs={{0,24},{8,16},{16,8},{24,0},{1,25},{9,17},{17,9},{25,1},{2,26},{10... | collective-permute-start | bytes 2359304 | tf_op jit(solution)/shard_map/ppermute | solution.py:314
  364.4 51.9 %all-to-all-start.5 = ((bf16[8,32,32,128]{3,2,1,0:T(8,128)(2,1)}), bf16[8,32,32,128]{3,2,1,0:T(8,128)(2,1)S(1)}, u32[]{:S(2)}, u32[]{:S(2)}) async-start(bf16[8,32,32,128]{3,2,1,0:T(8,128)(2,1)} %get-tuple-element.187), calls=%async_computation.5 | async-start | bytes 4194304 | tf_op jit(solution)/shard_map/all_to_all | solution.py:366
  371.8 21.9 %collective-permute-start.21 = (bf16[16,2,64,128]{3,2,1,0:T(8,128)(2,1)}, bf16[16,2,64,128]{3,2,1,0:T(8,128)(2,1)S(1)}, u32[]{:S(2)}, u32[]{:S(2)}) collective-permute-start(bf16[16,2,64,128]{3,2,1,0:T(8,128)(2,1)} %get-tuple-element.202), channel_id=1, source_target_pairs={{0,8},{8,0},{16,24},{24,16},{1,9},{9,1},{17,25},{25,17},{2,10},{10... | collective-permute-start | bytes 1572872 | tf_op jit(solution)/shard_map/ppermute | solution.py:314
  371.9 21.9 %collective-permute-start.22 = (bf16[16,2,64,128]{3,2,1,0:T(8,128)(2,1)}, bf16[16,2,64,128]{3,2,1,0:T(8,128)(2,1)S(1)}, u32[]{:S(2)}, u32[]{:S(2)}) collective-permute-start(bf16[16,2,64,128]{3,2,1,0:T(8,128)(2,1)} %get-tuple-element.203), channel_id=1, source_target_pairs={{0,16},{8,24},{16,0},{24,8},{1,17},{9,25},{17,1},{25,9},{2,18},{10... | collective-permute-start | bytes 1572872 | tf_op jit(solution)/shard_map/ppermute | solution.py:314
  373.4 23.9 %collective-permute-start.23 = (bf16[16,2,64,128]{3,2,1,0:T(8,128)(2,1)}, bf16[16,2,64,128]{3,2,1,0:T(8,128)(2,1)}, u32[]{:S(2)}, u32[]{:S(2)}) collective-permute-start(bf16[16,2,64,128]{3,2,1,0:T(8,128)(2,1)} %get-tuple-element.204), channel_id=1, source_target_pairs={{0,24},{8,16},{16,8},{24,0},{1,25},{9,17},{17,9},{25,1},{2,26},{10... | collective-permute-start | bytes 1572872 | tf_op jit(solution)/shard_map/ppermute | solution.py:314
  416.3 29.6 %all-to-all-start.6 = ((bf16[8,32,16,128]{3,2,1,0:T(8,128)(2,1)}), bf16[8,32,16,128]{3,2,1,0:T(8,128)(2,1)S(1)}, u32[]{:S(2)}, u32[]{:S(2)}) async-start(bf16[8,32,16,128]{3,2,1,0:T(8,128)(2,1)} %get-tuple-element.211), calls=%async_computation.6 | async-start | bytes 2097152 | tf_op jit(solution)/shard_map/all_to_all | solution.py:366
  423.9 27.5 %collective-permute-start.27 = (bf16[16,2,64,128]{3,2,1,0:T(8,128)(2,1)}, bf16[16,2,64,128]{3,2,1,0:T(8,128)(2,1)S(1)}, u32[]{:S(2)}, u32[]{:S(2)}) collective-permute-start(bf16[16,2,64,128]{3,2,1,0:T(8,128)(2,1)} %get-tuple-element.235), channel_id=1, source_target_pairs={{0,8},{8,0},{16,24},{24,16},{1,9},{9,1},{17,25},{25,17},{2,10},{10... | collective-permute-start | bytes 1572872 | tf_op jit(solution)/shard_map/ppermute | solution.py:314
  423.9 27.9 %collective-permute-start.28 = (bf16[16,2,64,128]{3,2,1,0:T(8,128)(2,1)}, bf16[16,2,64,128]{3,2,1,0:T(8,128)(2,1)S(1)}, u32[]{:S(2)}, u32[]{:S(2)}) collective-permute-start(bf16[16,2,64,128]{3,2,1,0:T(8,128)(2,1)} %get-tuple-element.236), channel_id=1, source_target_pairs={{0,16},{8,24},{16,0},{24,8},{1,17},{9,25},{17,1},{25,9},{2,18},{10... | collective-permute-start | bytes 1572872 | tf_op jit(solution)/shard_map/ppermute | solution.py:314
  425.4 26.4 %collective-permute-start.29 = (bf16[16,2,64,128]{3,2,1,0:T(8,128)(2,1)}, bf16[16,2,64,128]{3,2,1,0:T(8,128)(2,1)S(1)}, u32[]{:S(2)}, u32[]{:S(2)}) collective-permute-start(bf16[16,2,64,128]{3,2,1,0:T(8,128)(2,1)} %get-tuple-element.237), channel_id=1, source_target_pairs={{0,24},{8,16},{16,8},{24,0},{1,25},{9,17},{17,9},{25,1},{2,26},{10... | collective-permute-start | bytes 1572872 | tf_op jit(solution)/shard_map/ppermute | solution.py:314
  (37 other events, 556.3 us)

commit v4 on v3

--- a/solution.py
+++ b/solution.py
@@ -14,7 +14,8 @@
 STRIDE_X = 2
 LANES = 128
 U_TILE = 8
-VMEM_BYTES = 56 * 1024 * 1024
+VMEM_BYTES = 36 * 1024 * 1024
+LARGE_VMEM_BYTES = 56 * 1024 * 1024
 
 wiener_floor = 0.5
 
@@ -68,8 +69,8 @@
     return np.stack([upper, lower], axis=1).reshape(pixels // depth, 2 * depth, 2 * pixels)
 
 
-def params():
-    return pltpu.CompilerParams(vmem_limit_bytes=VMEM_BYTES)
+def params(limit=VMEM_BYTES):
+    return pltpu.CompilerParams(vmem_limit_bytes=limit)
 
 
 def y_transform(table, pieces, owners, u_chunks):
@@ -280,7 +281,7 @@
         out_specs=[pl.BlockSpec((step, v_own, pixels), lambda s: (here + s, 0, 0))] * 2,
         out_shape=[shape] * 2,
         input_output_aliases=aliases,
-        compiler_params=params(),
+        compiler_params=params(LARGE_VMEM_BYTES),
         cost_estimate=pl.CostEstimate(
             flops=4 * count * v_own * inner * pixels,
             bytes_accessed=4 * inner * pixels + 12 * count * v_own * pixels,
@@ -337,7 +338,7 @@
     n_q = pixels // (n_grp * depth)
     partners = grp ^ jnp.arange(n_grp, dtype=jnp.int32)
     if n_x >= 32:
-        opening = 2 * (n_x * 5 // 32)
+        opening = n_x // 4
         x_cuts = [(0, opening), (opening, n_x - opening)]
     else:
         x_cuts = [(0, n_x)]
@@ -374,7 +375,9 @@
     fronts = [(q, first, count) for q in range(n_q - 1) for first, count in x_cuts]
     fronts.append((n_q - 1, 0, n_x))
     halves = [u_chunks[0], (u_chunks[0][1], u_own - u_chunks[0][1])]
-    pieces = exchange(cut(*fronts[0]))
+    pieces = cut(*fronts[0])
+    pieces[n_grp // 2 :], probe_wave = lax.optimization_barrier((pieces[n_grp // 2 :], probe_wave))
+    pieces = exchange(pieces)
     whole_probe = gather_rows(probe_wave, "mem")
     arrived = []
     for i in range(len(fronts) - 1):
@@ -427,26 +430,27 @@
     def finish(c, outs):
         first, count = u_chunks[c]
         own = [(first, p) for p in late[c]]
-        if c == len(u_chunks) - 1 and partial:
-            return pixel_transform(tk, inner, own, factors, partial, first, count, u_own, outs)
+        if partials[c]:
+            return pixel_transform(tk, inner, own, factors, partials[c], first, count, u_own, outs)
         return pixel_transform(tk, 0, early_of(first) + own, factors, [], first, count, u_own, outs)
 
     outs = []
-    partial = []
+    partials = [[] for _ in u_chunks]
     for c in range(1, len(u_chunks)):
-        sending, last, early, late, partial, outs = lax.optimization_barrier(
-            (late_ready[c], last, early, late, partial, outs)
+        sending, last, early, late, partials, outs = lax.optimization_barrier(
+            (late_ready[c], last, early, late, partials, outs)
         )
         following = to_owners(sending)
         first, count = u_chunks[c - 1]
         late.append(exchange(x_transform(tx_late, [(first, last)], first, count, n_grp)))
         last = following
         if c == 1 and early:
-            first, count = u_chunks[-1]
-            partial = pixel_transform(tk, 0, early_of(first), [], [], first, count, u_own, [])
+            for later in range(len(u_chunks) - 2, len(u_chunks)):
+                first, count = u_chunks[later]
+                partials[later] = pixel_transform(tk, 0, early_of(first), [], [], first, count, u_own, [])
         if c >= 2:
             outs = finish(c - 2, outs)
-    last, partial, outs = lax.optimization_barrier((last, partial, outs))
+    last, partials, outs = lax.optimization_barrier((last, partials, outs))
     first, count = u_chunks[-1]
     late.append(exchange(x_transform(tx_late, [(first, last)], first, count, n_grp)))
     for c in range(max(0, len(u_chunks) - 2), len(u_chunks)):

time: 479 us -> 468 us (0.977)
  local copies, waits for them, and re-layouts: 46.7 us -> 73.1 us
  waiting for transfers between devices: 222 us -> 202 us
  Pallas kernels: 140 us -> 124 us
    unnamed x53 -> x76, local copies, waits for them, and re-layouts: 9.33 us -> 27.7 us
    ppermute x30, waiting for transfers between devices: 138 us -> 121 us  [swap(): return lax.ppermute(array, axis, [(i, i ^ partner) for i in range(size)])]
    pallas_call x6, Pallas kernels: 29.4 us -> 18.2 us  [x_transform(): pl.pallas_call(body, grid=(n_u // U_TILE,), in_specs=[pl.BlockSpec(table....]
    pallas_call x3, Pallas kernels: 31 us -> 21.4 us  [y_transform(): pl.pallas_call(body, grid=(n_x // step,), in_specs=[pl.BlockSpec(table.sh...]
    pallas_call x5 -> x6, Pallas kernels: 64.6 us -> 71.3 us  [pixel_transform(): pl.pallas_call(body, grid=(count // step,), in_specs=[pl.BlockSpec((inner...]
    slice x1, local copies, waits for them, and re-layouts: 4.72 us -> 9.94 us  [probe_windows(): moved[:, p:p + n_rows]]
  transfers between devices with their start and end apart: 37 -> 37, of which waited for: 18 -> 20; matrix products, arithmetic and copies ran while one was open for 11% -> 12% of each run, Pallas kernels for 27% -> 24%
where the time goes in v4:
time: 468 us; the launch traced here: 465 us
  waiting for transfers between devices  202 us (43%)
  Pallas kernels  124 us (26%)
  local copies, waits for them, and re-layouts  73.1 us (16%)
  starting transfers between devices  54.5 us (12%)
  other arithmetic  8.32 us (2%)
    ppermute x30, waiting for transfers between devices, swap(): return lax.ppermute(array, axis, [(i, i ^ partner) for i in range(size)])  121 us
    all_to_all x7, waiting for transfers between devices, to_owners(): return lax.all_to_all(array, 'mem', split_axis=0, concat_axis=0, tiled=True)  81 us
    pallas_call x6, Pallas kernels, pixel_transform(): pl.pallas_call(body, grid=(count // step,), in_specs=[pl.BlockSpec((inner...  71.3 us
    all_to_all x7, starting transfers between devices, to_owners(): return lax.all_to_all(array, 'mem', split_axis=0, concat_axis=0, tiled=True)  30.3 us
    unnamed x76, local copies, waits for them, and re-layouts  27.7 us
    ppermute x30, starting transfers between devices, swap(): return lax.ppermute(array, axis, [(i, i ^ partner) for i in range(size)])  24.2 us
    pallas_call x3, Pallas kernels, y_transform(): pl.pallas_call(body, grid=(n_x // step,), in_specs=[pl.BlockSpec(table.sh...  21.4 us
    pallas_call x6, Pallas kernels, x_transform(): pl.pallas_call(body, grid=(n_u // U_TILE,), in_specs=[pl.BlockSpec(table....  18.2 us
  transfers between devices with their start and end apart: 37, of which 20 were waited for; matrix products, arithmetic and copies ran while one was open for 12% of the time, Pallas kernels for 24%

profile of v4, /device:TPU:0, one launch (start us, length us, event | category | flops | bytes accessed | tf_op | source)
XLA Modules:
  0.0 465.4 jit_solution(8402861634196187499)
XLA Ops:
  26.7 5.3 %all-to-all-start = ((bf16[8,8,128,128]{3,2,1,0:T(8,128)(2,1)}), bf16[8,8,128,128]{3,2,1,0:T(8,128)(2,1)S(1)}, u32[]{:S(2)}, u32[]{:S(2)}) async-start(bf16[8,8,128,128]{3,2,1,0:T(8,128)(2,1)} %y_transform.3), calls=%async_computation | async-start | bytes 4194304 | tf_op jit(solution)/shard_map/all_to_all | solution.py:367
  41.4 11.3 %collective-permute-done.7.refs_2_ = bf16[24,128,128]{2,1,0:T(8,128)(2,1)S(1)} collective-permute-done((bf16[24,128,128]{2,1,0:T(8,128)(2,1)}, bf16[24,128,128]{2,1,0:T(8,128)(2,1)S(1)}, u32[]{:S(2)}, u32[]{:S(2)}) %collective-permute-start.7) | collective-permute-done | bytes 786464 | tf_op jit(solution)/shard_map/ppermute | solution.py:315
  52.6 15.9 %collective-permute-done.8.refs_3_ = bf16[24,128,128]{2,1,0:T(8,128)(2,1)S(1)} collective-permute-done((bf16[24,128,128]{2,1,0:T(8,128)(2,1)}, bf16[24,128,128]{2,1,0:T(8,128)(2,1)S(1)}, u32[]{:S(2)}, u32[]{:S(2)}) %collective-permute-start.8) | collective-permute-done | bytes 786464 | tf_op jit(solution)/shard_map/ppermute | solution.py:315
  68.5 5.6 %y_transform.4 = (bf16[8,24,48,128]{3,2,1,0:T(8,128)(2,1)S(1)}, bf16[8,24,80,128]{3,2,1,0:T(8,128)(2,1)S(1)}) custom-call(bf16[1024,512]{1,0:T(8,128)(2,1)S(1)} %copy_bitcast_fusion.t_ref, bf16[24,128,128]{2,1,0:T(8,128)(2,1)S(1)} %copy-done.11, bf16[24,128,128]{2,1,0:T(8,128)(2,1)S(1)} %collective-permute-done.6.refs_1_, ...), custom_call_target="tpu_custom_call" | custom-call | flops 3221225472 | bytes 10485760 | tf_op jit(solution)/shard_map/y_transform/pallas_call | solution.py:104
  80.1 4.8 %all-to-all-start.1 = ((bf16[8,24,48,128]{3,2,1,0:T(8,128)(2,1)}), bf16[8,24,48,128]{3,2,1,0:T(8,128)(2,1)S(1)}, u32[]{:S(2)}, u32[]{:S(2)}) async-start(bf16[8,24,48,128]{3,2,1,0:T(8,128)(2,1)} %copy-done.5), calls=%async_computation.1 | async-start | bytes 4718592 | tf_op jit(solution)/shard_map/all_to_all | solution.py:367
  98.8 9.9 %fusion.8 = (f32[2,44,64,32]{3,2,1,0:T(8,128)}, f32[2,44,64,32]{3,2,1,0:T(8,128)}, f32[2,44,64,32]{3,2,1,0:T(8,128)}, f32[2,44,64,32]{3,2,1,0:T(8,128)}) fusion(f32[2,47,64,32]{3,2,1,0:T(8,128)} %reshape.173), kind=kLoop, calls=%fused_computation.72 | loop fusion | bytes 5767168 | tf_op jit(solution)/shard_map/slice | solution.py:310
  108.8 6.6 %pad_maximum_fusion.w_ref = f32[2,44,64,128]{3,2,1,0:T(8,128)S(1)} fusion(f32[2,44,64,32]{3,2,1,0:T(8,128)} %get-tuple-element.277, f32[2,44,64,32]{3,2,1,0:T(8,128)} %get-tuple-element.278, f32[2,44,64,32]{3,2,1,0:T(8,128)} %get-tuple-element.279, f32[2,44,64,32]{3,2,1,0:T(8,128)} %get-tuple-element.276), kind=kLoop, calls=%fused_computation.5 | loop fusion | flops 2162688 | bytes 5767168 | tf_op jit(solution)/shard_map/concatenate | solution.py:310
  115.4 13.0 %chi_factors.1 = (f32[16,64,1024]{2,1,0:T(8,128)S(1)}, f32[16,64,1024]{2,1,0:T(8,128)S(1)}) custom-call(f32[2,44,64,128]{3,2,1,0:T(8,128)S(1)} %pad_maximum_fusion.w_ref, f32[2,8,128]{2,1,0:T(8,128)S(1)} %reshape.174.b_ref, bf16[2048,2048]{1,0:T(8,128)(2,1)} %constant.89.clone.t_ref), custom_call_target="tpu_custom_call" | custom-call | flops 8589934592 | bytes 16777216 | tf_op jit(solution)/shard_map/chi_factors/pallas_call | solution.py:203
  155.5 8.2 %gather_fusion.3 = bf16[8,256,2048]{2,1,0:T(8,128)(2,1)} fusion(bf16[8,256,2048]{2,1,0:T(8,128)(2,1)} %constant.92.clone, s32[1024]{0:T(1024)S(1)} %pad_clamp_fusion), kind=kCustom, calls=%fused_computation.3 | custom fusion | bytes 16777248 | tf_op jit(solution)/shard_map/jit(_take)/gather | solution.py:370
  163.8 12.9 %y_transform.5 = (bf16[8,32,48,128]{3,2,1,0:T(8,128)(2,1)S(1)}, bf16[8,32,32,128]{3,2,1,0:T(8,128)(2,1)S(1)}, bf16[8,32,32,128]{3,2,1,0:T(8,128)(2,1)}, bf16[8,32,16,128]{3,2,1,0:T(8,128)(2,1)}) custom-call(bf16[1024,512]{1,0:T(8,128)(2,1)S(1)} %copy_bitcast_fusion.t_ref, bf16[32,128,128]{2,1,0:T(8,128)(2,1)S(1)} %copy-done.10, ...), custom_call_target="tpu_custom_call" | custom-call | flops 4294967296 | bytes 13631488 | tf_op jit(solution)/shard_map/y_transform/pallas_call | solution.py:104
  179.7 8.1 %collective-permute-done.14.refs_3_ = bf16[24,2,64,128]{3,2,1,0:T(8,128)(2,1)} collective-permute-done((bf16[24,2,64,128]{3,2,1,0:T(8,128)(2,1)}, bf16[24,2,64,128]{3,2,1,0:T(8,128)(2,1)}, u32[]{:S(2)}, u32[]{:S(2)}) %collective-permute-start.14) | collective-permute-done | bytes 786464 | tf_op jit(solution)/shard_map/ppermute | solution.py:315
  187.7 43.8 %all-to-all-done.2 = bf16[8,24,80,128]{3,2,1,0:T(8,128)(2,1)} async-done(((bf16[8,24,80,128]{3,2,1,0:T(8,128)(2,1)}), bf16[8,24,80,128]{3,2,1,0:T(8,128)(2,1)}, u32[]{:S(2)}, u32[]{:S(2)}) %all-to-all-start.2) | async-done | bytes 3932192 | tf_op jit(solution)/shard_map/all_to_all | solution.py:367
  237.8 6.0 %x_transform.7 = (bf16[40,2,64,128]{3,2,1,0:T(8,128)(2,1)S(1)}, bf16[40,2,64,128]{3,2,1,0:T(8,128)(2,1)S(1)}, bf16[40,2,64,128]{3,2,1,0:T(8,128)(2,1)S(1)}, bf16[40,2,64,128]{3,2,1,0:T(8,128)(2,1)S(1)}) custom-call(bf16[512,512]{1,0:T(8,128)(2,1)S(1)} %bitcast.64, bf16[64,128,128]{2,1,0:T(8,128)(2,1)S(1)} %bitcast.55, bf16[192,80,128]{2,1,0:T(8,128)(2,1)} %bitcast.23.refs_1_), custom_call_target="tpu_custom_call" | custom-call | flops 2684354560 | bytes 11010048 | tf_op jit(solution)/shard_map/x_transform/pallas_call | solution.py:155
  247.9 28.5 %collective-permute-done.16.refs_2_ = bf16[40,2,64,128]{3,2,1,0:T(8,128)(2,1)S(1)} collective-permute-done((bf16[40,2,64,128]{3,2,1,0:T(8,128)(2,1)S(1)}, bf16[40,2,64,128]{3,2,1,0:T(8,128)(2,1)S(1)}, u32[]{:S(2)}, u32[]{:S(2)}) %collective-permute-start.16) | collective-permute-done | bytes 1310752 | tf_op jit(solution)/shard_map/ppermute | solution.py:315
  277.5 26.3 %collective-permute-done.17.refs_3_ = bf16[40,2,64,128]{3,2,1,0:T(8,128)(2,1)} collective-permute-done((bf16[40,2,64,128]{3,2,1,0:T(8,128)(2,1)S(1)}, bf16[40,2,64,128]{3,2,1,0:T(8,128)(2,1)}, u32[]{:S(2)}, u32[]{:S(2)}) %collective-permute-start.17) | collective-permute-done | bytes 1310752 | tf_op jit(solution)/shard_map/ppermute | solution.py:315
  316.2 6.5 %pixel_transform.7 = (f32[8,64,1024]{2,1,0:T(8,128)}, f32[8,64,1024]{2,1,0:T(8,128)}) custom-call(bf16[2048,2048]{1,0:T(8,128)(2,1)} %bitcast.65, bf16[40,2,64,128]{3,2,1,0:T(8,128)(2,1)} %copy-done.2, bf16[40,2,64,128]{3,2,1,0:T(8,128)(2,1)} %copy-done.23, bf16[40,2,64,128]{3,2,1,0:T(8,128)(2,1)} %copy-done.24, ...), custom_call_target="tpu_custom_call" | custom-call | flops 2147483648 | bytes 10485760 | tf_op jit(solution)/shard_map/pixel_transform/pallas_call | solution.py:273
  322.7 9.5 %pixel_transform.6 = (f32[16,64,1024]{2,1,0:T(8,128)}, f32[16,64,1024]{2,1,0:T(8,128)}) custom-call(bf16[2048,2048]{1,0:T(8,128)(2,1)} %bitcast.66, bf16[40,2,64,128]{3,2,1,0:T(8,128)(2,1)} %copy-done.2, bf16[40,2,64,128]{3,2,1,0:T(8,128)(2,1)} %copy-done.23, bf16[40,2,64,128]{3,2,1,0:T(8,128)(2,1)} %copy-done.24, ...), custom_call_target="tpu_custom_call" | custom-call | flops 4294967296 | bytes 16777216 | tf_op jit(solution)/shard_map/pixel_transform/pallas_call | solution.py:273
  335.7 15.1 %collective-permute-done.20.refs_7_ = bf16[24,2,64,128]{3,2,1,0:T(8,128)(2,1)} collective-permute-done((bf16[24,2,64,128]{3,2,1,0:T(8,128)(2,1)S(1)}, bf16[24,2,64,128]{3,2,1,0:T(8,128)(2,1)}, u32[]{:S(2)}, u32[]{:S(2)}) %collective-permute-start.20) | collective-permute-done | bytes 786464 | tf_op jit(solution)/shard_map/ppermute | solution.py:315
  350.8 7.9 %all-to-all-done.4 = bf16[8,32,32,128]{3,2,1,0:T(8,128)(2,1)} async-done(((bf16[8,32,32,128]{3,2,1,0:T(8,128)(2,1)}), bf16[8,32,32,128]{3,2,1,0:T(8,128)(2,1)}, u32[]{:S(2)}, u32[]{:S(2)}) %all-to-all-start.4) | async-done | bytes 2097184 | tf_op jit(solution)/shard_map/all_to_all | solution.py:367
  367.8 20.0 %pixel_transform.8 = (f32[64,64,1024]{2,1,0:T(8,128)}, f32[64,64,1024]{2,1,0:T(8,128)}) custom-call(bf16[2048,2048]{1,0:T(8,128)(2,1)} %bitcast.67, bf16[24,2,64,128]{3,2,1,0:T(8,128)(2,1)} %copy-done.21, bf16[24,2,64,128]{3,2,1,0:T(8,128)(2,1)} %copy-done.34, bf16[24,2,64,128]{3,2,1,0:T(8,128)(2,1)} %collective-permute-done.13.refs_2_, ...), custom_call_target="tpu_custom_call" | custom-call | flops 12884901888 | bytes 27262976 | tf_op jit(solution)/shard_map/pixel_transform/pallas_call | solution.py:273
  391.2 19.4 %all-to-all-done.5 = bf16[8,32,32,128]{3,2,1,0:T(8,128)(2,1)S(1)} async-done(((bf16[8,32,32,128]{3,2,1,0:T(8,128)(2,1)}), bf16[8,32,32,128]{3,2,1,0:T(8,128)(2,1)S(1)}, u32[]{:S(2)}, u32[]{:S(2)}) %all-to-all-start.5) | async-done | bytes 2097184 | tf_op jit(solution)/shard_map/all_to_all | solution.py:367
  420.7 15.2 %pixel_transform.9 = (f32[64,64,1024]{2,1,0:T(8,128)}, f32[64,64,1024]{2,1,0:T(8,128)}) custom-call(bf16[2048,2048]{1,0:T(8,128)(2,1)} %bitcast.68, bf16[40,2,64,128]{3,2,1,0:T(8,128)(2,1)} %copy-done.2, bf16[40,2,64,128]{3,2,1,0:T(8,128)(2,1)} %copy-done.23, bf16[40,2,64,128]{3,2,1,0:T(8,128)(2,1)} %copy-done.24, ...), custom_call_target="tpu_custom_call", output_to_operand_aliasing={{0}: (11, {}), {1}: (12, {})} | custom-call | flops 8589934592 | bytes 20971520 | tf_op jit(solution)/shard_map/pixel_transform/pallas_call | solution.py:273
  444.3 12.4 %pixel_transform.10 = (f32[64,64,1024]{2,1,0:T(8,128)}, f32[64,64,1024]{2,1,0:T(8,128)}) custom-call(bf16[2048,2048]{1,0:T(8,128)(2,1)} %bitcast.69, bf16[16,2,64,128]{3,2,1,0:T(8,128)(2,1)} %copy-done.19, bf16[16,2,64,128]{3,2,1,0:T(8,128)(2,1)} %copy-done.28, ...), custom_call_target="tpu_custom_call", output_to_operand_aliasing={{0}: (9, {}), {1}: (10, {})} | custom-call | flops 4294967296 | bytes 16777216 | tf_op jit(solution)/shard_map/pixel_transform/pallas_call | solution.py:273
  457.7 7.7 %pixel_transform.11 = (f32[64,64,1024]{2,1,0:T(8,128)}, f32[64,64,1024]{2,1,0:T(8,128)}) custom-call(bf16[2048,2048]{1,0:T(8,128)(2,1)} %bitcast.70, bf16[8,2,64,128]{3,2,1,0:T(8,128)(2,1)} %copy-done.20, bf16[8,2,64,128]{3,2,1,0:T(8,128)(2,1)} %copy-done.29, bf16[8,2,64,128]{3,2,1,0:T(8,128)(2,1)} %copy-done.30, ...), custom_call_target="tpu_custom_call", output_to_operand_aliasing={{0}: (9, {}), {1}: (10, {})} | custom-call | flops 2147483648 | bytes 10485760 | tf_op jit(solution)/shard_map/pixel_transform/pallas_call | solution.py:273
  (184 shorter events, 144.2 us)
Async XLA Ops:
  26.7 52.0 %all-to-all-start = ((bf16[8,8,128,128]{3,2,1,0:T(8,128)(2,1)}), bf16[8,8,128,128]{3,2,1,0:T(8,128)(2,1)S(1)}, u32[]{:S(2)}, u32[]{:S(2)}) async-start(bf16[8,8,128,128]{3,2,1,0:T(8,128)(2,1)} %y_transform.3), calls=%async_computation | async-start | bytes 4194304 | tf_op jit(solution)/shard_map/all_to_all | solution.py:367
  32.0 20.6 %collective-permute-start.7 = (bf16[24,128,128]{2,1,0:T(8,128)(2,1)}, bf16[24,128,128]{2,1,0:T(8,128)(2,1)S(1)}, u32[]{:S(2)}, u32[]{:S(2)}) collective-permute-start(bf16[24,128,128]{2,1,0:T(8,128)(2,1)} %get-tuple-element.138), channel_id=1, source_target_pairs={{0,16},{8,24},{16,0},{24,8},{1,17},{9,25},{17,1},{25,9},{2,18},{10... | collective-permute-start | bytes 2359304 | tf_op jit(solution)/shard_map/ppermute | solution.py:315
  33.6 35.0 %collective-permute-start.8 = (bf16[24,128,128]{2,1,0:T(8,128)(2,1)}, bf16[24,128,128]{2,1,0:T(8,128)(2,1)S(1)}, u32[]{:S(2)}, u32[]{:S(2)}) collective-permute-start(bf16[24,128,128]{2,1,0:T(8,128)(2,1)} %get-tuple-element.139), channel_id=1, source_target_pairs={{0,24},{8,16},{16,8},{24,0},{1,25},{9,17},{17,9},{25,1},{2,26},{10... | collective-permute-start | bytes 2359304 | tf_op jit(solution)/shard_map/ppermute | solution.py:315
  80.1 59.3 %all-to-all-start.1 = ((bf16[8,24,48,128]{3,2,1,0:T(8,128)(2,1)}), bf16[8,24,48,128]{3,2,1,0:T(8,128)(2,1)S(1)}, u32[]{:S(2)}, u32[]{:S(2)}) async-start(bf16[8,24,48,128]{3,2,1,0:T(8,128)(2,1)} %copy-done.5), calls=%async_computation.1 | async-start | bytes 4718592 | tf_op jit(solution)/shard_map/all_to_all | solution.py:367
  89.5 43.0 %collective-permute-start.9 = (bf16[32,128,128]{2,1,0:T(8,128)(2,1)}, bf16[32,128,128]{2,1,0:T(8,128)(2,1)}, u32[]{:S(2)}, u32[]{:S(2)}) collective-permute-start(bf16[32,128,128]{2,1,0:T(8,128)(2,1)} %get-tuple-element.151), channel_id=1, source_target_pairs={{0,8},{8,0},{16,24},{24,16},{1,9},{9,1},{17,25},{25,17},{2,10},{10... | collective-permute-start | bytes 3145736 | tf_op jit(solution)/shard_map/ppermute | solution.py:315
  89.7 42.7 %collective-permute-start.10 = (bf16[32,128,128]{2,1,0:T(8,128)(2,1)}, bf16[32,128,128]{2,1,0:T(8,128)(2,1)}, u32[]{:S(2)}, u32[]{:S(2)}) collective-permute-start(bf16[32,128,128]{2,1,0:T(8,128)(2,1)} %get-tuple-element.152), channel_id=1, source_target_pairs={{0,16},{8,24},{16,0},{24,8},{1,17},{9,25},{17,1},{25,9},{2,18},{10... | collective-permute-start | bytes 3145736 | tf_op jit(solution)/shard_map/ppermute | solution.py:315
  91.2 46.0 %collective-permute-start.11 = (bf16[32,128,128]{2,1,0:T(8,128)(2,1)}, bf16[32,128,128]{2,1,0:T(8,128)(2,1)}, u32[]{:S(2)}, u32[]{:S(2)}) collective-permute-start(bf16[32,128,128]{2,1,0:T(8,128)(2,1)} %get-tuple-element.153), channel_id=1, source_target_pairs={{0,24},{8,16},{16,8},{24,0},{1,25},{9,17},{17,9},{25,1},{2,26},{10... | collective-permute-start | bytes 3145736 | tf_op jit(solution)/shard_map/ppermute | solution.py:315
  139.4 92.1 %all-to-all-start.2 = ((bf16[8,24,80,128]{3,2,1,0:T(8,128)(2,1)}), bf16[8,24,80,128]{3,2,1,0:T(8,128)(2,1)}, u32[]{:S(2)}, u32[]{:S(2)}) async-start(bf16[8,24,80,128]{3,2,1,0:T(8,128)(2,1)} %copy-done.3), calls=%async_computation.2 | async-start | bytes 7864320 | tf_op jit(solution)/shard_map/all_to_all | solution.py:367
  151.0 28.7 %collective-permute-start.12 = (bf16[24,2,64,128]{3,2,1,0:T(8,128)(2,1)}, bf16[24,2,64,128]{3,2,1,0:T(8,128)(2,1)S(1)}, u32[]{:S(2)}, u32[]{:S(2)}) collective-permute-start(bf16[24,2,64,128]{3,2,1,0:T(8,128)(2,1)} %get-tuple-element.167), channel_id=1, source_target_pairs={{0,8},{8,0},{16,24},{24,16},{1,9},{9,1},{17,25},{25,17},{2,10},{10... | collective-permute-start | bytes 2359304 | tf_op jit(solution)/shard_map/ppermute | solution.py:315
  151.0 28.7 %collective-permute-start.13 = (bf16[24,2,64,128]{3,2,1,0:T(8,128)(2,1)}, bf16[24,2,64,128]{3,2,1,0:T(8,128)(2,1)}, u32[]{:S(2)}, u32[]{:S(2)}) collective-permute-start(bf16[24,2,64,128]{3,2,1,0:T(8,128)(2,1)} %get-tuple-element.168), channel_id=1, source_target_pairs={{0,16},{8,24},{16,0},{24,8},{1,17},{9,25},{17,1},{25,9},{2,18},{10... | collective-permute-start | bytes 2359304 | tf_op jit(solution)/shard_map/ppermute | solution.py:315
  152.5 35.2 %collective-permute-start.14 = (bf16[24,2,64,128]{3,2,1,0:T(8,128)(2,1)}, bf16[24,2,64,128]{3,2,1,0:T(8,128)(2,1)}, u32[]{:S(2)}, u32[]{:S(2)}) collective-permute-start(bf16[24,2,64,128]{3,2,1,0:T(8,128)(2,1)} %get-tuple-element.169), channel_id=1, source_target_pairs={{0,24},{8,16},{16,8},{24,0},{1,25},{9,17},{17,9},{25,1},{2,26},{10... | collective-permute-start | bytes 2359304 | tf_op jit(solution)/shard_map/ppermute | solution.py:315
  231.5 74.5 %all-to-all-start.3 = ((bf16[8,32,48,128]{3,2,1,0:T(8,128)(2,1)}), bf16[8,32,48,128]{3,2,1,0:T(8,128)(2,1)S(1)}, u32[]{:S(2)}, u32[]{:S(2)}) async-start(bf16[8,32,48,128]{3,2,1,0:T(8,128)(2,1)} %copy-done.4), calls=%async_computation.3 | async-start | bytes 6291456 | tf_op jit(solution)/shard_map/all_to_all | solution.py:367
  244.9 31.6 %collective-permute-start.16 = (bf16[40,2,64,128]{3,2,1,0:T(8,128)(2,1)S(1)}, bf16[40,2,64,128]{3,2,1,0:T(8,128)(2,1)S(1)}, u32[]{:S(2)}, u32[]{:S(2)}) collective-permute-start(bf16[40,2,64,128]{3,2,1,0:T(8,128)(2,1)S(1)} %get-tuple-element.183), channel_id=1, source_target_pairs={{0,16},{8,24},{16,0},{24,8},{1,17},{9,25},{17,1},{25,9},{2,18},{10... | collective-permute-start | bytes 3932168 | tf_op jit(solution)/shard_map/ppermute | solution.py:315
  246.3 57.5 %collective-permute-start.17 = (bf16[40,2,64,128]{3,2,1,0:T(8,128)(2,1)S(1)}, bf16[40,2,64,128]{3,2,1,0:T(8,128)(2,1)}, u32[]{:S(2)}, u32[]{:S(2)}) collective-permute-start(bf16[40,2,64,128]{3,2,1,0:T(8,128)(2,1)S(1)} %get-tuple-element.184), channel_id=1, source_target_pairs={{0,24},{8,16},{16,8},{24,0},{1,25},{9,17},{17,9},{25,1},{2,26},{10... | collective-permute-start | bytes 3932168 | tf_op jit(solution)/shard_map/ppermute | solution.py:315
  306.1 52.6 %all-to-all-start.4 = ((bf16[8,32,32,128]{3,2,1,0:T(8,128)(2,1)}), bf16[8,32,32,128]{3,2,1,0:T(8,128)(2,1)}, u32[]{:S(2)}, u32[]{:S(2)}) async-start(bf16[8,32,32,128]{3,2,1,0:T(8,128)(2,1)} %copy-done.9), calls=%async_computation.4 | async-start | bytes 4194304 | tf_op jit(solution)/shard_map/all_to_all | solution.py:367
  315.9 34.9 %collective-permute-start.20 = (bf16[24,2,64,128]{3,2,1,0:T(8,128)(2,1)S(1)}, bf16[24,2,64,128]{3,2,1,0:T(8,128)(2,1)}, u32[]{:S(2)}, u32[]{:S(2)}) collective-permute-start(bf16[24,2,64,128]{3,2,1,0:T(8,128)(2,1)S(1)} %get-tuple-element.198), channel_id=1, source_target_pairs={{0,24},{8,16},{16,8},{24,0},{1,25},{9,17},{17,9},{25,1},{2,26},{10... | collective-permute-start | bytes 2359304 | tf_op jit(solution)/shard_map/ppermute | solution.py:315
  358.7 51.9 %all-to-all-start.5 = ((bf16[8,32,32,128]{3,2,1,0:T(8,128)(2,1)}), bf16[8,32,32,128]{3,2,1,0:T(8,128)(2,1)S(1)}, u32[]{:S(2)}, u32[]{:S(2)}) async-start(bf16[8,32,32,128]{3,2,1,0:T(8,128)(2,1)} %get-tuple-element.203), calls=%async_computation.5 | async-start | bytes 4194304 | tf_op jit(solution)/shard_map/all_to_all | solution.py:367
  365.9 21.9 %collective-permute-start.21 = (bf16[16,2,64,128]{3,2,1,0:T(8,128)(2,1)S(1)}, bf16[16,2,64,128]{3,2,1,0:T(8,128)(2,1)S(1)}, u32[]{:S(2)}, u32[]{:S(2)}) collective-permute-start(bf16[16,2,64,128]{3,2,1,0:T(8,128)(2,1)S(1)} %get-tuple-element.218), channel_id=1, source_target_pairs={{0,8},{8,0},{16,24},{24,16},{1,9},{9,1},{17,25},{25,17},{2,10},{10... | collective-permute-start | bytes 1572872 | tf_op jit(solution)/shard_map/ppermute | solution.py:315
  366.0 21.9 %collective-permute-start.22 = (bf16[16,2,64,128]{3,2,1,0:T(8,128)(2,1)S(1)}, bf16[16,2,64,128]{3,2,1,0:T(8,128)(2,1)S(1)}, u32[]{:S(2)}, u32[]{:S(2)}) collective-permute-start(bf16[16,2,64,128]{3,2,1,0:T(8,128)(2,1)S(1)} %get-tuple-element.219), channel_id=1, source_target_pairs={{0,16},{8,24},{16,0},{24,8},{1,17},{9,25},{17,1},{25,9},{2,18},{10... | collective-permute-start | bytes 1572872 | tf_op jit(solution)/shard_map/ppermute | solution.py:315
  367.4 23.8 %collective-permute-start.23 = (bf16[16,2,64,128]{3,2,1,0:T(8,128)(2,1)S(1)}, bf16[16,2,64,128]{3,2,1,0:T(8,128)(2,1)}, u32[]{:S(2)}, u32[]{:S(2)}) collective-permute-start(bf16[16,2,64,128]{3,2,1,0:T(8,128)(2,1)S(1)} %get-tuple-element.220), channel_id=1, source_target_pairs={{0,24},{8,16},{16,8},{24,0},{1,25},{9,17},{17,9},{25,1},{2,26},{10... | collective-permute-start | bytes 1572872 | tf_op jit(solution)/shard_map/ppermute | solution.py:315
  410.6 29.6 %all-to-all-start.6 = ((bf16[8,32,16,128]{3,2,1,0:T(8,128)(2,1)}), bf16[8,32,16,128]{3,2,1,0:T(8,128)(2,1)S(1)}, u32[]{:S(2)}, u32[]{:S(2)}) async-start(bf16[8,32,16,128]{3,2,1,0:T(8,128)(2,1)} %get-tuple-element.229), calls=%async_computation.6 | async-start | bytes 2097152 | tf_op jit(solution)/shard_map/all_to_all | solution.py:367
  418.8 23.8 %collective-permute-start.27 = (bf16[16,2,64,128]{3,2,1,0:T(8,128)(2,1)}, bf16[16,2,64,128]{3,2,1,0:T(8,128)(2,1)S(1)}, u32[]{:S(2)}, u32[]{:S(2)}) collective-permute-start(bf16[16,2,64,128]{3,2,1,0:T(8,128)(2,1)} %get-tuple-element.255), channel_id=1, source_target_pairs={{0,8},{8,0},{16,24},{24,16},{1,9},{9,1},{17,25},{25,17},{2,10},{10... | collective-permute-start | bytes 1572872 | tf_op jit(solution)/shard_map/ppermute | solution.py:315
  418.8 24.1 %collective-permute-start.28 = (bf16[16,2,64,128]{3,2,1,0:T(8,128)(2,1)}, bf16[16,2,64,128]{3,2,1,0:T(8,128)(2,1)}, u32[]{:S(2)}, u32[]{:S(2)}) collective-permute-start(bf16[16,2,64,128]{3,2,1,0:T(8,128)(2,1)} %get-tuple-element.256), channel_id=1, source_target_pairs={{0,16},{8,24},{16,0},{24,8},{1,17},{9,25},{17,1},{25,9},{2,18},{10... | collective-permute-start | bytes 1572872 | tf_op jit(solution)/shard_map/ppermute | solution.py:315
  420.3 24.0 %collective-permute-start.29 = (bf16[16,2,64,128]{3,2,1,0:T(8,128)(2,1)}, bf16[16,2,64,128]{3,2,1,0:T(8,128)(2,1)}, u32[]{:S(2)}, u32[]{:S(2)}) collective-permute-start(bf16[16,2,64,128]{3,2,1,0:T(8,128)(2,1)} %get-tuple-element.257), channel_id=1, source_target_pairs={{0,24},{8,16},{16,8},{24,0},{1,25},{9,17},{17,9},{25,1},{2,26},{10... | collective-permute-start | bytes 1572872 | tf_op jit(solution)/shard_map/ppermute | solution.py:315
  (50 other events, 499.6 us)

commit v5 on v4

--- a/solution.py
+++ b/solution.py
@@ -281,7 +281,7 @@
         out_specs=[pl.BlockSpec((step, v_own, pixels), lambda s: (here + s, 0, 0))] * 2,
         out_shape=[shape] * 2,
         input_output_aliases=aliases,
-        compiler_params=params(LARGE_VMEM_BYTES),
+        compiler_params=params(VMEM_BYTES if factors and first + count == total_u else LARGE_VMEM_BYTES),
         cost_estimate=pl.CostEstimate(
             flops=4 * count * v_own * inner * pixels,
             bytes_accessed=4 * inner * pixels + 12 * count * v_own * pixels,

time: 468 us -> 469 us (level)
  no operation moved by 1% of the time
where the time goes in v5:
time: 469 us; the launch traced here: 467 us
  waiting for transfers between devices  201 us (43%)
  Pallas kernels  123 us (26%)
  local copies, waits for them, and re-layouts  76 us (16%)
  starting transfers between devices  54.4 us (12%)
  other arithmetic  8.32 us (2%)
    ppermute x30, waiting for transfers between devices, swap(): return lax.ppermute(array, axis, [(i, i ^ partner) for i in range(size)])  120 us
    all_to_all x7, waiting for transfers between devices, to_owners(): return lax.all_to_all(array, 'mem', split_axis=0, concat_axis=0, tiled=True)  81 us
    pallas_call x6, Pallas kernels, pixel_transform(): pl.pallas_call(body, grid=(count // step,), in_specs=[pl.BlockSpec((inner...  69.9 us
    unnamed x76, local copies, waits for them, and re-layouts  30.6 us
    all_to_all x7, starting transfers between devices, to_owners(): return lax.all_to_all(array, 'mem', split_axis=0, concat_axis=0, tiled=True)  30.3 us
    ppermute x30, starting transfers between devices, swap(): return lax.ppermute(array, axis, [(i, i ^ partner) for i in range(size)])  24.1 us
    pallas_call x3, Pallas kernels, y_transform(): pl.pallas_call(body, grid=(n_x // step,), in_specs=[pl.BlockSpec(table.sh...  21.4 us
    pallas_call x6, Pallas kernels, x_transform(): pl.pallas_call(body, grid=(n_u // U_TILE,), in_specs=[pl.BlockSpec(table....  19 us
  transfers between devices with their start and end apart: 37, of which 20 were waited for; matrix products, arithmetic and copies ran while one was open for 12% of the time, Pallas kernels for 24%

profile of v5, /device:TPU:0, one launch (start us, length us, event | category | flops | bytes accessed | tf_op | source)
XLA Modules:
  0.0 466.9 jit_solution(4457769126731907189)
XLA Ops:
  26.7 5.3 %all-to-all-start = ((bf16[8,8,128,128]{3,2,1,0:T(8,128)(2,1)}), bf16[8,8,128,128]{3,2,1,0:T(8,128)(2,1)S(1)}, u32[]{:S(2)}, u32[]{:S(2)}) async-start(bf16[8,8,128,128]{3,2,1,0:T(8,128)(2,1)} %y_transform.3), calls=%async_computation | async-start | bytes 4194304 | tf_op jit(solution)/shard_map/all_to_all | solution.py:367
  41.4 11.3 %collective-permute-done.7.refs_2_ = bf16[24,128,128]{2,1,0:T(8,128)(2,1)S(1)} collective-permute-done((bf16[24,128,128]{2,1,0:T(8,128)(2,1)}, bf16[24,128,128]{2,1,0:T(8,128)(2,1)S(1)}, u32[]{:S(2)}, u32[]{:S(2)}) %collective-permute-start.7) | collective-permute-done | bytes 786464 | tf_op jit(solution)/shard_map/ppermute | solution.py:315
  52.6 15.9 %collective-permute-done.8.refs_3_ = bf16[24,128,128]{2,1,0:T(8,128)(2,1)S(1)} collective-permute-done((bf16[24,128,128]{2,1,0:T(8,128)(2,1)}, bf16[24,128,128]{2,1,0:T(8,128)(2,1)S(1)}, u32[]{:S(2)}, u32[]{:S(2)}) %collective-permute-start.8) | collective-permute-done | bytes 786464 | tf_op jit(solution)/shard_map/ppermute | solution.py:315
  68.5 5.6 %y_transform.4 = (bf16[8,24,48,128]{3,2,1,0:T(8,128)(2,1)S(1)}, bf16[8,24,80,128]{3,2,1,0:T(8,128)(2,1)S(1)}) custom-call(bf16[1024,512]{1,0:T(8,128)(2,1)S(1)} %copy_bitcast_fusion.t_ref, bf16[24,128,128]{2,1,0:T(8,128)(2,1)S(1)} %copy-done.15, bf16[24,128,128]{2,1,0:T(8,128)(2,1)S(1)} %collective-permute-done.6.refs_1_, ...), custom_call_target="tpu_custom_call" | custom-call | flops 3221225472 | bytes 10485760 | tf_op jit(solution)/shard_map/y_transform/pallas_call | solution.py:104
  80.1 4.8 %all-to-all-start.1 = ((bf16[8,24,48,128]{3,2,1,0:T(8,128)(2,1)}), bf16[8,24,48,128]{3,2,1,0:T(8,128)(2,1)S(1)}, u32[]{:S(2)}, u32[]{:S(2)}) async-start(bf16[8,24,48,128]{3,2,1,0:T(8,128)(2,1)} %copy-done.7), calls=%async_computation.1 | async-start | bytes 4718592 | tf_op jit(solution)/shard_map/all_to_all | solution.py:367
  98.8 9.9 %fusion.8 = (f32[2,44,64,32]{3,2,1,0:T(8,128)}, f32[2,44,64,32]{3,2,1,0:T(8,128)}, f32[2,44,64,32]{3,2,1,0:T(8,128)}, f32[2,44,64,32]{3,2,1,0:T(8,128)}) fusion(f32[2,47,64,32]{3,2,1,0:T(8,128)} %reshape.173), kind=kLoop, calls=%fused_computation.72 | loop fusion | bytes 5767168 | tf_op jit(solution)/shard_map/slice | solution.py:310
  108.8 6.6 %pad_maximum_fusion.w_ref = f32[2,44,64,128]{3,2,1,0:T(8,128)S(1)} fusion(f32[2,44,64,32]{3,2,1,0:T(8,128)} %get-tuple-element.277, f32[2,44,64,32]{3,2,1,0:T(8,128)} %get-tuple-element.278, f32[2,44,64,32]{3,2,1,0:T(8,128)} %get-tuple-element.279, f32[2,44,64,32]{3,2,1,0:T(8,128)} %get-tuple-element.276), kind=kLoop, calls=%fused_computation.5 | loop fusion | flops 2162688 | bytes 5767168 | tf_op jit(solution)/shard_map/concatenate | solution.py:310
  115.4 13.0 %chi_factors.1 = (f32[16,64,1024]{2,1,0:T(8,128)S(1)}, f32[16,64,1024]{2,1,0:T(8,128)S(1)}) custom-call(f32[2,44,64,128]{3,2,1,0:T(8,128)S(1)} %pad_maximum_fusion.w_ref, f32[2,8,128]{2,1,0:T(8,128)S(1)} %reshape.174.b_ref, bf16[2048,2048]{1,0:T(8,128)(2,1)} %constant.89.clone.t_ref), custom_call_target="tpu_custom_call" | custom-call | flops 8589934592 | bytes 16777216 | tf_op jit(solution)/shard_map/chi_factors/pallas_call | solution.py:203
  155.5 8.2 %gather_fusion.3 = bf16[8,256,2048]{2,1,0:T(8,128)(2,1)} fusion(bf16[8,256,2048]{2,1,0:T(8,128)(2,1)} %constant.92.clone, s32[1024]{0:T(1024)S(1)} %pad_clamp_fusion), kind=kCustom, calls=%fused_computation.3 | custom fusion | bytes 16777248 | tf_op jit(solution)/shard_map/jit(_take)/gather | solution.py:370
  163.8 12.9 %y_transform.5 = (bf16[8,32,48,128]{3,2,1,0:T(8,128)(2,1)S(1)}, bf16[8,32,32,128]{3,2,1,0:T(8,128)(2,1)S(1)}, bf16[8,32,32,128]{3,2,1,0:T(8,128)(2,1)}, bf16[8,32,16,128]{3,2,1,0:T(8,128)(2,1)}) custom-call(bf16[1024,512]{1,0:T(8,128)(2,1)S(1)} %copy_bitcast_fusion.t_ref, bf16[32,128,128]{2,1,0:T(8,128)(2,1)S(1)} %copy-done.14, ...), custom_call_target="tpu_custom_call" | custom-call | flops 4294967296 | bytes 13631488 | tf_op jit(solution)/shard_map/y_transform/pallas_call | solution.py:104
  179.7 8.1 %collective-permute-done.14.refs_3_ = bf16[24,2,64,128]{3,2,1,0:T(8,128)(2,1)} collective-permute-done((bf16[24,2,64,128]{3,2,1,0:T(8,128)(2,1)}, bf16[24,2,64,128]{3,2,1,0:T(8,128)(2,1)}, u32[]{:S(2)}, u32[]{:S(2)}) %collective-permute-start.14) | collective-permute-done | bytes 786464 | tf_op jit(solution)/shard_map/ppermute | solution.py:315
  187.7 43.8 %all-to-all-done.2 = bf16[8,24,80,128]{3,2,1,0:T(8,128)(2,1)} async-done(((bf16[8,24,80,128]{3,2,1,0:T(8,128)(2,1)}), bf16[8,24,80,128]{3,2,1,0:T(8,128)(2,1)}, u32[]{:S(2)}, u32[]{:S(2)}) %all-to-all-start.2) | async-done | bytes 3932192 | tf_op jit(solution)/shard_map/all_to_all | solution.py:367
  237.8 6.0 %x_transform.7 = (bf16[40,2,64,128]{3,2,1,0:T(8,128)(2,1)S(1)}, bf16[40,2,64,128]{3,2,1,0:T(8,128)(2,1)S(1)}, bf16[40,2,64,128]{3,2,1,0:T(8,128)(2,1)S(1)}, bf16[40,2,64,128]{3,2,1,0:T(8,128)(2,1)S(1)}) custom-call(bf16[512,512]{1,0:T(8,128)(2,1)S(1)} %bitcast.64, bf16[64,128,128]{2,1,0:T(8,128)(2,1)S(1)} %bitcast.55, bf16[192,80,128]{2,1,0:T(8,128)(2,1)} %bitcast.23.refs_1_), custom_call_target="tpu_custom_call" | custom-call | flops 2684354560 | bytes 11010048 | tf_op jit(solution)/shard_map/x_transform/pallas_call | solution.py:155
  247.9 28.5 %collective-permute-done.16.refs_2_ = bf16[40,2,64,128]{3,2,1,0:T(8,128)(2,1)S(1)} collective-permute-done((bf16[40,2,64,128]{3,2,1,0:T(8,128)(2,1)S(1)}, bf16[40,2,64,128]{3,2,1,0:T(8,128)(2,1)S(1)}, u32[]{:S(2)}, u32[]{:S(2)}) %collective-permute-start.16) | collective-permute-done | bytes 1310752 | tf_op jit(solution)/shard_map/ppermute | solution.py:315
  277.5 26.3 %collective-permute-done.17.refs_3_ = bf16[40,2,64,128]{3,2,1,0:T(8,128)(2,1)} collective-permute-done((bf16[40,2,64,128]{3,2,1,0:T(8,128)(2,1)S(1)}, bf16[40,2,64,128]{3,2,1,0:T(8,128)(2,1)}, u32[]{:S(2)}, u32[]{:S(2)}) %collective-permute-start.17) | collective-permute-done | bytes 1310752 | tf_op jit(solution)/shard_map/ppermute | solution.py:315
  316.2 6.4 %pixel_transform.7 = (f32[8,64,1024]{2,1,0:T(8,128)}, f32[8,64,1024]{2,1,0:T(8,128)}) custom-call(bf16[2048,2048]{1,0:T(8,128)(2,1)} %bitcast.65, bf16[40,2,64,128]{3,2,1,0:T(8,128)(2,1)} %copy-done.4, bf16[40,2,64,128]{3,2,1,0:T(8,128)(2,1)} %copy-done.26, bf16[40,2,64,128]{3,2,1,0:T(8,128)(2,1)} %copy-done.27, ...), custom_call_target="tpu_custom_call" | custom-call | flops 2147483648 | bytes 10485760 | tf_op jit(solution)/shard_map/pixel_transform/pallas_call | solution.py:273
  322.7 9.5 %pixel_transform.6 = (f32[16,64,1024]{2,1,0:T(8,128)}, f32[16,64,1024]{2,1,0:T(8,128)}) custom-call(bf16[2048,2048]{1,0:T(8,128)(2,1)} %bitcast.66, bf16[40,2,64,128]{3,2,1,0:T(8,128)(2,1)} %copy-done.4, bf16[40,2,64,128]{3,2,1,0:T(8,128)(2,1)} %copy-done.26, bf16[40,2,64,128]{3,2,1,0:T(8,128)(2,1)} %copy-done.27, ...), custom_call_target="tpu_custom_call" | custom-call | flops 4294967296 | bytes 16777216 | tf_op jit(solution)/shard_map/pixel_transform/pallas_call | solution.py:273
  335.7 15.1 %collective-permute-done.20.refs_7_ = bf16[24,2,64,128]{3,2,1,0:T(8,128)(2,1)} collective-permute-done((bf16[24,2,64,128]{3,2,1,0:T(8,128)(2,1)S(1)}, bf16[24,2,64,128]{3,2,1,0:T(8,128)(2,1)}, u32[]{:S(2)}, u32[]{:S(2)}) %collective-permute-start.20) | collective-permute-done | bytes 786464 | tf_op jit(solution)/shard_map/ppermute | solution.py:315
  350.8 7.9 %all-to-all-done.4 = bf16[8,32,32,128]{3,2,1,0:T(8,128)(2,1)} async-done(((bf16[8,32,32,128]{3,2,1,0:T(8,128)(2,1)}), bf16[8,32,32,128]{3,2,1,0:T(8,128)(2,1)}, u32[]{:S(2)}, u32[]{:S(2)}) %all-to-all-start.4) | async-done | bytes 2097184 | tf_op jit(solution)/shard_map/all_to_all | solution.py:367
  367.8 20.0 %pixel_transform.8 = (f32[64,64,1024]{2,1,0:T(8,128)}, f32[64,64,1024]{2,1,0:T(8,128)}) custom-call(bf16[2048,2048]{1,0:T(8,128)(2,1)} %bitcast.67, bf16[24,2,64,128]{3,2,1,0:T(8,128)(2,1)} %copy-done.24, bf16[24,2,64,128]{3,2,1,0:T(8,128)(2,1)} %copy-done.34, bf16[24,2,64,128]{3,2,1,0:T(8,128)(2,1)} %collective-permute-done.13.refs_2_, ...), custom_call_target="tpu_custom_call" | custom-call | flops 12884901888 | bytes 27262976 | tf_op jit(solution)/shard_map/pixel_transform/pallas_call | solution.py:273
  391.2 19.4 %all-to-all-done.5 = bf16[8,32,32,128]{3,2,1,0:T(8,128)(2,1)S(1)} async-done(((bf16[8,32,32,128]{3,2,1,0:T(8,128)(2,1)}), bf16[8,32,32,128]{3,2,1,0:T(8,128)(2,1)S(1)}, u32[]{:S(2)}, u32[]{:S(2)}) %all-to-all-start.5) | async-done | bytes 2097184 | tf_op jit(solution)/shard_map/all_to_all | solution.py:367
  420.7 15.2 %pixel_transform.9 = (f32[64,64,1024]{2,1,0:T(8,128)}, f32[64,64,1024]{2,1,0:T(8,128)}) custom-call(bf16[2048,2048]{1,0:T(8,128)(2,1)} %bitcast.68, bf16[40,2,64,128]{3,2,1,0:T(8,128)(2,1)} %copy-done.4, bf16[40,2,64,128]{3,2,1,0:T(8,128)(2,1)} %copy-done.26, bf16[40,2,64,128]{3,2,1,0:T(8,128)(2,1)} %copy-done.27, ...), custom_call_target="tpu_custom_call", output_to_operand_aliasing={{0}: (11, {}), {1}: (12, {})} | custom-call | flops 8589934592 | bytes 20971520 | tf_op jit(solution)/shard_map/pixel_transform/pallas_call | solution.py:273
  444.4 12.5 %pixel_transform.10 = (f32[64,64,1024]{2,1,0:T(8,128)}, f32[64,64,1024]{2,1,0:T(8,128)}) custom-call(bf16[2048,2048]{1,0:T(8,128)(2,1)} %bitcast.69, bf16[16,2,64,128]{3,2,1,0:T(8,128)(2,1)} %copy-done.23, bf16[16,2,64,128]{3,2,1,0:T(8,128)(2,1)} %copy-done.31, ...), custom_call_target="tpu_custom_call", output_to_operand_aliasing={{0}: (9, {}), {1}: (10, {})} | custom-call | flops 4294967296 | bytes 16777216 | tf_op jit(solution)/shard_map/pixel_transform/pallas_call | solution.py:273
  460.7 6.2 %pixel_transform.11 = (f32[64,64,1024]{2,1,0:T(8,128)}, f32[64,64,1024]{2,1,0:T(8,128)}) custom-call(bf16[2048,2048]{1,0:T(8,128)(2,1)} %bitcast.70, bf16[8,2,64,128]{3,2,1,0:T(8,128)(2,1)S(1)} %get-tuple-element.247.refs_0_, bf16[8,2,64,128]{3,2,1,0:T(8,128)(2,1)S(1)} %collective-permute-done.24.refs_1_, ...), custom_call_target="tpu_custom_call", output_to_operand_aliasing={{0}: (9, {}), {1}: (10, {})} | custom-call | flops 2147483648 | bytes 10485760 | tf_op jit(solution)/shard_map/pixel_transform/pallas_call | solution.py:273
  (184 shorter events, 147.1 us)
Async XLA Ops:
  26.7 52.0 %all-to-all-start = ((bf16[8,8,128,128]{3,2,1,0:T(8,128)(2,1)}), bf16[8,8,128,128]{3,2,1,0:T(8,128)(2,1)S(1)}, u32[]{:S(2)}, u32[]{:S(2)}) async-start(bf16[8,8,128,128]{3,2,1,0:T(8,128)(2,1)} %y_transform.3), calls=%async_computation | async-start | bytes 4194304 | tf_op jit(solution)/shard_map/all_to_all | solution.py:367
  32.0 20.6 %collective-permute-start.7 = (bf16[24,128,128]{2,1,0:T(8,128)(2,1)}, bf16[24,128,128]{2,1,0:T(8,128)(2,1)S(1)}, u32[]{:S(2)}, u32[]{:S(2)}) collective-permute-start(bf16[24,128,128]{2,1,0:T(8,128)(2,1)} %get-tuple-element.138), channel_id=1, source_target_pairs={{0,16},{8,24},{16,0},{24,8},{1,17},{9,25},{17,1},{25,9},{2,18},{10... | collective-permute-start | bytes 2359304 | tf_op jit(solution)/shard_map/ppermute | solution.py:315
  33.6 35.0 %collective-permute-start.8 = (bf16[24,128,128]{2,1,0:T(8,128)(2,1)}, bf16[24,128,128]{2,1,0:T(8,128)(2,1)S(1)}, u32[]{:S(2)}, u32[]{:S(2)}) collective-permute-start(bf16[24,128,128]{2,1,0:T(8,128)(2,1)} %get-tuple-element.139), channel_id=1, source_target_pairs={{0,24},{8,16},{16,8},{24,0},{1,25},{9,17},{17,9},{25,1},{2,26},{10... | collective-permute-start | bytes 2359304 | tf_op jit(solution)/shard_map/ppermute | solution.py:315
  80.1 59.3 %all-to-all-start.1 = ((bf16[8,24,48,128]{3,2,1,0:T(8,128)(2,1)}), bf16[8,24,48,128]{3,2,1,0:T(8,128)(2,1)S(1)}, u32[]{:S(2)}, u32[]{:S(2)}) async-start(bf16[8,24,48,128]{3,2,1,0:T(8,128)(2,1)} %copy-done.7), calls=%async_computation.1 | async-start | bytes 4718592 | tf_op jit(solution)/shard_map/all_to_all | solution.py:367
  89.5 43.0 %collective-permute-start.9 = (bf16[32,128,128]{2,1,0:T(8,128)(2,1)}, bf16[32,128,128]{2,1,0:T(8,128)(2,1)}, u32[]{:S(2)}, u32[]{:S(2)}) collective-permute-start(bf16[32,128,128]{2,1,0:T(8,128)(2,1)} %get-tuple-element.151), channel_id=1, source_target_pairs={{0,8},{8,0},{16,24},{24,16},{1,9},{9,1},{17,25},{25,17},{2,10},{10... | collective-permute-start | bytes 3145736 | tf_op jit(solution)/shard_map/ppermute | solution.py:315
  89.7 42.7 %collective-permute-start.10 = (bf16[32,128,128]{2,1,0:T(8,128)(2,1)}, bf16[32,128,128]{2,1,0:T(8,128)(2,1)}, u32[]{:S(2)}, u32[]{:S(2)}) collective-permute-start(bf16[32,128,128]{2,1,0:T(8,128)(2,1)} %get-tuple-element.152), channel_id=1, source_target_pairs={{0,16},{8,24},{16,0},{24,8},{1,17},{9,25},{17,1},{25,9},{2,18},{10... | collective-permute-start | bytes 3145736 | tf_op jit(solution)/shard_map/ppermute | solution.py:315
  91.2 46.0 %collective-permute-start.11 = (bf16[32,128,128]{2,1,0:T(8,128)(2,1)}, bf16[32,128,128]{2,1,0:T(8,128)(2,1)}, u32[]{:S(2)}, u32[]{:S(2)}) collective-permute-start(bf16[32,128,128]{2,1,0:T(8,128)(2,1)} %get-tuple-element.153), channel_id=1, source_target_pairs={{0,24},{8,16},{16,8},{24,0},{1,25},{9,17},{17,9},{25,1},{2,26},{10... | collective-permute-start | bytes 3145736 | tf_op jit(solution)/shard_map/ppermute | solution.py:315
  139.4 92.1 %all-to-all-start.2 = ((bf16[8,24,80,128]{3,2,1,0:T(8,128)(2,1)}), bf16[8,24,80,128]{3,2,1,0:T(8,128)(2,1)}, u32[]{:S(2)}, u32[]{:S(2)}) async-start(bf16[8,24,80,128]{3,2,1,0:T(8,128)(2,1)} %copy-done.5), calls=%async_computation.2 | async-start | bytes 7864320 | tf_op jit(solution)/shard_map/all_to_all | solution.py:367
  151.0 28.7 %collective-permute-start.12 = (bf16[24,2,64,128]{3,2,1,0:T(8,128)(2,1)}, bf16[24,2,64,128]{3,2,1,0:T(8,128)(2,1)S(1)}, u32[]{:S(2)}, u32[]{:S(2)}) collective-permute-start(bf16[24,2,64,128]{3,2,1,0:T(8,128)(2,1)} %get-tuple-element.167), channel_id=1, source_target_pairs={{0,8},{8,0},{16,24},{24,16},{1,9},{9,1},{17,25},{25,17},{2,10},{10... | collective-permute-start | bytes 2359304 | tf_op jit(solution)/shard_map/ppermute | solution.py:315
  151.0 28.7 %collective-permute-start.13 = (bf16[24,2,64,128]{3,2,1,0:T(8,128)(2,1)}, bf16[24,2,64,128]{3,2,1,0:T(8,128)(2,1)}, u32[]{:S(2)}, u32[]{:S(2)}) collective-permute-start(bf16[24,2,64,128]{3,2,1,0:T(8,128)(2,1)} %get-tuple-element.168), channel_id=1, source_target_pairs={{0,16},{8,24},{16,0},{24,8},{1,17},{9,25},{17,1},{25,9},{2,18},{10... | collective-permute-start | bytes 2359304 | tf_op jit(solution)/shard_map/ppermute | solution.py:315
  152.5 35.2 %collective-permute-start.14 = (bf16[24,2,64,128]{3,2,1,0:T(8,128)(2,1)}, bf16[24,2,64,128]{3,2,1,0:T(8,128)(2,1)}, u32[]{:S(2)}, u32[]{:S(2)}) collective-permute-start(bf16[24,2,64,128]{3,2,1,0:T(8,128)(2,1)} %get-tuple-element.169), channel_id=1, source_target_pairs={{0,24},{8,16},{16,8},{24,0},{1,25},{9,17},{17,9},{25,1},{2,26},{10... | collective-permute-start | bytes 2359304 | tf_op jit(solution)/shard_map/ppermute | solution.py:315
  231.5 74.5 %all-to-all-start.3 = ((bf16[8,32,48,128]{3,2,1,0:T(8,128)(2,1)}), bf16[8,32,48,128]{3,2,1,0:T(8,128)(2,1)S(1)}, u32[]{:S(2)}, u32[]{:S(2)}) async-start(bf16[8,32,48,128]{3,2,1,0:T(8,128)(2,1)} %copy-done.6), calls=%async_computation.3 | async-start | bytes 6291456 | tf_op jit(solution)/shard_map/all_to_all | solution.py:367
  244.9 31.6 %collective-permute-start.16 = (bf16[40,2,64,128]{3,2,1,0:T(8,128)(2,1)S(1)}, bf16[40,2,64,128]{3,2,1,0:T(8,128)(2,1)S(1)}, u32[]{:S(2)}, u32[]{:S(2)}) collective-permute-start(bf16[40,2,64,128]{3,2,1,0:T(8,128)(2,1)S(1)} %get-tuple-element.183), channel_id=1, source_target_pairs={{0,16},{8,24},{16,0},{24,8},{1,17},{9,25},{17,1},{25,9},{2,18},{10... | collective-permute-start | bytes 3932168 | tf_op jit(solution)/shard_map/ppermute | solution.py:315
  246.3 57.5 %collective-permute-start.17 = (bf16[40,2,64,128]{3,2,1,0:T(8,128)(2,1)S(1)}, bf16[40,2,64,128]{3,2,1,0:T(8,128)(2,1)}, u32[]{:S(2)}, u32[]{:S(2)}) collective-permute-start(bf16[40,2,64,128]{3,2,1,0:T(8,128)(2,1)S(1)} %get-tuple-element.184), channel_id=1, source_target_pairs={{0,24},{8,16},{16,8},{24,0},{1,25},{9,17},{17,9},{25,1},{2,26},{10... | collective-permute-start | bytes 3932168 | tf_op jit(solution)/shard_map/ppermute | solution.py:315
  306.1 52.6 %all-to-all-start.4 = ((bf16[8,32,32,128]{3,2,1,0:T(8,128)(2,1)}), bf16[8,32,32,128]{3,2,1,0:T(8,128)(2,1)}, u32[]{:S(2)}, u32[]{:S(2)}) async-start(bf16[8,32,32,128]{3,2,1,0:T(8,128)(2,1)} %copy-done.11), calls=%async_computation.4 | async-start | bytes 4194304 | tf_op jit(solution)/shard_map/all_to_all | solution.py:367
  315.9 34.9 %collective-permute-start.20 = (bf16[24,2,64,128]{3,2,1,0:T(8,128)(2,1)S(1)}, bf16[24,2,64,128]{3,2,1,0:T(8,128)(2,1)}, u32[]{:S(2)}, u32[]{:S(2)}) collective-permute-start(bf16[24,2,64,128]{3,2,1,0:T(8,128)(2,1)S(1)} %get-tuple-element.198), channel_id=1, source_target_pairs={{0,24},{8,16},{16,8},{24,0},{1,25},{9,17},{17,9},{25,1},{2,26},{10... | collective-permute-start | bytes 2359304 | tf_op jit(solution)/shard_map/ppermute | solution.py:315
  358.7 51.9 %all-to-all-start.5 = ((bf16[8,32,32,128]{3,2,1,0:T(8,128)(2,1)}), bf16[8,32,32,128]{3,2,1,0:T(8,128)(2,1)S(1)}, u32[]{:S(2)}, u32[]{:S(2)}) async-start(bf16[8,32,32,128]{3,2,1,0:T(8,128)(2,1)} %get-tuple-element.203), calls=%async_computation.5 | async-start | bytes 4194304 | tf_op jit(solution)/shard_map/all_to_all | solution.py:367
  365.9 21.9 %collective-permute-start.21 = (bf16[16,2,64,128]{3,2,1,0:T(8,128)(2,1)S(1)}, bf16[16,2,64,128]{3,2,1,0:T(8,128)(2,1)S(1)}, u32[]{:S(2)}, u32[]{:S(2)}) collective-permute-start(bf16[16,2,64,128]{3,2,1,0:T(8,128)(2,1)S(1)} %get-tuple-element.218), channel_id=1, source_target_pairs={{0,8},{8,0},{16,24},{24,16},{1,9},{9,1},{17,25},{25,17},{2,10},{10... | collective-permute-start | bytes 1572872 | tf_op jit(solution)/shard_map/ppermute | solution.py:315
  366.0 21.9 %collective-permute-start.22 = (bf16[16,2,64,128]{3,2,1,0:T(8,128)(2,1)S(1)}, bf16[16,2,64,128]{3,2,1,0:T(8,128)(2,1)S(1)}, u32[]{:S(2)}, u32[]{:S(2)}) collective-permute-start(bf16[16,2,64,128]{3,2,1,0:T(8,128)(2,1)S(1)} %get-tuple-element.219), channel_id=1, source_target_pairs={{0,16},{8,24},{16,0},{24,8},{1,17},{9,25},{17,1},{25,9},{2,18},{10... | collective-permute-start | bytes 1572872 | tf_op jit(solution)/shard_map/ppermute | solution.py:315
  367.4 23.8 %collective-permute-start.23 = (bf16[16,2,64,128]{3,2,1,0:T(8,128)(2,1)S(1)}, bf16[16,2,64,128]{3,2,1,0:T(8,128)(2,1)}, u32[]{:S(2)}, u32[]{:S(2)}) collective-permute-start(bf16[16,2,64,128]{3,2,1,0:T(8,128)(2,1)S(1)} %get-tuple-element.220), channel_id=1, source_target_pairs={{0,24},{8,16},{16,8},{24,0},{1,25},{9,17},{17,9},{25,1},{2,26},{10... | collective-permute-start | bytes 1572872 | tf_op jit(solution)/shard_map/ppermute | solution.py:315
  410.6 29.6 %all-to-all-start.6 = ((bf16[8,32,16,128]{3,2,1,0:T(8,128)(2,1)}), bf16[8,32,16,128]{3,2,1,0:T(8,128)(2,1)S(1)}, u32[]{:S(2)}, u32[]{:S(2)}) async-start(bf16[8,32,16,128]{3,2,1,0:T(8,128)(2,1)} %get-tuple-element.229), calls=%async_computation.6 | async-start | bytes 2097152 | tf_op jit(solution)/shard_map/all_to_all | solution.py:367
  418.8 24.4 %collective-permute-start.27 = (bf16[16,2,64,128]{3,2,1,0:T(8,128)(2,1)}, bf16[16,2,64,128]{3,2,1,0:T(8,128)(2,1)S(1)}, u32[]{:S(2)}, u32[]{:S(2)}) collective-permute-start(bf16[16,2,64,128]{3,2,1,0:T(8,128)(2,1)} %get-tuple-element.255), channel_id=1, source_target_pairs={{0,8},{8,0},{16,24},{24,16},{1,9},{9,1},{17,25},{25,17},{2,10},{10... | collective-permute-start | bytes 1572872 | tf_op jit(solution)/shard_map/ppermute | solution.py:315
  418.8 24.8 %collective-permute-start.28 = (bf16[16,2,64,128]{3,2,1,0:T(8,128)(2,1)}, bf16[16,2,64,128]{3,2,1,0:T(8,128)(2,1)}, u32[]{:S(2)}, u32[]{:S(2)}) collective-permute-start(bf16[16,2,64,128]{3,2,1,0:T(8,128)(2,1)} %get-tuple-element.256), channel_id=1, source_target_pairs={{0,16},{8,24},{16,0},{24,8},{1,17},{9,25},{17,1},{25,9},{2,18},{10... | collective-permute-start | bytes 1572872 | tf_op jit(solution)/shard_map/ppermute | solution.py:315
  420.3 24.0 %collective-permute-start.29 = (bf16[16,2,64,128]{3,2,1,0:T(8,128)(2,1)}, bf16[16,2,64,128]{3,2,1,0:T(8,128)(2,1)}, u32[]{:S(2)}, u32[]{:S(2)}) collective-permute-start(bf16[16,2,64,128]{3,2,1,0:T(8,128)(2,1)} %get-tuple-element.257), channel_id=1, source_target_pairs={{0,24},{8,16},{16,8},{24,0},{1,25},{9,17},{17,9},{25,1},{2,26},{10... | collective-permute-start | bytes 1572872 | tf_op jit(solution)/shard_map/ppermute | solution.py:315
  (50 other events, 508.2 us)
